TPU v7x, 256 devices: a whole 4x4x8 slice. The times are simulated.
256 devices in a mesh: dp: 8 (over x, y_hi), expert: 32 (over y_lo, z, core).
Axes of the slice: x: 4, y: 4 (y_hi: 2, y_lo: 2; y = y_hi * 2 + y_lo), z: 8, core: 2. Of those that a mesh axis runs over, the one named last changes fastest.
Arguments:
- patches: bfloat16 [32768, 1280], P(('dp', 'expert')), may hold values from -6 to 6
- teacher: bfloat16 [32768, 1280], P(('dp', 'expert')), may hold values from -6 to 6
- route: int32 [32768, 1], P(('dp', 'expert')), may hold values from 0 to 31; in each aligned block of 128 rows (0 to 127, 128 to 255, ...) at most 8 rows name the same one
- gates: bfloat16 [32768], P(('dp', 'expert')), may hold values from 0.25 to 1
- w_in: bfloat16 [32, 40, 128, 128], P('expert'), may hold values from -0.5 to 0.5
- in_rows: int32 [32, 40], P('expert'), may hold values from 0 to 9
- in_cols: int32 [32, 40], P('expert'), may hold values from 0 to 39, each once within a row
- w_out: bfloat16 [32, 40, 128, 128], P('expert'), may hold values from -0.25 to 0.25
- out_rows: int32 [32, 40], P('expert'), may hold values from 0 to 39
Outputs:
- student: bfloat16 [32768, 1280], P(('dp', 'expert'))
- grad_patches: float32 [32768, 1280], P(('dp', 'expert'))
- grad_w_in: float32 [32, 40, 128, 128], P('expert', 'dp')
- grad_w_out: float32 [32, 40, 128, 128], P('expert', 'dp')
Inputs may be any that keep to these rules, and one draw needn't show every extreme that they name: `route`: within the rows of one device no expert is named by more than 8 rows, a bound that some block reaches. in_rows[e, b] is the feature block read by block b of expert e's first matrix. Each row of in_cols names every hidden block once. Block m of expert e's second matrix reads hidden block out_rows[e, m] and writes output block m // 4.
All inputs are finite; a program needn't handle non-finite values.
Results may differ from a plain program's by a relative error of at most 0.014.
Values may be sent and summed in bfloat16 or wider, within the bound.
No kernel may reach another device: no remote copies, remote signals or barrier semaphores. Data moves between devices by JAX's collectives and lax.ppermute only.
A program may use at most 64 MiB of HBM per device.

v0:
```python
import jax
import jax.numpy as jnp
from jax import lax
from jax.sharding import PartitionSpec as P

BLK = 128
K2 = 4
DB = 10
FB = 40


def normalize(features):
    centred = features - jnp.mean(features, axis=-1, keepdims=True)
    variance = jnp.mean(centred * centred, axis=-1, keepdims=True)
    return centred * lax.rsqrt(variance + 1e-06)


def hidden_order(columns):
    labels = jnp.arange(FB, dtype=jnp.int32)
    matches = columns[:, None] == labels[None, :]
    return jnp.sum(jnp.where(matches, labels[:, None], 0), axis=0)


def expert_hidden(normed_rows, weight_in, rows_in, read_blocks):
    row_count = normed_rows.shape[0]
    picked = jnp.take(normed_rows.reshape(row_count, DB, BLK), rows_in, axis=1)
    pre_hidden = jnp.einsum("rbi,bio->rbo", picked, weight_in, preferred_element_type=jnp.float32)
    hidden = jax.nn.gelu(pre_hidden).astype(jnp.bfloat16)
    spread = jnp.take(hidden, read_blocks, axis=1).reshape(row_count, DB, K2, BLK)
    return (picked, pre_hidden, spread)


def expert_output(spread, weight_out):
    out_blocks = weight_out.reshape(DB, K2, BLK, BLK)
    produced = jnp.einsum("rjkf,jkfd->rjd", spread, out_blocks, preferred_element_type=jnp.float32)
    return produced.reshape(spread.shape[0], DB * BLK)


def expert_backward(
    grad_out_rows, picked, pre_hidden, spread, weight_in, rows_in, weight_out, read_blocks
):
    row_count = grad_out_rows.shape[0]
    grad_blocks = grad_out_rows.reshape(row_count, DB, BLK)
    out_blocks = weight_out.reshape(DB, K2, BLK, BLK)
    grad_weight_out = jnp.einsum(
        "rjkf,rjd->jkfd", spread, grad_blocks, preferred_element_type=jnp.float32
    ).reshape(DB * K2, BLK, BLK)
    backward = jnp.einsum(
        "rjd,jkfd->rjkf", grad_blocks, out_blocks, preferred_element_type=jnp.float32
    ).reshape(row_count, DB * K2, BLK)
    labels = jnp.arange(FB, dtype=jnp.int32)
    gather_matrix = (read_blocks[:, None] == labels[None, :]).astype(jnp.float32)
    grad_hidden = jnp.einsum(
        "rmf,mb->rbf", backward, gather_matrix, precision=lax.Precision.HIGHEST
    )
    _, pullback = jax.vjp(jax.nn.gelu, pre_hidden)
    grad_pre = pullback(grad_hidden)[0].astype(jnp.bfloat16)
    grad_weight_in = jnp.einsum(
        "rbi,rbo->bio", picked, grad_pre, preferred_element_type=jnp.float32
    )
    grad_picked = jnp.einsum(
        "rbo,bio->rbi", grad_pre, weight_in, preferred_element_type=jnp.float32
    )
    input_labels = jnp.arange(DB, dtype=jnp.int32)
    fold_matrix = (rows_in[:, None] == input_labels[None, :]).astype(jnp.float32)
    grad_normed = jnp.einsum(
        "rbi,bj->rji", grad_picked, fold_matrix, precision=lax.Precision.HIGHEST
    )
    return (
        grad_normed.reshape(row_count, DB * BLK).astype(jnp.bfloat16),
        grad_weight_in,
        grad_weight_out,
    )


def local(patches, teacher, route, gates, w_in, in_rows, in_cols, w_out, out_rows):
    row_count = patches.shape[0]
    feature_count = patches.shape[1]
    owners = lax.axis_size("expert")
    slot_cap = max(2, 2 * row_count // owners)
    slot_total = owners * slot_cap
    row_block = min(256, slot_total)
    expert_of = route[:, 0]
    owner_hits = (expert_of[:, None] == jnp.arange(owners, dtype=jnp.int32)[None, :]).astype(
        jnp.int32
    )
    slot_rank = jnp.sum((jnp.cumsum(owner_hits, axis=0) - 1) * owner_hits, axis=1)
    counts = jnp.sum(owner_hits, axis=0)
    slot_of = expert_of * slot_cap + slot_rank
    source_row = (
        jnp.full((slot_total,), row_count, jnp.int32)
        .at[slot_of]
        .set(jnp.arange(row_count, dtype=jnp.int32))
    )
    weight_in = w_in[0]
    rows_in = in_rows[0]
    weight_out = w_out[0]
    read_blocks = hidden_order(in_cols[0])[out_rows[0]]
    features = patches.astype(jnp.float32)
    gate_rows = gates.astype(jnp.float32)[:, None]

    def to_slots(values):
        packed = jnp.take(values, source_row, axis=0, mode="fill", fill_value=0)
        return packed.reshape((owners, slot_cap) + values.shape[1:])

    def from_slots(values):
        return jnp.take(values.reshape((slot_total,) + values.shape[2:]), slot_of, axis=0)

    def row_layout():
        block_total = slot_total // row_block

        def gather_rows(values):
            return values.reshape((slot_total,) + values.shape[2:])

        def scatter_rows(values):
            return values.reshape((owners, slot_cap) + values.shape[1:])

        return (gather_rows, scatter_rows, block_total)

    empty_rows = jnp.zeros((slot_total, feature_count), jnp.bfloat16)
    empty_in = jnp.zeros((FB, BLK, BLK), jnp.float32)
    empty_out = jnp.zeros((DB * K2, BLK, BLK), jnp.float32)
    normed = normalize(features).astype(jnp.bfloat16)
    arrived_rows, arrived = (
        lax.all_to_all(to_slots(normed), "expert", split_axis=0, concat_axis=0, tiled=True),
        lax.all_to_all(counts, "expert", split_axis=0, concat_axis=0, tiled=True),
    )
    gather_rows, scatter_rows, block_total = row_layout()
    normed_rows = gather_rows(arrived_rows)

    def forward_block(block_index, produced_rows):
        picked, pre_hidden, spread = expert_hidden(normed_rows, weight_in, rows_in, read_blocks)
        produced = expert_output(spread, weight_out).astype(jnp.bfloat16)
        return produced

    produced_rows = lax.fori_loop(0, block_total, forward_block, empty_rows)
    returned = lax.all_to_all(
        scatter_rows(produced_rows), "expert", split_axis=0, concat_axis=0, tiled=True
    )
    summed = features + gate_rows * from_slots(returned).astype(jnp.float32)
    mismatch = summed - teacher.astype(jnp.float32)
    grad_expert = (gate_rows * mismatch).astype(jnp.bfloat16)
    arrived_grads = lax.all_to_all(
        to_slots(grad_expert), "expert", split_axis=0, concat_axis=0, tiled=True
    )
    grad_expert_rows = gather_rows(arrived_grads)

    def backward_block(block_index, running):
        grad_rows, grad_in, grad_out = running
        picked, pre_hidden, spread = expert_hidden(normed_rows, weight_in, rows_in, read_blocks)
        grad_normed, part_in, part_out = expert_backward(
            grad_expert_rows,
            picked,
            pre_hidden,
            spread,
            weight_in,
            rows_in,
            weight_out,
            read_blocks,
        )
        return (grad_normed, grad_in + part_in, grad_out + part_out)

    grad_rows, grad_in, grad_out = lax.fori_loop(
        0, block_total, backward_block, (empty_rows, empty_in, empty_out)
    )
    grad_back = lax.all_to_all(
        scatter_rows(grad_rows), "expert", split_axis=0, concat_axis=0, tiled=True
    )
    grad_normed_rows = from_slots(grad_back).astype(jnp.float32)
    _, pullback = jax.vjp(normalize, features)
    grad_patches = mismatch + pullback(grad_normed_rows)[0]
    part_in, part_out = (
        lax.psum_scatter(
            grad_in.astype(jnp.bfloat16), "dp", scatter_dimension=0, tiled=True
        ).astype(jnp.float32),
        lax.psum_scatter(
            grad_out.astype(jnp.bfloat16), "dp", scatter_dimension=0, tiled=True
        ).astype(jnp.float32),
    )
    return (summed.astype(jnp.bfloat16), grad_patches, part_in[None], part_out[None])


def solution(mesh):
    placed = (
        P(("dp", "expert"), None),
        P(("dp", "expert"), None),
        P(("dp", "expert"), None),
        P(("dp", "expert")),
        P("expert", None, None, None),
        P("expert", None),
        P("expert", None),
        P("expert", None, None, None),
        P("expert", None),
    )
    return jax.shard_map(
        local,
        mesh=mesh,
        in_specs=placed,
        out_specs=(
            P(("dp", "expert"), None),
            P(("dp", "expert"), None),
            P("expert", "dp", None, None),
            P("expert", "dp", None, None),
        ),
        check_vma=False,
    )
```

profile of v0, /device:TPU:1, one launch (start us, length us, event | category | flops | bytes accessed | tf_op | source)
XLA Modules:
  0.0 295.0 jit_solution(8365876505923572841)
XLA Ops:
  7.2 0.8 fusion.44
  8.0 0.2 reduce_window_sum.11
  8.2 0.8 select_reduce_fusion
  9.0 0.7 fusion.51
  9.7 1.0 scatter_custom_fusion
  10.7 1.1 convert_reduce_fusion
  11.8 1.2 fusion.36
  13.0 1.2 fusion.37
  14.2 1.3 gather_fusion.1
  15.5 1.0 select_bitcast_fusion.1
  16.5 11.2 %all-to-all-start = ((bf16[32,8,1280]{2,1,0:T(8,128)(2,1)}), bf16[32,8,1280]{2,1,0:T(8,128)(2,1)}, u32[]{:S(2)}, u32[]{:S(2)}) async-start(bf16[32,8,1280]{2,1,0:T(8,128)(2,1)} %select_bitcast_fusion.1), calls=%async_computation | async-start | bytes 1310720 | tf_op jit(solution)/shard_map/all_to_all | solution.py:125
  27.8 0.8 gather_fusion
  28.7 18.1 %all-to-all-done = bf16[32,8,1280]{2,1,0:T(8,128)(2,1)} async-done(((bf16[32,8,1280]{2,1,0:T(8,128)(2,1)}), bf16[32,8,1280]{2,1,0:T(8,128)(2,1)}, u32[]{:S(2)}, u32[]{:S(2)}) %all-to-all-start) | async-done | bytes 655392 | tf_op jit(solution)/shard_map/all_to_all | solution.py:125
  46.7 1.4 reshape_reshape.10
  48.4 2.5 gather_fusion.2
  50.9 6.7 %fusion.10 = (bf16[256,40,128]{2,0,1:T(8,128)(2,1)}, f32[40,256,128]{2,1,0:T(8,128)}) fusion(bf16[1,40,128,128]{3,2,1,0:T(8,128)(2,1)S(1)} %copy-done, bf16[40,256,128]{2,1,0:T(8,128)(2,1)} %gather_fusion.2, pred[40]{0:T(512)(128)(4,1)S(1)} %compare_and_fusion.2), kind=kOutput, calls=%fused_computation.23 | convolution fusion | flops 348651520 | bytes 11796520 | tf_op jit(solution)/shard_map/while/body/eval_jaxpr/rbi,bio->rbo/dot_general | solution.py:27
  57.6 4.3 %gather_fusion.3 = bf16[40,256,128]{2,1,0:T(8,128)(2,1)} fusion(bf16[256,40,128]{2,0,1:T(8,128)(2,1)} %get-tuple-element.53, s32[1024]{0:T(1024)S(1)} %pad_clamp_fusion.1), kind=kCustom, calls=%fused_computation.2.clone | custom fusion | bytes 5243040 | tf_op jit(solution)/shard_map/while/body/eval_jaxpr/jit(_take)/gather | solution.py:29
  62.0 2.1 broadcast_select_fusion
  64.1 0.8 fusion.31
  65.0 0.7 copy-done.2
  65.6 0.5 copy.26
  66.1 1.2 convert_element_type.81
  67.4 5.6 %all-to-all-start.1 = ((bf16[32,8,1280]{2,1,0:T(8,128)(2,1)}), bf16[32,8,1280]{2,1,0:T(8,128)(2,1)S(1)}, u32[]{:S(2)}, u32[]{:S(2)}) async-start(bf16[32,8,1280]{2,1,0:T(8,128)(2,1)} %convert_element_type.81), calls=%async_computation.1 | async-start | bytes 1310720 | tf_op jit(solution)/shard_map/all_to_all | solution.py:137
  73.0 19.0 %all-to-all-done.1 = bf16[32,8,1280]{2,1,0:T(8,128)(2,1)S(1)} async-done(((bf16[32,8,1280]{2,1,0:T(8,128)(2,1)}), bf16[32,8,1280]{2,1,0:T(8,128)(2,1)S(1)}, u32[]{:S(2)}, u32[]{:S(2)}) %all-to-all-start.1) | async-done | bytes 655392 | tf_op jit(solution)/shard_map/all_to_all | solution.py:137
  92.1 0.9 gather_fusion.4
  93.0 0.3 multiply_convert_fusion
  93.3 1.3 gather_fusion.5
  94.7 24.4 %all_to_all.20 = bf16[32,8,1280]{2,1,0:T(8,128)(2,1)} all-to-all(bf16[32,8,1280]{2,1,0:T(8,128)(2,1)S(1)} %select_bitcast_fusion), channel_id=1, replica_groups=mesh['dp'=8,'expert'=32] {'expert'}, dimensions={0} | all-to-all | bytes 1310720 | tf_op jit(solution)/shard_map/all_to_all | solution.py:143
  119.1 1.4 reshape_reshape.11
  120.6 3.9 %convolution_convert_fusion = bf16[10,4,128,128]{3,2,1,0:T(8,128)(2,1)} fusion(bf16[256,10,4,128]{3,0,2,1:T(8,128)(2,1)} %bitcast.112, bf16[256,10,128,1]{2,1,0,3:T(8,128)(2,1)S(1)} %bitcast.113), kind=kOutput, calls=%fused_computation.36 | convolution fusion | flops 336199680 | bytes 4587520 | tf_op jit(solution)/shard_map/while/body/eval_jaxpr/rjkf,rjd->jkfd/dot_general | solution.py:45
  124.5 3.2 %fusion.42 = f32[10,256,4,128]{3,1,2,0:T(8,128)} fusion(bf16[10,4,128,128]{3,2,1,0:T(8,128)(2,1)S(1)} %bitcast.117, bf16[256,10,128,1]{2,1,0,3:T(8,128)(2,1)S(1)} %bitcast.114), kind=kOutput, calls=%fused_computation.64 | convolution fusion | flops 335544320 | bytes 7208960 | tf_op jit(solution)/shard_map/while/body/eval_jaxpr/rjd,jkfd->rjkf/dot_general | solution.py:48
  127.7 8.6 %fusion.13 = f32[40,256,128]{2,0,1:T(8,128)S(1)} fusion(f32[256,40,128]{2,0,1:T(8,128)} %bitcast.108, s32[40]{0:T(128)S(1)} %gather_fusion), kind=kOutput, calls=%fused_computation.26 | convolution fusion | flops 629147200 | bytes 10485920 | tf_op jit(solution)/shard_map/while/body/eval_jaxpr/rmf,mb->rbf/dot_general | solution.py:53
  136.3 5.8 %fusion.6 = bf16[256,40,128]{2,0,1:T(8,128)(2,1)S(1)} fusion(f32[40,256,128]{2,1,0:T(8,128)} %get-tuple-element.54, f32[40,256,128]{2,0,1:T(8,128)S(1)} %fusion.13), kind=kLoop, calls=%fused_computation.16 | loop fusion | flops 26214400 | bytes 13107200 | tf_op jit(solution)/shard_map/while/body/eval_jaxpr/convert_element_type | solution.py:57
  142.1 0.9 convolution_bitcast_fusion
  143.0 0.6 copy-done.3
  143.6 4.9 %fusion.25 = bf16[256,10,128]{2,1,0:T(8,128)(2,1)S(1)} fusion(f32[256,40,128]{2,0,1:T(8,128)S(1)} %convolution_bitcast_fusion, s32[40]{0:T(128)S(1)} %bitcast.120), kind=kOutput, calls=%fused_computation.39 | convolution fusion | flops 157614480 | bytes 5898400 | tf_op jit(solution)/shard_map/while/body/eval_jaxpr/rbi,bj->rji/dot_general | solution.py:66
  148.5 1.2 convert_element_type.89
  149.7 5.7 %all-to-all-start.3 = ((bf16[32,8,1280]{2,1,0:T(8,128)(2,1)}), bf16[32,8,1280]{2,1,0:T(8,128)(2,1)S(1)}, u32[]{:S(2)}, u32[]{:S(2)}) async-start(bf16[32,8,1280]{2,1,0:T(8,128)(2,1)} %convert_element_type.89), calls=%async_computation.3 | async-start | bytes 1310720 | tf_op jit(solution)/shard_map/all_to_all | solution.py:166
  155.4 4.7 %fusion.19 = bf16[40,128,128]{2,1,0:T(8,128)(2,1)} fusion(bf16[256,40,128]{2,0,1:T(8,128)(2,1)} %copy-done.3, bf16[40,256,128]{2,1,0:T(8,128)(2,1)} %gather_fusion.2, pred[40]{0:T(512)(128)(4,1)S(1)} %compare_and_fusion.2), kind=kOutput, calls=%fused_computation.35 | convolution fusion | flops 337510400 | bytes 6553640 | tf_op jit(solution)/shard_map/while/body/eval_jaxpr/rbi,rbo->bio/dot_general | solution.py:58
  160.2 14.3 %all-to-all-done.3 = bf16[32,8,1280]{2,1,0:T(8,128)(2,1)S(1)} async-done(((bf16[32,8,1280]{2,1,0:T(8,128)(2,1)}), bf16[32,8,1280]{2,1,0:T(8,128)(2,1)S(1)}, u32[]{:S(2)}, u32[]{:S(2)}) %all-to-all-start.3) | async-done | bytes 655392 | tf_op jit(solution)/shard_map/all_to_all | solution.py:166
  174.5 0.9 gather_fusion.6
  175.4 0.3 fusion.38
  175.7 0.3 fusion.40
  176.1 1.4 add_add_fusion.1
  177.5 26.6 %reduce-scatter.5.cloned.1.call-done = bf16[5,128,128]{2,1,0:T(8,128)(2,1)} async-done(((bf16[40,128,128]{2,1,0:T(8,128)(2,1)}), bf16[5,128,128]{2,1,0:T(8,128)(2,1)}) %reduce-scatter.5.cloned.1.call-update) | async-done | bytes 163856 | tf_op jit(solution)/shard_map/reduce_scatter | solution.py:176
  204.0 1.7 bitcast_convert_fusion
  205.7 80.8 %reduce-scatter.3.cloned.1.call-done = bf16[5,128,128]{2,1,0:T(8,128)(2,1)} async-done(((bf16[40,128,128]{2,1,0:T(8,128)(2,1)}), bf16[5,128,128]{2,1,0:T(8,128)(2,1)}) %reduce-scatter.3.cloned.1.call-update) | async-done | bytes 163856 | tf_op jit(solution)/shard_map/reduce_scatter | solution.py:173
  286.5 1.7 bitcast_convert_fusion.1
  (48 shorter events, 0.7 us)
Async XLA Ops:
  7.2 43.7 %copy-start = (bf16[1,40,128,128]{3,2,1,0:T(8,128)(2,1)S(1)}, bf16[1,40,128,128]{3,2,1,0:T(8,128)(2,1)}, u32[]{:S(2)}) copy-start(bf16[1,40,128,128]{3,2,1,0:T(8,128)(2,1)} %param.21) | copy-start | bytes 3932164
  15.5 12.2 %copy-start.9 = (s32[1,40]{1,0:T(1,128)S(1)}, s32[1,40]{1,0:T(1,128)}, u32[]{:S(2)}) copy-start(s32[1,40]{1,0:T(1,128)} %param.25) | copy-start | bytes 484
  15.5 12.2 %copy-start.10 = (s32[1,40]{1,0:T(1,128)S(1)}, s32[1,40]{1,0:T(1,128)}, u32[]{:S(2)}) copy-start(s32[1,40]{1,0:T(1,128)} %param.23) | copy-start | bytes 484
  15.5 13.1 %copy-start.8 = (s32[1,40]{1,0:T(1,128)S(1)}, s32[1,40]{1,0:T(1,128)}, u32[]{:S(2)}) copy-start(s32[1,40]{1,0:T(1,128)} %param.22) | copy-start | bytes 484
  16.5 30.2 %all-to-all-start = ((bf16[32,8,1280]{2,1,0:T(8,128)(2,1)}), bf16[32,8,1280]{2,1,0:T(8,128)(2,1)}, u32[]{:S(2)}, u32[]{:S(2)}) async-start(bf16[32,8,1280]{2,1,0:T(8,128)(2,1)} %select_bitcast_fusion.1), calls=%async_computation | async-start | bytes 1310720 | tf_op jit(solution)/shard_map/all_to_all | solution.py:125
  62.0 2.2 copy-start.4
  64.1 1.5 copy-start.2
  65.6 7.4 %copy-start.11 = (bf16[128]{0:T(256)(128)(2,1)S(1)}, bf16[128]{0:T(256)(128)(2,1)}, u32[]{:S(2)}) copy-start(bf16[128]{0:T(256)(128)(2,1)} %param.20) | copy-start | bytes 772
  65.6 7.4 %copy-start.7 = (s32[128,1]{0,1:T(1,128)S(1)}, s32[128,1]{0,1:T(1,128)}, u32[]{:S(2)}) copy-start(s32[128,1]{0,1:T(1,128)} %param.19) | copy-start | bytes 1540
  66.1 26.8 %copy-start.1 = (bf16[128,1280]{1,0:T(8,128)(2,1)S(1)}, bf16[128,1280]{1,0:T(8,128)(2,1)}, u32[]{:S(2)}) copy-start(bf16[128,1280]{1,0:T(8,128)(2,1)} %param.17) | copy-start | bytes 983044
  66.1 26.8 %copy-start.6 = (bf16[128,1280]{1,0:T(8,128)(2,1)S(1)}, bf16[128,1280]{1,0:T(8,128)(2,1)}, u32[]{:S(2)}) copy-start(bf16[128,1280]{1,0:T(8,128)(2,1)} %param.18) | copy-start | bytes 983044
  67.4 24.7 %all-to-all-start.1 = ((bf16[32,8,1280]{2,1,0:T(8,128)(2,1)}), bf16[32,8,1280]{2,1,0:T(8,128)(2,1)S(1)}, u32[]{:S(2)}, u32[]{:S(2)}) async-start(bf16[32,8,1280]{2,1,0:T(8,128)(2,1)} %convert_element_type.81), calls=%async_computation.1 | async-start | bytes 1310720 | tf_op jit(solution)/shard_map/all_to_all | solution.py:137
  72.9 131.1 %reduce-scatter.5.cloned.1.call-start = ((), (), s32[]{:S(2)}) async-start(), calls=%async_computation.7 | async-start | bytes 1474560 | tf_op jit(solution)/shard_map/reduce_scatter | solution.py:176
  120.6 3.9 %copy-start.5 = (bf16[1,40,128,128]{3,2,1,0:T(8,128)(2,1)S(1)}, bf16[1,40,128,128]{3,2,1,0:T(8,128)(2,1)}, u32[]{:S(2)}) copy-start(bf16[1,40,128,128]{3,2,1,0:T(8,128)(2,1)} %param.24) | copy-start | bytes 3932164
  142.1 1.5 copy-start.3
  149.7 24.8 %all-to-all-start.3 = ((bf16[32,8,1280]{2,1,0:T(8,128)(2,1)}), bf16[32,8,1280]{2,1,0:T(8,128)(2,1)S(1)}, u32[]{:S(2)}, u32[]{:S(2)}) async-start(bf16[32,8,1280]{2,1,0:T(8,128)(2,1)} %convert_element_type.89), calls=%async_computation.3 | async-start | bytes 1310720 | tf_op jit(solution)/shard_map/all_to_all | solution.py:166
  155.4 131.1 %reduce-scatter.3.cloned.1.call-start = ((), (), s32[]{:S(2)}) async-start(), calls=%async_computation.6 | async-start | bytes 1474560 | tf_op jit(solution)/shard_map/reduce_scatter | solution.py:173
Sparse Core Ops, SparseCore 0:
  127.8 76.1 reduce-scatter.4
  208.6 77.8 reduce-scatter.2
where the time goes:
time: 296 us; the launch traced here: 295 us
  waiting for transfers between devices  159 us (54%)
  matrix products  33.7 us (11%)
  blocking collectives  24.4 us (8%)
  starting transfers between devices  22.5 us (8%)
  other arithmetic  20.9 us (7%)
  local copies, waits for them, and re-layouts  20.3 us (7%)
  between operations  14.4 us (5%)
    reduce_scatter x1, waiting for transfers between devices, local(): lax.psum_scatter(grad_in.astype(jnp.bfloat16), 'dp', scatter_dimension=0,...  80.8 us
    reduce_scatter x1, waiting for transfers between devices, local(): lax.psum_scatter(grad_out.astype(jnp.bfloat16), 'dp', scatter_dimension=0...  26.6 us
    all_to_all x1, blocking collectives, local(): lax.all_to_all(to_slots(grad_expert), 'expert', split_axis=0, concat_axis...  24.4 us
    all_to_all x1, waiting for transfers between devices, local(): lax.all_to_all(scatter_rows(produced_rows), 'expert', split_axis=0, conca...  19 us
    all_to_all x1, waiting for transfers between devices, local(): lax.all_to_all(to_slots(normed), 'expert', split_axis=0, concat_axis=0, t...  18.1 us
    all_to_all x1, waiting for transfers between devices, local(): lax.all_to_all(scatter_rows(grad_rows), 'expert', split_axis=0, concat_ax...  14.3 us
    all_to_all x1, starting transfers between devices, local(): lax.all_to_all(to_slots(normed), 'expert', split_axis=0, concat_axis=0, t...  11.2 us
    dot_general x1, matrix products, expert_backward(): jnp.einsum('rmf,mb->rbf', backward, gather_matrix, precision=lax.Precisio...  8.58 us
  transfers between devices with their start and end apart: 5, of which 5 were waited for; matrix products, arithmetic and copies ran while one was open for 11% of the time, Pallas kernels for 0%

commit v1 on v0

v1 whole, which is shorter than its diff:
```python
import jax
import jax.numpy as jnp
from jax import lax
from jax.experimental import pallas as pl
from jax.experimental.pallas import tpu as pltpu
from jax.sharding import PartitionSpec as P

BLK = 128
K2 = 4
DB = 10
FB = 40
D = DB * BLK
SLOT = 8
EPS = 1e-06
GELU_K = 0.7978845608028654
GELU_C = 0.044715
F32 = jnp.float32
BF16 = jnp.bfloat16
NT = (((1,), (1,)), ((), ()))


def dot(a, b):
    return jnp.dot(a, b, preferred_element_type=F32)


def dot_nt(a, b):
    return lax.dot_general(a, b, NT, preferred_element_type=F32)


def slot_matrix(route_row, owners):
    rows = route_row.shape[1]
    slots = owners * SLOT
    expert = lax.broadcasted_iota(jnp.int32, (owners, rows), 0)
    hits = expert == route_row
    first = lax.broadcasted_iota(jnp.int32, (rows, rows), 0)
    second = lax.broadcasted_iota(jnp.int32, (rows, rows), 1)
    before = dot(hits.astype(BF16), (first < second).astype(BF16))
    rank = jnp.sum(jnp.where(hits, before, 0.0), axis=0, keepdims=True).astype(jnp.int32)
    slot_row = route_row * SLOT + rank
    slot = lax.broadcasted_iota(jnp.int32, (slots, rows), 0)
    return slot == slot_row


def pack_kernel(route_ref, gates_ref, patches_ref, teacher_ref, out_ref):
    owners = out_ref.shape[0] // SLOT
    place = slot_matrix(route_ref[...], owners)
    one_hot = place.astype(BF16)
    out_ref[:, :D] = dot(one_hot, patches_ref[...]).astype(BF16)
    out_ref[:, D : 2 * D] = dot(one_hot, teacher_ref[...]).astype(BF16)
    gates = jnp.broadcast_to(gates_ref[...].astype(F32), place.shape)
    gate = jnp.sum(jnp.where(place, gates, 0.0), axis=1, keepdims=True)
    out_ref[:, 2 * D :] = jnp.broadcast_to(gate, (place.shape[0], BLK)).astype(BF16)


def expert_kernel(
    in_rows,
    in_cols,
    out_rows,
    where_ref,
    pay_ref,
    w_in_ref,
    w_out_ref,
    ret_ref,
    *rest,
):
    n_x = len(rest) - 9
    parts = rest[:n_x]
    xn, xnt, hid, slope, gh, gn, grads, gate, sems = rest[n_x:]
    share = FB // n_x
    half = share // 2
    my_x, my_y = where_ref[0], where_ref[1]

    def place(block, kind):
        x = block // share
        y = (block % share) // half
        rel_x = lax.rem(x - my_x + n_x, n_x)
        rel_y = lax.rem(y - my_y + 2, 2)
        return rel_x, rel_y * share + kind * half + block % half

    feats = pay_ref[:, :D].astype(F32)
    centred = feats - jnp.mean(feats, axis=-1, keepdims=True)
    variance = jnp.mean(centred * centred, axis=-1, keepdims=True)
    normed = centred * lax.rsqrt(variance + EPS)
    for i in range(DB):
        piece = normed[:, i * BLK : (i + 1) * BLK]
        xn[i] = piece.astype(BF16)
        xnt[i] = piece.T.astype(BF16)
    gn[...] = jnp.zeros_like(gn)
    gate[...] = pay_ref[:, 2 * D :].astype(F32)

    def forward(step, carry):
        for q in range(4):
            b = step * 4 + q
            c = in_cols[b]
            v = dot(xn[in_rows[b]], w_in_ref[b])
            v2 = v * v
            t = jnp.tanh(GELU_K * v * (1.0 + GELU_C * v2))
            half_p = 0.5 + 0.5 * t
            hid[c] = (v * half_p).astype(BF16)
            slope[c] = half_p + (0.5 * GELU_K) * v * (1.0 - t * t) * (1.0 + (3.0 * GELU_C) * v2)
            gh[c] = jnp.zeros_like(v)
        return carry

    lax.fori_loop(0, FB // 4, forward, 0)

    for j in range(DB):
        lanes = slice(j * BLK, (j + 1) * BLK)
        reads = [out_rows[K2 * j + k] for k in range(K2)]
        spread = jnp.concatenate([hid[r] for r in reads], axis=1)
        weight = w_out_ref[K2 * j : K2 * (j + 1)].reshape(K2 * BLK, BLK)
        produced = dot(spread, weight).astype(BF16)
        ret_ref[:, lanes] = produced
        g = gate[...]
        summed = pay_ref[:, lanes].astype(F32) + g * produced.astype(F32)
        mismatch = summed - pay_ref[:, D + j * BLK : D + (j + 1) * BLK].astype(F32)
        grad = g * mismatch
        grad_b = grad.astype(BF16)
        grad_t = grad.T.astype(BF16)
        outer = dot(grad_t, spread)
        back = dot_nt(grad_b, weight)
        for k in range(K2):
            rel_x, pos = place(K2 * j + k, 1)
            grads[rel_x, pos] = outer[:, k * BLK : (k + 1) * BLK].astype(BF16)
            gh[reads[k]] += back[:, k * BLK : (k + 1) * BLK]

    def backward(step, carry):
        for q in range(4):
            b = step * 4 + q
            c = in_cols[b]
            i = in_rows[b]
            grad_pre = (gh[c] * slope[c]).astype(BF16)
            rel_x, pos = place(b, 0)
            grads[rel_x, pos] = dot(xnt[i], grad_pre).astype(BF16)
            gn[i] += dot_nt(grad_pre, w_in_ref[b])
        return carry

    lax.fori_loop(0, FB // 4, backward, 0)

    copies = [
        pltpu.make_async_copy(grads.at[k], part, sems.at[k]) for k, part in enumerate(parts)
    ]
    for copy in copies:
        copy.start()
    for i in range(DB):
        ret_ref[:, D + i * BLK : D + (i + 1) * BLK] = gn[i].astype(BF16)
    for copy in copies:
        copy.wait()


def finish_kernel(route_ref, gates_ref, patches_ref, teacher_ref, ret_ref, student_ref, grad_ref):
    owners = ret_ref.shape[0] // SLOT
    place = slot_matrix(route_ref[...], owners).astype(F32)
    pick = place.T
    gates = gates_ref[...].astype(F32)
    gated = jnp.broadcast_to(gates, place.shape) * place
    gate = jnp.sum(gated.T, axis=1, keepdims=True)
    pick = pick.astype(BF16)
    feats = patches_ref[...].astype(F32)
    summed = feats + gate * dot(pick, ret_ref[:, :D])
    student_ref[...] = summed.astype(BF16)
    mismatch = summed - teacher_ref[...].astype(F32)
    grad = dot(pick, ret_ref[:, D:])
    centred = feats - jnp.mean(feats, axis=-1, keepdims=True)
    variance = jnp.mean(centred * centred, axis=-1, keepdims=True)
    scale = lax.rsqrt(variance + EPS)
    normed = centred * scale
    mean_grad = jnp.mean(grad, axis=-1, keepdims=True)
    mean_both = jnp.mean(grad * normed, axis=-1, keepdims=True)
    grad_ref[...] = mismatch + scale * (grad - mean_grad - normed * mean_both)


def shift(n_x, dx, dy):
    return [
        (x * 2 + y, ((x + dx) % n_x) * 2 + (y + dy) % 2) for x in range(n_x) for y in range(2)
    ]


VMEM_SPEC = pl.BlockSpec(memory_space=pltpu.VMEM)
SMEM_SPEC = pl.BlockSpec(memory_space=pltpu.SMEM)
ANY_SPEC = pl.BlockSpec(memory_space=pl.ANY)


def local(patches, teacher, route, gates, w_in, in_rows, in_cols, w_out, out_rows):
    rows = patches.shape[0]
    owners = lax.axis_size("expert")
    n_x = lax.axis_size("dp") // 2
    slots = owners * SLOT
    share = FB // n_x
    route_row = route.reshape(1, rows)
    gates_row = gates.reshape(1, rows)
    payload = pl.pallas_call(
        pack_kernel,
        out_shape=jax.ShapeDtypeStruct((slots, 2 * D + BLK), BF16),
        in_specs=[VMEM_SPEC] * 4,
        out_specs=VMEM_SPEC,
        compiler_params=pltpu.CompilerParams(vmem_limit_bytes=16 << 20),
        name="pack",
    )(route_row, gates_row, patches, teacher)

    def exchange(values):
        width = values.shape[1]
        blocks = values.reshape(owners, SLOT, width)
        out = lax.all_to_all(blocks, "expert", split_axis=0, concat_axis=0, tiled=True)
        return out.reshape(slots, width)

    arrived = exchange(payload)
    me = lax.axis_index("dp")
    where = jnp.stack([me // 2, me % 2]).astype(jnp.int32)
    part = jax.ShapeDtypeStruct((2 * share, BLK, BLK), BF16)
    returned, *parts = pl.pallas_call(
        expert_kernel,
        out_shape=(jax.ShapeDtypeStruct((slots, 2 * D), BF16),) + (part,) * n_x,
        in_specs=[SMEM_SPEC] * 4 + [VMEM_SPEC] * 3,
        out_specs=(VMEM_SPEC,) + (ANY_SPEC,) * n_x,
        scratch_shapes=[
            pltpu.VMEM((DB, slots, BLK), BF16),
            pltpu.VMEM((DB, BLK, slots), BF16),
            pltpu.VMEM((FB, slots, BLK), BF16),
            pltpu.VMEM((FB, slots, BLK), F32),
            pltpu.VMEM((FB, slots, BLK), F32),
            pltpu.VMEM((DB, slots, BLK), F32),
            pltpu.VMEM((n_x, 2 * share, BLK, BLK), BF16),
            pltpu.VMEM((slots, BLK), F32),
            pltpu.SemaphoreType.DMA((n_x,)),
        ],
        compiler_params=pltpu.CompilerParams(vmem_limit_bytes=44 << 20),
        name="expert",
    )(in_rows[0], in_cols[0], out_rows[0], where, arrived, w_in[0], w_out[0])

    back = exchange(returned)
    total = parts[0].astype(F32)
    for dx in (2, 1, 3):
        total = total + lax.ppermute(parts[dx], "dp", shift(n_x, dx, 0)).astype(F32)
    other = lax.ppermute(total[share:].astype(BF16), "dp", shift(n_x, 0, 1))
    total = total[:share] + other.astype(F32)
    half = share // 2
    part_in = total[:half]
    part_out = jnp.swapaxes(total[half:], 1, 2)

    student, grad_patches = pl.pallas_call(
        finish_kernel,
        out_shape=(
            jax.ShapeDtypeStruct((rows, D), BF16),
            jax.ShapeDtypeStruct((rows, D), F32),
        ),
        in_specs=[VMEM_SPEC] * 5,
        out_specs=(VMEM_SPEC, VMEM_SPEC),
        compiler_params=pltpu.CompilerParams(vmem_limit_bytes=16 << 20),
        name="finish",
    )(route_row, gates_row, patches, teacher, back)
    return (student, grad_patches, part_in[None], part_out[None])


def solution(mesh):
    placed = (
        P(("dp", "expert"), None),
        P(("dp", "expert"), None),
        P(("dp", "expert"), None),
        P(("dp", "expert")),
        P("expert", None, None, None),
        P("expert", None),
        P("expert", None),
        P("expert", None, None, None),
        P("expert", None),
    )
    return jax.shard_map(
        local,
        mesh=mesh,
        in_specs=placed,
        out_specs=(
            P(("dp", "expert"), None),
            P(("dp", "expert"), None),
            P("expert", "dp", None, None),
            P("expert", "dp", None, None),
        ),
        check_vma=False,
    )
```

time: 296 us -> 123 us (0.42)
  waiting for transfers between devices: 159 us -> 68.6 us
  matrix products: 33.7 us -> 0 us
  blocking collectives: 24.4 us -> 0 us
  other arithmetic: 20.9 us -> 0.57 us
  Pallas kernels: 0 us -> 17.2 us
  between operations: 14.4 us -> 0.8 us
  local copies, waits for them, and re-layouts: 20.3 us -> 9.93 us
    reduce_scatter x2 -> x0, waiting for transfers between devices: 107 us -> none  [the longest x1 80.8 us: local(): lax.psum_scatter(grad_in.astype(jnp.bfloat16), 'dp', scatter_dimension=0,...]
    ppermute x0 -> x4, waiting for transfers between devices: none -> 34.6 us  [the longest x3 27 us: local(): total = total + lax.ppermute(parts[dx], 'dp', shift(n_x, dx, 0)).astype(F32)]
    dot_general x8 -> x0, matrix products: 33.7 us -> none  [the longest x1 8.58 us: expert_backward(): jnp.einsum('rmf,mb->rbf', backward, gather_matrix, precision=lax.Precisio...]
    all_to_all x1 -> x0, blocking collectives: 24.4 us -> none  [local(): lax.all_to_all(to_slots(grad_expert), 'expert', split_axis=0, concat_axis...]
    all_to_all x3 -> x2, waiting for transfers between devices: 51.4 us -> 34 us  [exchange(): lax.all_to_all(blocks, 'expert', split_axis=0, concat_axis=0, tiled=True)]
    pallas_call x0 -> x3, Pallas kernels: none -> 17.2 us  [the longest x1 13.7 us: local(): pl.pallas_call(expert_kernel, out_shape=(jax.ShapeDtypeStruct((slots, 2 *...]
    gather x7 -> x0, local copies, waits for them, and re-layouts: 11.9 us -> none  [the longest x1 4.34 us: expert_hidden(): jnp.take(hidden, read_blocks, axis=1).reshape(row_count, DB, K2, BLK)]
    convert_element_type x5 -> x0, other arithmetic: 8.17 us -> none  [the longest x1 5.81 us: expert_backward(): grad_pre = pullback(grad_hidden)[0].astype(jnp.bfloat16)]
  transfers between devices with their start and end apart: 5 -> 6, of which waited for: 5 -> 4; matrix products, arithmetic and copies ran while one was open for 11% -> 2% of each run, Pallas kernels for 0% -> 0%
where the time goes in v1:
time: 123 us; the launch traced here: 122 us
  waiting for transfers between devices  68.6 us (56%)
  starting transfers between devices  24.9 us (20%)
  Pallas kernels  17.2 us (14%)
  local copies, waits for them, and re-layouts  9.93 us (8%)
    all_to_all x2, waiting for transfers between devices, exchange(): lax.all_to_all(blocks, 'expert', split_axis=0, concat_axis=0, tiled=True)  34 us
    ppermute x3, waiting for transfers between devices, local(): total = total + lax.ppermute(parts[dx], 'dp', shift(n_x, dx, 0)).astype(F32)  27 us
    all_to_all x2, starting transfers between devices, exchange(): lax.all_to_all(blocks, 'expert', split_axis=0, concat_axis=0, tiled=True)  16.8 us
    pallas_call x1, Pallas kernels, local(): pl.pallas_call(expert_kernel, out_shape=(jax.ShapeDtypeStruct((slots, 2 *...  13.7 us
    unnamed x39, local copies, waits for them, and re-layouts  9.11 us
    ppermute x1, waiting for transfers between devices, local(): other = lax.ppermute(total[share:].astype(BF16), 'dp', shift(n_x, 0, 1))  7.53 us
    ppermute x3, starting transfers between devices, local(): total = total + lax.ppermute(parts[dx], 'dp', shift(n_x, dx, 0)).astype(F32)  5.46 us
    ppermute x1, starting transfers between devices, local(): other = lax.ppermute(total[share:].astype(BF16), 'dp', shift(n_x, 0, 1))  2.71 us
  transfers between devices with their start and end apart: 6, of which 4 were waited for; matrix products, arithmetic and copies ran while one was open for 2% of the time, Pallas kernels for 0%

profile of v1, /device:TPU:1, one launch (start us, length us, event | category | flops | bytes accessed | tf_op | source)
XLA Modules:
  0.0 122.0 jit_solution(3911733809198390978)
XLA Ops:
  0.6 0.0 copy-start.2
  0.6 1.0 copy-done.2
  1.6 0.0 copy-start.4
  1.6 1.0 copy-done.4
  2.6 0.7 copy-done.7
  3.2 0.7 copy-done.9
  3.9 1.7 %pack.1 = bf16[256,2688]{1,0:T(8,128)(2,1)} custom-call(s32[1,128]{1,0:T(1,128)S(1)} %bitcast.24, bf16[1,128]{1,0:T(2,128)(2,1)S(1)} %bitcast.26, bf16[128,1280]{1,0:T(8,128)(2,1)S(1)} %copy-done.2, bf16[128,1280]{1,0:T(8,128)(2,1)S(1)} %copy-done.4), custom_call_target="tpu_custom_call" | custom-call | tf_op jit(solution)/shard_map/pack/pallas_call | solution.py:191
  5.6 11.3 %all-to-all-start = ((bf16[32,8,2688]{2,1,0:T(8,128)(2,1)}), bf16[32,8,2688]{2,1,0:T(8,128)(2,1)S(1)}, u32[]{:S(2)}, u32[]{:S(2)}) async-start(bf16[32,8,2688]{2,1,0:T(8,128)(2,1)} %bitcast.7), calls=%async_computation | async-start | bytes 2752512 | tf_op jit(solution)/shard_map/all_to_all | solution.py:203
  16.9 0.1 pad_add_fusion.where_ref
  17.0 34.0 %all-to-all-done = bf16[32,8,2688]{2,1,0:T(8,128)(2,1)S(1)} async-done(((bf16[32,8,2688]{2,1,0:T(8,128)(2,1)}), bf16[32,8,2688]{2,1,0:T(8,128)(2,1)S(1)}, u32[]{:S(2)}, u32[]{:S(2)}) %all-to-all-start) | async-done | bytes 1376288 | tf_op jit(solution)/shard_map/all_to_all | solution.py:203
  51.0 0.0 copy-done
  51.0 0.0 copy-done.11
  51.1 0.0 copy-done.12
  51.1 0.0 copy-done.13
  51.1 0.0 copy-start.1
  51.1 1.3 %copy-done.1 = bf16[1,40,128,128]{3,2,1,0:T(8,128)(2,1)S(1)} copy-done((bf16[1,40,128,128]{3,2,1,0:T(8,128)(2,1)S(1)}, bf16[1,40,128,128]{3,2,1,0:T(8,128)(2,1)}, u32[]{:S(2)}) %copy-start.1) | copy-done | bytes 1310744
  52.4 13.7 %expert.1 = (bf16[256,2560]{1,0:T(8,128)(2,1)S(1)}, bf16[20,128,128]{2,1,0:T(8,128)(2,1)S(1)}, bf16[20,128,128]{2,1,0:T(8,128)(2,1)S(1)}, bf16[20,128,128]{2,1,0:T(8,128)(2,1)S(1)}, bf16[20,128,128]{2,1,0:T(8,128)(2,1)S(1)}) custom-call(s32[40]{0:T(128)S(1)} %bitcast.28, s32[40]{0:T(128)S(1)} %bitcast.29, s32[40]{0:T(128)S(1)} %bitcast.30, ...), custom_call_target="tpu_custom_call" | custom-call | tf_op jit(solution)/shard_map/expert/pallas_call | solution.py:210
  66.1 0.0 copy-start.6
  66.1 1.1 copy-done.6
  67.2 0.8 copy-done.14
  68.1 0.9 copy-done.16
  68.9 0.8 copy-done.18
  69.8 5.5 %all-to-all-start.1 = ((bf16[32,8,2560]{2,1,0:T(8,128)(2,1)}), bf16[32,8,2560]{2,1,0:T(8,128)(2,1)S(1)}, u32[]{:S(2)}, u32[]{:S(2)}) async-start(bf16[32,8,2560]{2,1,0:T(8,128)(2,1)} %bitcast.23), calls=%async_computation.1 | async-start | bytes 2621440 | tf_op jit(solution)/shard_map/all_to_all | solution.py:203
  75.2 2.8 %collective-permute-start = (bf16[20,128,128]{2,1,0:T(8,128)(2,1)}, bf16[20,128,128]{2,1,0:T(8,128)(2,1)S(1)}, u32[]{:S(2)}, u32[]{:S(2)}) collective-permute-start(bf16[20,128,128]{2,1,0:T(8,128)(2,1)} %copy-done.18), channel_id=1, source_target_pairs={{0,128},{32,160},{64,192},{96,224},{128,0},{160,32},{192,64},{224,... | collective-permute-start | bytes 1966088 | tf_op jit(solution)/shard_map/ppermute | solution.py:233
  78.0 0.0 copy-done.17
  78.0 0.4 collective-permute-start.1
  78.4 0.0 copy-done.15
  78.4 2.3 %collective-permute-start.2 = (bf16[20,128,128]{2,1,0:T(8,128)(2,1)S(1)}, bf16[20,128,128]{2,1,0:T(8,128)(2,1)S(1)}, u32[]{:S(2)}, u32[]{:S(2)}) collective-permute-start(bf16[20,128,128]{2,1,0:T(8,128)(2,1)S(1)} %copy-done.15), channel_id=1, source_target_pairs={{0,192},{32,224},{64,0},{96,32},{128,64},{160,96},{192,128},{224,1... | collective-permute-start | bytes 1966088 | tf_op jit(solution)/shard_map/ppermute | solution.py:233
  80.7 12.5 %collective-permute-done = bf16[20,128,128]{2,1,0:T(8,128)(2,1)S(1)} collective-permute-done((bf16[20,128,128]{2,1,0:T(8,128)(2,1)}, bf16[20,128,128]{2,1,0:T(8,128)(2,1)S(1)}, u32[]{:S(2)}, u32[]{:S(2)}) %collective-permute-start) | collective-permute-done | bytes 655392 | tf_op jit(solution)/shard_map/ppermute | solution.py:233
  93.2 14.6 %collective-permute-done.1 = bf16[20,128,128]{2,1,0:T(8,128)(2,1)S(1)} collective-permute-done((bf16[20,128,128]{2,1,0:T(8,128)(2,1)S(1)}, bf16[20,128,128]{2,1,0:T(8,128)(2,1)S(1)}, u32[]{:S(2)}, u32[]{:S(2)}) %collective-permute-start.1) | collective-permute-done | bytes 655392 | tf_op jit(solution)/shard_map/ppermute | solution.py:233
  107.7 0.0 collective-permute-done.2
  107.8 0.4 convert_add_fusion
  108.2 0.1 slice.25
  108.3 2.7 %collective-permute-start.3 = (bf16[10,128,128]{2,1,0:T(8,128)(2,1)S(1)}, bf16[10,128,128]{2,1,0:T(8,128)(2,1)S(1)}, u32[]{:S(2)}, u32[]{:S(2)}) collective-permute-start(bf16[10,128,128]{2,1,0:T(8,128)(2,1)S(1)} %slice.25), channel_id=1, source_target_pairs={{0,32},{32,0},{64,96},{96,64},{128,160},{160,128},{192,224},{224,1... | collective-permute-start | bytes 983048 | tf_op jit(solution)/shard_map/ppermute | solution.py:234
  111.0 7.5 %collective-permute-done.3 = bf16[10,128,128]{2,1,0:T(8,128)(2,1)S(1)} collective-permute-done((bf16[10,128,128]{2,1,0:T(8,128)(2,1)S(1)}, bf16[10,128,128]{2,1,0:T(8,128)(2,1)S(1)}, u32[]{:S(2)}, u32[]{:S(2)}) %collective-permute-start.3) | collective-permute-done | bytes 327712 | tf_op jit(solution)/shard_map/ppermute | solution.py:234
  118.5 0.1 slice_add_fusion
  118.6 0.0 copy-start.3
  118.6 0.0 copy-start.5
  118.6 0.0 copy-start.8
  118.6 0.0 copy-start.10
  118.6 0.8 slice_bitcast_fusion
  119.4 0.9 copy.13
  120.3 0.0 all-to-all-done.1
  120.3 0.0 copy-done.3
  120.3 0.0 copy-done.5
  120.3 0.0 copy-done.8
  120.3 0.0 copy-done.10
  120.3 1.7 %finish.1 = (bf16[128,1280]{1,0:T(8,128)(2,1)}, f32[128,1280]{1,0:T(8,128)}) custom-call(s32[1,128]{1,0:T(1,128)S(1)} %bitcast.25, bf16[1,128]{1,0:T(2,128)(2,1)S(1)} %bitcast.27, bf16[128,1280]{1,0:T(8,128)(2,1)S(1)} %copy-done.3, bf16[128,1280]{1,0:T(8,128)(2,1)S(1)} %copy-done.5, bf16[256,2560]{1,0:T(8,128)(2,1)S(1)} %bitcast.20), custom_call_target="tpu_custom_call" | custom-call | tf_op jit(solution)/shard_map/finish/pallas_call | solution.py:240
  (11 shorter events, 0.0 us)
Async XLA Ops:
  0.6 1.0 copy-start.2
  1.6 1.0 copy-start.4
  2.6 0.7 copy-start.7
  3.2 0.7 copy-start.9
  5.6 45.4 %copy-start = (bf16[1,40,128,128]{3,2,1,0:T(8,128)(2,1)S(1)}, bf16[1,40,128,128]{3,2,1,0:T(8,128)(2,1)}, u32[]{:S(2)}) copy-start(bf16[1,40,128,128]{3,2,1,0:T(8,128)(2,1)} %param.13) | copy-start | bytes 3932164
  5.6 45.4 %copy-start.11 = (s32[1,40]{1,0:T(1,128)S(1)}, s32[1,40]{1,0:T(1,128)}, u32[]{:S(2)}) copy-start(s32[1,40]{1,0:T(1,128)} %param.14) | copy-start | bytes 484
  5.6 45.4 %copy-start.12 = (s32[1,40]{1,0:T(1,128)S(1)}, s32[1,40]{1,0:T(1,128)}, u32[]{:S(2)}) copy-start(s32[1,40]{1,0:T(1,128)} %param.15) | copy-start | bytes 484
  5.6 45.4 %copy-start.13 = (s32[1,40]{1,0:T(1,128)S(1)}, s32[1,40]{1,0:T(1,128)}, u32[]{:S(2)}) copy-start(s32[1,40]{1,0:T(1,128)} %param.17) | copy-start | bytes 484
  5.6 45.4 %all-to-all-start = ((bf16[32,8,2688]{2,1,0:T(8,128)(2,1)}), bf16[32,8,2688]{2,1,0:T(8,128)(2,1)S(1)}, u32[]{:S(2)}, u32[]{:S(2)}) async-start(bf16[32,8,2688]{2,1,0:T(8,128)(2,1)} %bitcast.7), calls=%async_computation | async-start | bytes 2752512 | tf_op jit(solution)/shard_map/all_to_all | solution.py:203
  51.1 1.3 %copy-start.1 = (bf16[1,40,128,128]{3,2,1,0:T(8,128)(2,1)S(1)}, bf16[1,40,128,128]{3,2,1,0:T(8,128)(2,1)}, u32[]{:S(2)}) copy-start(bf16[1,40,128,128]{3,2,1,0:T(8,128)(2,1)} %param.16) | copy-start | bytes 3932164
  66.1 1.1 copy-start.6
  67.2 0.8 copy-start.14
  68.1 0.9 copy-start.16
  68.9 0.8 copy-start.18
  69.8 8.3 %copy-start.17 = (bf16[20,128,128]{2,1,0:T(8,128)(2,1)S(1)}, bf16[20,128,128]{2,1,0:T(8,128)(2,1)}, u32[]{:S(2)}) copy-start(bf16[20,128,128]{2,1,0:T(8,128)(2,1)} %copy-done.16) | copy-start | bytes 1966084
  69.8 8.6 %copy-start.15 = (bf16[20,128,128]{2,1,0:T(8,128)(2,1)S(1)}, bf16[20,128,128]{2,1,0:T(8,128)(2,1)}, u32[]{:S(2)}) copy-start(bf16[20,128,128]{2,1,0:T(8,128)(2,1)} %copy-done.14) | copy-start | bytes 1966084
  69.8 50.5 %all-to-all-start.1 = ((bf16[32,8,2560]{2,1,0:T(8,128)(2,1)}), bf16[32,8,2560]{2,1,0:T(8,128)(2,1)S(1)}, u32[]{:S(2)}, u32[]{:S(2)}) async-start(bf16[32,8,2560]{2,1,0:T(8,128)(2,1)} %bitcast.23), calls=%async_computation.1 | async-start | bytes 2621440 | tf_op jit(solution)/shard_map/all_to_all | solution.py:203
  75.2 17.9 %collective-permute-start = (bf16[20,128,128]{2,1,0:T(8,128)(2,1)}, bf16[20,128,128]{2,1,0:T(8,128)(2,1)S(1)}, u32[]{:S(2)}, u32[]{:S(2)}) collective-permute-start(bf16[20,128,128]{2,1,0:T(8,128)(2,1)} %copy-done.18), channel_id=1, source_target_pairs={{0,128},{32,160},{64,192},{96,224},{128,0},{160,32},{192,64},{224,... | collective-permute-start | bytes 1966088 | tf_op jit(solution)/shard_map/ppermute | solution.py:233
  78.0 29.7 %collective-permute-start.1 = (bf16[20,128,128]{2,1,0:T(8,128)(2,1)S(1)}, bf16[20,128,128]{2,1,0:T(8,128)(2,1)S(1)}, u32[]{:S(2)}, u32[]{:S(2)}) collective-permute-start(bf16[20,128,128]{2,1,0:T(8,128)(2,1)S(1)} %copy-done.17), channel_id=1, source_target_pairs={{0,64},{32,96},{64,128},{96,160},{128,192},{160,224},{192,0},{224,... | collective-permute-start | bytes 1966088 | tf_op jit(solution)/shard_map/ppermute | solution.py:233
  78.4 29.4 %collective-permute-start.2 = (bf16[20,128,128]{2,1,0:T(8,128)(2,1)S(1)}, bf16[20,128,128]{2,1,0:T(8,128)(2,1)S(1)}, u32[]{:S(2)}, u32[]{:S(2)}) collective-permute-start(bf16[20,128,128]{2,1,0:T(8,128)(2,1)S(1)} %copy-done.15), channel_id=1, source_target_pairs={{0,192},{32,224},{64,0},{96,32},{128,64},{160,96},{192,128},{224,1... | collective-permute-start | bytes 1966088 | tf_op jit(solution)/shard_map/ppermute | solution.py:233
  108.3 10.2 %collective-permute-start.3 = (bf16[10,128,128]{2,1,0:T(8,128)(2,1)S(1)}, bf16[10,128,128]{2,1,0:T(8,128)(2,1)S(1)}, u32[]{:S(2)}, u32[]{:S(2)}) collective-permute-start(bf16[10,128,128]{2,1,0:T(8,128)(2,1)S(1)} %slice.25), channel_id=1, source_target_pairs={{0,32},{32,0},{64,96},{96,64},{128,160},{160,128},{192,224},{224,1... | collective-permute-start | bytes 983048 | tf_op jit(solution)/shard_map/ppermute | solution.py:234
  118.6 1.7 %copy-start.3 = (bf16[128,1280]{1,0:T(8,128)(2,1)S(1)}, bf16[128,1280]{1,0:T(8,128)(2,1)}, u32[]{:S(2)}) copy-start(bf16[128,1280]{1,0:T(8,128)(2,1)} %patches_ref.3) | copy-start | bytes 983044
  118.6 1.7 %copy-start.5 = (bf16[128,1280]{1,0:T(8,128)(2,1)S(1)}, bf16[128,1280]{1,0:T(8,128)(2,1)}, u32[]{:S(2)}) copy-start(bf16[128,1280]{1,0:T(8,128)(2,1)} %teacher_ref.3) | copy-start | bytes 983044
  118.6 1.7 %copy-start.8 = (s32[128,1]{0,1:T(1,128)S(1)}, s32[128,1]{0,1:T(1,128)}, u32[]{:S(2)}) copy-start(s32[128,1]{0,1:T(1,128)} %param.11) | copy-start | bytes 1540
  118.6 1.7 %copy-start.10 = (bf16[128]{0:T(256)(128)(2,1)S(1)}, bf16[128]{0:T(256)(128)(2,1)}, u32[]{:S(2)}) copy-start(bf16[128]{0:T(256)(128)(2,1)} %param.12) | copy-start | bytes 772

commit v2 on v1

v2 whole, which is shorter than its diff:
```python
import jax
import jax.numpy as jnp
from jax import lax
from jax.experimental import pallas as pl
from jax.experimental.pallas import tpu as pltpu
from jax.sharding import PartitionSpec as P

BLK = 128
K2 = 4
DB = 10
FB = 40
D = DB * BLK
SLOT = 8
EPS = 1e-06
GELU_K = 0.7978845608028654
GELU_C = 0.044715
F32 = jnp.float32
BF16 = jnp.bfloat16
NT = (((1,), (1,)), ((), ()))


def dot(a, b):
    return jnp.dot(a, b, preferred_element_type=F32)


def dot_nt(a, b):
    return lax.dot_general(a, b, NT, preferred_element_type=F32)


def slot_matrix(route_row, owners):
    rows = route_row.shape[1]
    slots = owners * SLOT
    expert = lax.broadcasted_iota(jnp.int32, (owners, rows), 0)
    hits = expert == route_row
    first = lax.broadcasted_iota(jnp.int32, (rows, rows), 0)
    second = lax.broadcasted_iota(jnp.int32, (rows, rows), 1)
    before = dot(hits.astype(BF16), (first < second).astype(BF16))
    rank = jnp.sum(jnp.where(hits, before, 0.0), axis=0, keepdims=True).astype(jnp.int32)
    slot_row = route_row * SLOT + rank
    slot = lax.broadcasted_iota(jnp.int32, (slots, rows), 0)
    return slot == slot_row


def layer_norm(feats):
    centred = feats - jnp.mean(feats, axis=-1, keepdims=True)
    variance = jnp.mean(centred * centred, axis=-1, keepdims=True)
    scale = lax.rsqrt(variance + EPS)
    return centred * scale, scale


def pack_kernel(route_ref, gates_ref, patches_hbm, teacher_hbm, out_hbm, patches, teacher, out, sems):
    loads = [
        pltpu.make_async_copy(patches_hbm, patches, sems.at[0]),
        pltpu.make_async_copy(teacher_hbm, teacher, sems.at[1]),
    ]
    for load in loads:
        load.start()
    owners = out.shape[0] // SLOT
    place = slot_matrix(route_ref[...], owners)
    one_hot = place.astype(BF16)
    gates = gates_ref[...].astype(F32)
    gate = jnp.sum(jnp.where(place, gates, 0.0), axis=1, keepdims=True)
    out[:, 2 * D :] = jnp.broadcast_to(gate, (place.shape[0], BLK)).astype(BF16)
    loads[0].wait()
    feats = patches[...].astype(F32)
    normed, _ = layer_norm(feats)
    out[:, :D] = dot(one_hot, normed.astype(BF16)).astype(BF16)
    loads[1].wait()
    differ = (feats - teacher[...].astype(F32)).astype(BF16)
    out[:, D : 2 * D] = (gate * dot(one_hot, differ)).astype(BF16)
    store = pltpu.make_async_copy(out, out_hbm, sems.at[2])
    store.start()
    store.wait()


def expert_kernel(
    in_rows,
    in_cols,
    out_rows,
    where_ref,
    pay_ref,
    w_in_ref,
    w_out_hbm,
    ret_hbm,
    *rest,
):
    n_x = len(rest) // 2 - 6
    parts = (rest[:n_x], rest[n_x : 2 * n_x])
    w_out_ref, ret, xnt, hid, slope, gh, gn, grads, gate, load_sem, ret_sems, sems = rest[2 * n_x :]
    share = FB // n_x
    half = share // 2
    my_x, my_y = where_ref[0], where_ref[1]
    load = pltpu.make_async_copy(w_out_hbm, w_out_ref, load_sem.at[0])
    load.start()

    def place(block):
        x = block // share
        y = (block % share) // half
        return lax.rem(x - my_x + n_x, n_x), lax.rem(y - my_y + 2, 2) * half + block % half

    def send(kind):
        copies = [
            pltpu.make_async_copy(grads.at[kind, x], parts[kind][x], sems.at[kind, x])
            for x in range(n_x)
        ]
        copies.append(
            pltpu.make_async_copy(
                ret.at[:, pl.ds((1 - kind) * D, D)],
                ret_hbm.at[:, pl.ds((1 - kind) * D, D)],
                ret_sems.at[kind],
            )
        )
        for copy in copies:
            copy.start()
        return copies

    for i in range(DB):
        xnt[i] = pay_ref[:, i * BLK : (i + 1) * BLK].T
    gn[...] = jnp.zeros_like(gn)
    gate[...] = jnp.square(pay_ref[:, 2 * D :].astype(F32))

    def forward(step, carry):
        for q in range(4):
            b = step * 4 + q
            c = in_cols[b]
            lanes = pl.ds(pl.multiple_of(in_rows[b] * BLK, BLK), BLK)
            v = dot(pay_ref[:, lanes], w_in_ref[b])
            v2 = v * v
            t = jnp.tanh(v * (GELU_K + (GELU_K * GELU_C) * v2))
            half_p = 0.5 + 0.5 * t
            hid[c] = (v * half_p).astype(BF16)
            slope[c] = half_p + v * (1.0 - t * t) * (
                0.5 * GELU_K + (1.5 * GELU_K * GELU_C) * v2
            )
            gh[c] = jnp.zeros_like(v)
        return carry

    lax.fori_loop(0, FB // 4, forward, 0)
    load.wait()

    for j in range(DB):
        lanes = slice(j * BLK, (j + 1) * BLK)
        reads = [out_rows[K2 * j + k] for k in range(K2)]
        spread = jnp.concatenate([hid[r] for r in reads], axis=1)
        weight = w_out_ref[K2 * j : K2 * (j + 1)].reshape(K2 * BLK, BLK)
        produced = dot(spread, weight).astype(BF16)
        ret[:, lanes] = produced
        grad = pay_ref[:, D + j * BLK : D + (j + 1) * BLK].astype(F32) + gate[
            ...
        ] * produced.astype(F32)
        grad_b = grad.astype(BF16)
        outer = dot(grad_b.T, spread)
        back = dot_nt(grad_b, weight)
        for k in range(K2):
            rel_x, pos = place(K2 * j + k)
            grads[1, rel_x, pos] = outer[:, k * BLK : (k + 1) * BLK].astype(BF16)
            gh[reads[k]] += back[:, k * BLK : (k + 1) * BLK]

    copies = send(1)

    def backward(step, carry):
        for q in range(4):
            b = step * 4 + q
            c = in_cols[b]
            i = in_rows[b]
            grad_pre = (gh[c] * slope[c]).astype(BF16)
            rel_x, pos = place(b)
            grads[0, rel_x, pos] = dot(xnt[i], grad_pre).astype(BF16)
            gn[i] += dot_nt(grad_pre, w_in_ref[b])
        return carry

    lax.fori_loop(0, FB // 4, backward, 0)
    for i in range(DB):
        ret[:, D + i * BLK : D + (i + 1) * BLK] = gn[i].astype(BF16)
    copies += send(0)
    for copy in copies:
        copy.wait()


def finish_kernel(route_ref, gates_ref, patches_ref, teacher_ref, ret_ref, student_ref, grad_ref):
    owners = ret_ref.shape[0] // SLOT
    place = slot_matrix(route_ref[...], owners).astype(F32)
    pick = place.T
    gates = gates_ref[...].astype(F32)
    gated = jnp.broadcast_to(gates, place.shape) * place
    gate = jnp.sum(gated.T, axis=1, keepdims=True)
    pick = pick.astype(BF16)
    feats = patches_ref[...].astype(F32)
    summed = feats + gate * dot(pick, ret_ref[:, :D])
    student_ref[...] = summed.astype(BF16)
    mismatch = summed - teacher_ref[...].astype(F32)
    grad = dot(pick, ret_ref[:, D:])
    normed, scale = layer_norm(feats)
    mean_grad = jnp.mean(grad, axis=-1, keepdims=True)
    mean_both = jnp.mean(grad * normed, axis=-1, keepdims=True)
    grad_ref[...] = mismatch + scale * (grad - mean_grad - normed * mean_both)


def total_kernel(mine_in_ref, mine_out_ref, other_ref, in_ref, out_ref):
    half = in_ref.shape[0]
    for q in range(half):
        in_ref[q] = mine_in_ref[q] + other_ref[q].astype(F32)
        out_ref[q] = (mine_out_ref[q] + other_ref[half + q].astype(F32)).T


def shift(n_x, dx, dy):
    return [
        (x * 2 + y, ((x + dx) % n_x) * 2 + (y + dy) % 2) for x in range(n_x) for y in range(2)
    ]


VMEM_SPEC = pl.BlockSpec(memory_space=pltpu.VMEM)
SMEM_SPEC = pl.BlockSpec(memory_space=pltpu.SMEM)
HBM_SPEC = pl.BlockSpec(memory_space=pltpu.HBM)


def local(patches, teacher, route, gates, w_in, in_rows, in_cols, w_out, out_rows):
    rows = patches.shape[0]
    owners = lax.axis_size("expert")
    n_x = lax.axis_size("dp") // 2
    slots = owners * SLOT
    share = FB // n_x
    route_row = route.reshape(1, rows)
    gates_row = gates.reshape(1, rows)
    payload = pl.pallas_call(
        pack_kernel,
        out_shape=jax.ShapeDtypeStruct((slots, 2 * D + BLK), BF16),
        in_specs=[VMEM_SPEC] * 2 + [HBM_SPEC] * 2,
        out_specs=HBM_SPEC,
        scratch_shapes=[
            pltpu.VMEM((rows, D), BF16),
            pltpu.VMEM((rows, D), BF16),
            pltpu.VMEM((slots, 2 * D + BLK), BF16),
            pltpu.SemaphoreType.DMA((3,)),
        ],
        compiler_params=pltpu.CompilerParams(vmem_limit_bytes=60 << 20),
        name="pack",
    )(route_row, gates_row, patches, teacher)

    def exchange(values):
        width = values.shape[1]
        blocks = values.reshape(owners, SLOT, width)
        out = lax.all_to_all(blocks, "expert", split_axis=0, concat_axis=0, tiled=True)
        return out.reshape(slots, width)

    arrived = exchange(payload)
    me = lax.axis_index("dp")
    where = jnp.stack([me // 2, me % 2]).astype(jnp.int32)
    part = jax.ShapeDtypeStruct((share, BLK, BLK), BF16)
    returned, *parts = pl.pallas_call(
        expert_kernel,
        out_shape=(jax.ShapeDtypeStruct((slots, 2 * D), BF16),) + (part,) * (2 * n_x),
        in_specs=[SMEM_SPEC] * 4 + [VMEM_SPEC] * 2 + [HBM_SPEC],
        out_specs=(HBM_SPEC,) * (1 + 2 * n_x),
        scratch_shapes=[
            pltpu.VMEM((FB, BLK, BLK), BF16),
            pltpu.VMEM((slots, 2 * D), BF16),
            pltpu.VMEM((DB, BLK, slots), BF16),
            pltpu.VMEM((FB, slots, BLK), BF16),
            pltpu.VMEM((FB, slots, BLK), F32),
            pltpu.VMEM((FB, slots, BLK), F32),
            pltpu.VMEM((DB, slots, BLK), F32),
            pltpu.VMEM((2, n_x, share, BLK, BLK), BF16),
            pltpu.VMEM((slots, BLK), F32),
            pltpu.SemaphoreType.DMA((1,)),
            pltpu.SemaphoreType.DMA((2,)),
            pltpu.SemaphoreType.DMA((2, n_x)),
        ],
        compiler_params=pltpu.CompilerParams(vmem_limit_bytes=60 << 20),
        name="expert",
    )(in_rows[0], in_cols[0], out_rows[0], where, arrived, w_in[0], w_out[0])
    part_in, part_out = parts[:n_x], parts[n_x:]

    back = exchange(returned)
    half = share // 2

    def pass_on(values, dx, dy=0):
        return lax.ppermute(values, "dp", shift(n_x, dx, dy))

    def add(*values):
        return sum(v.astype(F32) for v in values)

    far_in = pass_on(part_in[2], 1)
    far_out = pass_on(part_out[2], 3)
    near_out = pass_on(part_out[1], 1)
    near_in = pass_on(part_in[3], 3)
    pair_in = pass_on(add(part_in[1], far_in).astype(BF16), 1)
    pair_out = pass_on(add(part_out[3], far_out).astype(BF16), 3)
    total_in = add(part_in[0], near_in, pair_in)
    total_out = add(part_out[0], near_out, pair_out)
    other = pass_on(jnp.concatenate([total_in[half:], total_out[half:]]).astype(BF16), 0, 1)
    block = jax.ShapeDtypeStruct((half, BLK, BLK), F32)
    grad_in, grad_out = pl.pallas_call(
        total_kernel,
        out_shape=(block, block),
        in_specs=[VMEM_SPEC] * 3,
        out_specs=(VMEM_SPEC, VMEM_SPEC),
        compiler_params=pltpu.CompilerParams(vmem_limit_bytes=16 << 20),
        name="total",
    )(total_in[:half], total_out[:half], other)

    student, grad_patches = pl.pallas_call(
        finish_kernel,
        out_shape=(
            jax.ShapeDtypeStruct((rows, D), BF16),
            jax.ShapeDtypeStruct((rows, D), F32),
        ),
        in_specs=[VMEM_SPEC] * 5,
        out_specs=(VMEM_SPEC, VMEM_SPEC),
        compiler_params=pltpu.CompilerParams(vmem_limit_bytes=16 << 20),
        name="finish",
    )(route_row, gates_row, patches, teacher, back)
    return (student, grad_patches, grad_in[None], grad_out[None])


def solution(mesh):
    placed = (
        P(("dp", "expert"), None),
        P(("dp", "expert"), None),
        P(("dp", "expert"), None),
        P(("dp", "expert")),
        P("expert", None, None, None),
        P("expert", None),
        P("expert", None),
        P("expert", None, None, None),
        P("expert", None),
    )
    return jax.shard_map(
        local,
        mesh=mesh,
        in_specs=placed,
        out_specs=(
            P(("dp", "expert"), None),
            P(("dp", "expert"), None),
            P("expert", "dp", None, None),
            P("expert", "dp", None, None),
        ),
        check_vma=False,
    )
```

time: 123 us -> 113 us (0.919)
  local copies, waits for them, and re-layouts: 9.93 us -> 1.27 us
  waiting for transfers between devices: 68.6 us -> 62.3 us
  Pallas kernels: 17.2 us -> 20.8 us
  starting transfers between devices: 24.9 us -> 26.3 us
    unnamed x39 -> x26, local copies, waits for them, and re-layouts: 9.11 us -> 1.18 us
    ppermute x4 -> x7, waiting for transfers between devices: 34.6 us -> 28.8 us  [pass_on(): return lax.ppermute(values, 'dp', shift(n_x, dx, dy))]
    pallas_call x1, Pallas kernels: 1.73 us -> 3.71 us  [local(): pl.pallas_call(pack_kernel, out_shape=jax.ShapeDtypeStruct((slots, 2 * D...]
    ppermute x4 -> x7, starting transfers between devices: 8.16 us -> 9.65 us  [pass_on(): return lax.ppermute(values, 'dp', shift(n_x, dx, dy))]
  transfers between devices with their start and end apart: 6 -> 9, of which waited for: 4 -> 6; matrix products, arithmetic and copies ran while one was open for 2% -> 1% of each run, Pallas kernels for 0% -> 1%
where the time goes in v2:
time: 113 us
  waiting for transfers between devices  62.3 us (55%)
  starting transfers between devices  26.3 us (23%)
  Pallas kernels  20.8 us (18%)
  local copies, waits for them, and re-layouts  1.27 us (1%)
    all_to_all x2, waiting for transfers between devices, exchange(): lax.all_to_all(blocks, 'expert', split_axis=0, concat_axis=0, tiled=True)  33.6 us
    ppermute x7, waiting for transfers between devices, pass_on(): return lax.ppermute(values, 'dp', shift(n_x, dx, dy))  28.8 us
    all_to_all x2, starting transfers between devices, exchange(): lax.all_to_all(blocks, 'expert', split_axis=0, concat_axis=0, tiled=True)  16.6 us
    pallas_call x1, Pallas kernels, local(): pl.pallas_call(expert_kernel, out_shape=(jax.ShapeDtypeStruct((slots, 2 *...  14.4 us
    ppermute x7, starting transfers between devices, pass_on(): return lax.ppermute(values, 'dp', shift(n_x, dx, dy))  9.65 us
    pallas_call x1, Pallas kernels, local(): pl.pallas_call(pack_kernel, out_shape=jax.ShapeDtypeStruct((slots, 2 * D...  3.71 us
  transfers between devices with their start and end apart: 9, of which 6 were waited for; matrix products, arithmetic and copies ran while one was open for 1% of the time, Pallas kernels for 1%

profile of v2, /device:TPU:1, one launch (start us, length us, event | category | flops | bytes accessed | tf_op | source)
XLA Modules:
  0.0 112.5 jit_solution(9939249046575986645)
XLA Ops:
  0.6 3.7 %pack.1 = bf16[256,2688]{1,0:T(8,128)(2,1)} custom-call(s32[1,128]{1,0:T(1,128)} %bitcast.16, bf16[1,128]{1,0:T(2,128)(2,1)} %bitcast.18, bf16[128,1280]{1,0:T(8,128)(2,1)} %patches_ref.1, bf16[128,1280]{1,0:T(8,128)(2,1)} %teacher_ref.1), custom_call_target="tpu_custom_call" | custom-call | tf_op jit(solution)/shard_map/pack/pallas_call | solution.py:225
  4.4 11.1 %all-to-all-start = ((bf16[32,8,2688]{2,1,0:T(8,128)(2,1)}), bf16[32,8,2688]{2,1,0:T(8,128)(2,1)S(1)}, u32[]{:S(2)}, u32[]{:S(2)}) async-start(bf16[32,8,2688]{2,1,0:T(8,128)(2,1)} %bitcast.21), calls=%async_computation | async-start | bytes 2752512 | tf_op jit(solution)/shard_map/all_to_all | solution.py:243
  15.5 0.6 pad_add_fusion.where_ref
  16.1 33.6 %all-to-all-done = bf16[32,8,2688]{2,1,0:T(8,128)(2,1)S(1)} async-done(((bf16[32,8,2688]{2,1,0:T(8,128)(2,1)}), bf16[32,8,2688]{2,1,0:T(8,128)(2,1)S(1)}, u32[]{:S(2)}, u32[]{:S(2)}) %all-to-all-start) | async-done | bytes 1376288 | tf_op jit(solution)/shard_map/all_to_all | solution.py:243
  49.6 1.1 copy-done.4
  50.7 14.4 %expert.1 = (bf16[256,2560]{1,0:T(8,128)(2,1)}, bf16[10,128,128]{2,1,0:T(8,128)(2,1)}, bf16[10,128,128]{2,1,0:T(8,128)(2,1)}, bf16[10,128,128]{2,1,0:T(8,128)(2,...) custom-call(s32[40]{0:T(128)} %bitcast.25, ...), custom_call_target="tpu_custom_call" | custom-call | tf_op jit(solution)/shard_map/expert/pallas_call | solution.py:250
  65.1 0.0 copy-start.12
  65.2 0.0 copy-start.11
  65.2 0.0 copy-start.10
  65.2 0.0 copy-start.8
  65.2 0.0 copy-start.9
  65.2 0.0 copy-start.7
  65.2 5.5 %all-to-all-start.1 = ((bf16[32,8,2560]{2,1,0:T(8,128)(2,1)}), bf16[32,8,2560]{2,1,0:T(8,128)(2,1)S(1)}, u32[]{:S(2)}, u32[]{:S(2)}) async-start(bf16[32,8,2560]{2,1,0:T(8,128)(2,1)} %bitcast.24), calls=%async_computation.1 | async-start | bytes 2621440 | tf_op jit(solution)/shard_map/all_to_all | solution.py:243
  70.7 0.0 copy-start.6
  70.7 0.0 copy-done.12
  70.7 1.3 %collective-permute-start.1 = (bf16[10,128,128]{2,1,0:T(8,128)(2,1)S(1)}, bf16[10,128,128]{2,1,0:T(8,128)(2,1)S(1)}, u32[]{:S(2)}, u32[]{:S(2)}) collective-permute-start(bf16[10,128,128]{2,1,0:T(8,128)(2,1)S(1)} %copy-done.12), channel_id=1, source_target_pairs={{0,64},{32,96},{64,128},{96,160},{128,192},{160,224},{192,0},{224,... | collective-permute-start | bytes 983048 | tf_op jit(solution)/shard_map/ppermute | solution.py:278
  72.0 0.0 copy-done.11
  72.0 1.5 %collective-permute-start.4 = (bf16[10,128,128]{2,1,0:T(8,128)(2,1)S(1)}, bf16[10,128,128]{2,1,0:T(8,128)(2,1)S(1)}, u32[]{:S(2)}, u32[]{:S(2)}) collective-permute-start(bf16[10,128,128]{2,1,0:T(8,128)(2,1)S(1)} %copy-done.11), channel_id=1, source_target_pairs={{0,192},{32,224},{64,0},{96,32},{128,64},{160,96},{192,128},{224,1... | collective-permute-start | bytes 983048 | tf_op jit(solution)/shard_map/ppermute | solution.py:278
  73.5 0.0 copy-done.10
  73.5 1.3 %collective-permute-start = (bf16[10,128,128]{2,1,0:T(8,128)(2,1)S(1)}, bf16[10,128,128]{2,1,0:T(8,128)(2,1)S(1)}, u32[]{:S(2)}, u32[]{:S(2)}) collective-permute-start(bf16[10,128,128]{2,1,0:T(8,128)(2,1)S(1)} %copy-done.10), channel_id=1, source_target_pairs={{0,192},{32,224},{64,0},{96,32},{128,64},{160,96},{192,128},{224,1... | collective-permute-start | bytes 983048 | tf_op jit(solution)/shard_map/ppermute | solution.py:278
  74.8 6.3 %collective-permute-done.1 = bf16[10,128,128]{2,1,0:T(8,128)(2,1)S(1)} collective-permute-done((bf16[10,128,128]{2,1,0:T(8,128)(2,1)S(1)}, bf16[10,128,128]{2,1,0:T(8,128)(2,1)S(1)}, u32[]{:S(2)}, u32[]{:S(2)}) %collective-permute-start.1) | collective-permute-done | bytes 327712 | tf_op jit(solution)/shard_map/ppermute | solution.py:278
  81.1 0.0 copy-done.8
  81.1 0.1 add_convert_fusion.1
  81.2 0.1 collective-permute-start.2
  81.3 0.0 copy-done.9
  81.3 1.2 %collective-permute-start.3 = (bf16[10,128,128]{2,1,0:T(8,128)(2,1)S(1)}, bf16[10,128,128]{2,1,0:T(8,128)(2,1)S(1)}, u32[]{:S(2)}, u32[]{:S(2)}) collective-permute-start(bf16[10,128,128]{2,1,0:T(8,128)(2,1)S(1)} %copy-done.9), channel_id=1, source_target_pairs={{0,64},{32,96},{64,128},{96,160},{128,192},{160,224},{192,0},{224,... | collective-permute-start | bytes 983048 | tf_op jit(solution)/shard_map/ppermute | solution.py:278
  82.5 0.0 collective-permute-done.4
  82.5 0.0 copy-done.7
  82.5 0.1 add_convert_fusion
  82.6 1.6 %collective-permute-start.5 = (bf16[10,128,128]{2,1,0:T(8,128)(2,1)S(1)}, bf16[10,128,128]{2,1,0:T(8,128)(2,1)S(1)}, u32[]{:S(2)}, u32[]{:S(2)}) collective-permute-start(bf16[10,128,128]{2,1,0:T(8,128)(2,1)S(1)} %add_convert_fusion), channel_id=1, source_target_pairs={{0,192},{32,224},{64,0},{96,32},{128,64},{160,96},{192,128},{224,1... | collective-permute-start | bytes 983048 | tf_op jit(solution)/shard_map/ppermute | solution.py:278
  84.2 3.6 %collective-permute-done = bf16[10,128,128]{2,1,0:T(8,128)(2,1)S(1)} collective-permute-done((bf16[10,128,128]{2,1,0:T(8,128)(2,1)S(1)}, bf16[10,128,128]{2,1,0:T(8,128)(2,1)S(1)}, u32[]{:S(2)}, u32[]{:S(2)}) %collective-permute-start) | collective-permute-done | bytes 327712 | tf_op jit(solution)/shard_map/ppermute | solution.py:278
  87.8 2.8 %collective-permute-done.2 = bf16[10,128,128]{2,1,0:T(8,128)(2,1)S(1)} collective-permute-done((bf16[10,128,128]{2,1,0:T(8,128)(2,1)S(1)}, bf16[10,128,128]{2,1,0:T(8,128)(2,1)S(1)}, u32[]{:S(2)}, u32[]{:S(2)}) %collective-permute-start.2) | collective-permute-done | bytes 327712 | tf_op jit(solution)/shard_map/ppermute | solution.py:278
  90.6 0.0 copy-done.6
  90.6 0.1 convert_add_fusion.1
  90.8 6.9 %collective-permute-done.3 = bf16[10,128,128]{2,1,0:T(8,128)(2,1)S(1)} collective-permute-done((bf16[10,128,128]{2,1,0:T(8,128)(2,1)S(1)}, bf16[10,128,128]{2,1,0:T(8,128)(2,1)S(1)}, u32[]{:S(2)}, u32[]{:S(2)}) %collective-permute-start.3) | collective-permute-done | bytes 327712 | tf_op jit(solution)/shard_map/ppermute | solution.py:278
  97.7 0.0 collective-permute-done.5
  97.7 0.0 copy-done.5
  97.7 0.1 convert_add_fusion
  97.9 0.0 copy-start
  97.9 0.0 copy-start.1
  97.9 0.0 copy-start.2
  97.9 0.0 copy-start.3
  97.9 2.7 %collective-permute-start.6 = (bf16[10,128,128]{2,1,0:T(8,128)(2,1)S(1)}, bf16[10,128,128]{2,1,0:T(8,128)(2,1)S(1)}, u32[]{:S(2)}, u32[]{:S(2)}) collective-permute-start(bf16[10,128,128]{2,1,0:T(8,128)(2,1)S(1)} %pad_maximum_fusion), channel_id=1, source_target_pairs={{0,32},{32,0},{64,96},{96,64},{128,160},{160,128},{192,224},{224,1... | collective-permute-start | bytes 983048 | tf_op jit(solution)/shard_map/ppermute | solution.py:278
  100.7 9.1 %collective-permute-done.6.other_ref = bf16[10,128,128]{2,1,0:T(8,128)(2,1)S(1)} collective-permute-done((bf16[10,128,128]{2,1,0:T(8,128)(2,1)S(1)}, bf16[10,128,128]{2,1,0:T(8,128)(2,1)S(1)}, u32[]{:S(2)}, u32[]{:S(2)}) %collective-permute-start.6) | collective-permute-done | bytes 327712 | tf_op jit(solution)/shard_map/ppermute | solution.py:278
  109.8 1.0 total.1
  110.8 0.0 all-to-all-done.1
  110.8 0.0 copy-done
  110.8 1.7 %finish.1 = (bf16[128,1280]{1,0:T(8,128)(2,1)}, f32[128,1280]{1,0:T(8,128)}) custom-call(s32[1,128]{1,0:T(1,128)S(1)} %bitcast.17, bf16[1,128]{1,0:T(2,128)(2,1)S(1)} %bitcast.19, bf16[128,1280]{1,0:T(8,128)(2,1)S(1)} %copy-done, bf16[128,1280]{1,0:T(8,128)(2,1)S(1)} %copy-done.1, bf16[256,2560]{1,0:T(8,128)(2,1)S(1)} %bitcast.15), custom_call_target="tpu_custom_call" | custom-call | tf_op jit(solution)/shard_map/finish/pallas_call | solution.py:302
  (10 shorter events, 0.1 us)
Async XLA Ops:
  4.4 45.3 %all-to-all-start = ((bf16[32,8,2688]{2,1,0:T(8,128)(2,1)}), bf16[32,8,2688]{2,1,0:T(8,128)(2,1)S(1)}, u32[]{:S(2)}, u32[]{:S(2)}) async-start(bf16[32,8,2688]{2,1,0:T(8,128)(2,1)} %bitcast.21), calls=%async_computation | async-start | bytes 2752512 | tf_op jit(solution)/shard_map/all_to_all | solution.py:243
  49.6 1.1 copy-start.4
  65.1 5.6 %copy-start.12 = (bf16[10,128,128]{2,1,0:T(8,128)(2,1)S(1)}, bf16[10,128,128]{2,1,0:T(8,128)(2,1)}, u32[]{:S(2)}) copy-start(bf16[10,128,128]{2,1,0:T(8,128)(2,1)} %get-tuple-element.23) | copy-start | bytes 983044
  65.2 6.9 %copy-start.11 = (bf16[10,128,128]{2,1,0:T(8,128)(2,1)S(1)}, bf16[10,128,128]{2,1,0:T(8,128)(2,1)}, u32[]{:S(2)}) copy-start(bf16[10,128,128]{2,1,0:T(8,128)(2,1)} %get-tuple-element.27) | copy-start | bytes 983044
  65.2 8.3 %copy-start.10 = (bf16[10,128,128]{2,1,0:T(8,128)(2,1)S(1)}, bf16[10,128,128]{2,1,0:T(8,128)(2,1)}, u32[]{:S(2)}) copy-start(bf16[10,128,128]{2,1,0:T(8,128)(2,1)} %get-tuple-element.21) | copy-start | bytes 983044
  65.2 15.9 %copy-start.8 = (bf16[10,128,128]{2,1,0:T(8,128)(2,1)S(1)}, bf16[10,128,128]{2,1,0:T(8,128)(2,1)}, u32[]{:S(2)}) copy-start(bf16[10,128,128]{2,1,0:T(8,128)(2,1)} %get-tuple-element.22) | copy-start | bytes 983044
  65.2 16.1 %copy-start.9 = (bf16[10,128,128]{2,1,0:T(8,128)(2,1)S(1)}, bf16[10,128,128]{2,1,0:T(8,128)(2,1)}, u32[]{:S(2)}) copy-start(bf16[10,128,128]{2,1,0:T(8,128)(2,1)} %get-tuple-element.25) | copy-start | bytes 983044
  65.2 17.3 %copy-start.7 = (bf16[10,128,128]{2,1,0:T(8,128)(2,1)S(1)}, bf16[10,128,128]{2,1,0:T(8,128)(2,1)}, u32[]{:S(2)}) copy-start(bf16[10,128,128]{2,1,0:T(8,128)(2,1)} %get-tuple-element.26) | copy-start | bytes 983044
  65.2 45.6 %all-to-all-start.1 = ((bf16[32,8,2560]{2,1,0:T(8,128)(2,1)}), bf16[32,8,2560]{2,1,0:T(8,128)(2,1)S(1)}, u32[]{:S(2)}, u32[]{:S(2)}) async-start(bf16[32,8,2560]{2,1,0:T(8,128)(2,1)} %bitcast.24), calls=%async_computation.1 | async-start | bytes 2621440 | tf_op jit(solution)/shard_map/all_to_all | solution.py:243
  70.7 19.9 %copy-start.6 = (bf16[10,128,128]{2,1,0:T(8,128)(2,1)S(1)}, bf16[10,128,128]{2,1,0:T(8,128)(2,1)}, u32[]{:S(2)}) copy-start(bf16[10,128,128]{2,1,0:T(8,128)(2,1)} %get-tuple-element.20) | copy-start | bytes 983044
  70.7 10.4 %collective-permute-start.1 = (bf16[10,128,128]{2,1,0:T(8,128)(2,1)S(1)}, bf16[10,128,128]{2,1,0:T(8,128)(2,1)S(1)}, u32[]{:S(2)}, u32[]{:S(2)}) collective-permute-start(bf16[10,128,128]{2,1,0:T(8,128)(2,1)S(1)} %copy-done.12), channel_id=1, source_target_pairs={{0,64},{32,96},{64,128},{96,160},{128,192},{160,224},{192,0},{224,... | collective-permute-start | bytes 983048 | tf_op jit(solution)/shard_map/ppermute | solution.py:278
  72.0 10.5 %collective-permute-start.4 = (bf16[10,128,128]{2,1,0:T(8,128)(2,1)S(1)}, bf16[10,128,128]{2,1,0:T(8,128)(2,1)S(1)}, u32[]{:S(2)}, u32[]{:S(2)}) collective-permute-start(bf16[10,128,128]{2,1,0:T(8,128)(2,1)S(1)} %copy-done.11), channel_id=1, source_target_pairs={{0,192},{32,224},{64,0},{96,32},{128,64},{160,96},{192,128},{224,1... | collective-permute-start | bytes 983048 | tf_op jit(solution)/shard_map/ppermute | solution.py:278
  73.5 14.3 %collective-permute-start = (bf16[10,128,128]{2,1,0:T(8,128)(2,1)S(1)}, bf16[10,128,128]{2,1,0:T(8,128)(2,1)S(1)}, u32[]{:S(2)}, u32[]{:S(2)}) collective-permute-start(bf16[10,128,128]{2,1,0:T(8,128)(2,1)S(1)} %copy-done.10), channel_id=1, source_target_pairs={{0,192},{32,224},{64,0},{96,32},{128,64},{160,96},{192,128},{224,1... | collective-permute-start | bytes 983048 | tf_op jit(solution)/shard_map/ppermute | solution.py:278
  81.2 9.4 %collective-permute-start.2 = (bf16[10,128,128]{2,1,0:T(8,128)(2,1)S(1)}, bf16[10,128,128]{2,1,0:T(8,128)(2,1)S(1)}, u32[]{:S(2)}, u32[]{:S(2)}) collective-permute-start(bf16[10,128,128]{2,1,0:T(8,128)(2,1)S(1)} %add_convert_fusion.1), channel_id=1, source_target_pairs={{0,64},{32,96},{64,128},{96,160},{128,192},{160,224},{192,0},{224,... | collective-permute-start | bytes 983048 | tf_op jit(solution)/shard_map/ppermute | solution.py:278
  81.3 16.4 %collective-permute-start.3 = (bf16[10,128,128]{2,1,0:T(8,128)(2,1)S(1)}, bf16[10,128,128]{2,1,0:T(8,128)(2,1)S(1)}, u32[]{:S(2)}, u32[]{:S(2)}) collective-permute-start(bf16[10,128,128]{2,1,0:T(8,128)(2,1)S(1)} %copy-done.9), channel_id=1, source_target_pairs={{0,64},{32,96},{64,128},{96,160},{128,192},{160,224},{192,0},{224,... | collective-permute-start | bytes 983048 | tf_op jit(solution)/shard_map/ppermute | solution.py:278
  82.5 15.2 %copy-start.5 = (bf16[10,128,128]{2,1,0:T(8,128)(2,1)S(1)}, bf16[10,128,128]{2,1,0:T(8,128)(2,1)}, u32[]{:S(2)}) copy-start(bf16[10,128,128]{2,1,0:T(8,128)(2,1)} %get-tuple-element.24) | copy-start | bytes 983044
  82.6 15.1 %collective-permute-start.5 = (bf16[10,128,128]{2,1,0:T(8,128)(2,1)S(1)}, bf16[10,128,128]{2,1,0:T(8,128)(2,1)S(1)}, u32[]{:S(2)}, u32[]{:S(2)}) collective-permute-start(bf16[10,128,128]{2,1,0:T(8,128)(2,1)S(1)} %add_convert_fusion), channel_id=1, source_target_pairs={{0,192},{32,224},{64,0},{96,32},{128,64},{160,96},{192,128},{224,1... | collective-permute-start | bytes 983048 | tf_op jit(solution)/shard_map/ppermute | solution.py:278
  97.9 12.9 %copy-start = (bf16[128,1280]{1,0:T(8,128)(2,1)S(1)}, bf16[128,1280]{1,0:T(8,128)(2,1)}, u32[]{:S(2)}) copy-start(bf16[128,1280]{1,0:T(8,128)(2,1)} %patches_ref.1) | copy-start | bytes 983044
  97.9 12.9 %copy-start.1 = (bf16[128,1280]{1,0:T(8,128)(2,1)S(1)}, bf16[128,1280]{1,0:T(8,128)(2,1)}, u32[]{:S(2)}) copy-start(bf16[128,1280]{1,0:T(8,128)(2,1)} %teacher_ref.1) | copy-start | bytes 983044
  97.9 12.9 %copy-start.2 = (s32[128,1]{0,1:T(1,128)S(1)}, s32[128,1]{0,1:T(1,128)}, u32[]{:S(2)}) copy-start(s32[128,1]{0,1:T(1,128)} %param.11) | copy-start | bytes 1540
  97.9 12.9 %copy-start.3 = (bf16[128]{0:T(256)(128)(2,1)S(1)}, bf16[128]{0:T(256)(128)(2,1)}, u32[]{:S(2)}) copy-start(bf16[128]{0:T(256)(128)(2,1)} %param.12) | copy-start | bytes 772
  97.9 11.9 %collective-permute-start.6 = (bf16[10,128,128]{2,1,0:T(8,128)(2,1)S(1)}, bf16[10,128,128]{2,1,0:T(8,128)(2,1)S(1)}, u32[]{:S(2)}, u32[]{:S(2)}) collective-permute-start(bf16[10,128,128]{2,1,0:T(8,128)(2,1)S(1)} %pad_maximum_fusion), channel_id=1, source_target_pairs={{0,32},{32,0},{64,96},{96,64},{128,160},{160,128},{192,224},{224,1... | collective-permute-start | bytes 983048 | tf_op jit(solution)/shard_map/ppermute | solution.py:278

commit v3 on v2

--- a/solution.py
+++ b/solution.py
@@ -11,6 +11,7 @@
 FB = 40
 D = DB * BLK
 SLOT = 8
+UNROLL = 20
 EPS = 1e-06
 GELU_K = 0.7978845608028654
 GELU_C = 0.044715
@@ -55,6 +56,11 @@
     ]
     for load in loads:
         load.start()
+
+    def store(second):
+        lanes = pl.ds(second * D, D + second * BLK)
+        return pltpu.make_async_copy(out.at[:, lanes], out_hbm.at[:, lanes], sems.at[2 + second])
+
     owners = out.shape[0] // SLOT
     place = slot_matrix(route_ref[...], owners)
     one_hot = place.astype(BF16)
@@ -65,12 +71,15 @@
     feats = patches[...].astype(F32)
     normed, _ = layer_norm(feats)
     out[:, :D] = dot(one_hot, normed.astype(BF16)).astype(BF16)
+    early = store(0)
+    early.start()
     loads[1].wait()
     differ = (feats - teacher[...].astype(F32)).astype(BF16)
     out[:, D : 2 * D] = (gate * dot(one_hot, differ)).astype(BF16)
-    store = pltpu.make_async_copy(out, out_hbm, sems.at[2])
-    store.start()
-    store.wait()
+    late = store(1)
+    late.start()
+    early.wait()
+    late.wait()
 
 
 def expert_kernel(
@@ -78,20 +87,26 @@
     in_cols,
     out_rows,
     where_ref,
-    pay_ref,
+    pay_hbm,
     w_in_ref,
     w_out_hbm,
     ret_hbm,
     *rest,
 ):
-    n_x = len(rest) // 2 - 6
+    n_x = (len(rest) - 15) // 2
     parts = (rest[:n_x], rest[n_x : 2 * n_x])
-    w_out_ref, ret, xnt, hid, slope, gh, gn, grads, gate, load_sem, ret_sems, sems = rest[2 * n_x :]
+    pay_ref, w_out_ref, ret, xnt, hid, slope, gh, gn, grads, gate, ge, get, load_sem, ret_sems, sems = rest[2 * n_x :]
     share = FB // n_x
     half = share // 2
     my_x, my_y = where_ref[0], where_ref[1]
-    load = pltpu.make_async_copy(w_out_hbm, w_out_ref, load_sem.at[0])
-    load.start()
+    first, rest_of = pl.ds(0, D), pl.ds(D, D + BLK)
+    loads = [
+        pltpu.make_async_copy(pay_hbm.at[:, first], pay_ref.at[:, first], load_sem.at[0]),
+        pltpu.make_async_copy(pay_hbm.at[:, rest_of], pay_ref.at[:, rest_of], load_sem.at[1]),
+        pltpu.make_async_copy(w_out_hbm, w_out_ref, load_sem.at[2]),
+    ]
+    for load in loads:
+        load.start()
 
     def place(block):
         x = block // share
@@ -114,14 +129,14 @@
             copy.start()
         return copies
 
+    gn[...] = jnp.zeros_like(gn)
+    loads[0].wait()
     for i in range(DB):
         xnt[i] = pay_ref[:, i * BLK : (i + 1) * BLK].T
-    gn[...] = jnp.zeros_like(gn)
-    gate[...] = jnp.square(pay_ref[:, 2 * D :].astype(F32))
 
     def forward(step, carry):
-        for q in range(4):
-            b = step * 4 + q
+        for q in range(UNROLL):
+            b = step * UNROLL + q
             c = in_cols[b]
             lanes = pl.ds(pl.multiple_of(in_rows[b] * BLK, BLK), BLK)
             v = dot(pay_ref[:, lanes], w_in_ref[b])
@@ -135,32 +150,40 @@
             gh[c] = jnp.zeros_like(v)
         return carry
 
-    lax.fori_loop(0, FB // 4, forward, 0)
-    load.wait()
+    lax.fori_loop(0, FB // UNROLL, forward, 0)
+    loads[1].wait()
+    loads[2].wait()
+    gate[...] = jnp.square(pay_ref[:, 2 * D :].astype(F32))
+
+    def read(j):
+        return [out_rows[K2 * j + k] for k in range(K2)]
+
+    def spread(j):
+        return jnp.concatenate([hid[r] for r in read(j)], axis=1)
+
+    def weight(j):
+        return w_out_ref[K2 * j : K2 * (j + 1)].reshape(K2 * BLK, BLK)
 
     for j in range(DB):
-        lanes = slice(j * BLK, (j + 1) * BLK)
-        reads = [out_rows[K2 * j + k] for k in range(K2)]
-        spread = jnp.concatenate([hid[r] for r in reads], axis=1)
-        weight = w_out_ref[K2 * j : K2 * (j + 1)].reshape(K2 * BLK, BLK)
-        produced = dot(spread, weight).astype(BF16)
-        ret[:, lanes] = produced
-        grad = pay_ref[:, D + j * BLK : D + (j + 1) * BLK].astype(F32) + gate[
-            ...
-        ] * produced.astype(F32)
-        grad_b = grad.astype(BF16)
-        outer = dot(grad_b.T, spread)
-        back = dot_nt(grad_b, weight)
-        for k in range(K2):
+        produced = dot(spread(j), weight(j)).astype(BF16)
+        ret[:, j * BLK : (j + 1) * BLK] = produced
+        given = pay_ref[:, D + j * BLK : D + (j + 1) * BLK].astype(F32)
+        grad = (given + gate[...] * produced.astype(F32)).astype(BF16)
+        ge[j] = grad
+        get[j] = grad.T
+    for j in range(DB):
+        outer = dot(get[j], spread(j))
+        back = dot_nt(ge[j], weight(j))
+        for k, r in enumerate(read(j)):
             rel_x, pos = place(K2 * j + k)
             grads[1, rel_x, pos] = outer[:, k * BLK : (k + 1) * BLK].astype(BF16)
-            gh[reads[k]] += back[:, k * BLK : (k + 1) * BLK]
+            gh[r] += back[:, k * BLK : (k + 1) * BLK]
 
     copies = send(1)
 
     def backward(step, carry):
-        for q in range(4):
-            b = step * 4 + q
+        for q in range(UNROLL):
+            b = step * UNROLL + q
             c = in_cols[b]
             i = in_rows[b]
             grad_pre = (gh[c] * slope[c]).astype(BF16)
@@ -169,7 +192,7 @@
             gn[i] += dot_nt(grad_pre, w_in_ref[b])
         return carry
 
-    lax.fori_loop(0, FB // 4, backward, 0)
+    lax.fori_loop(0, FB // UNROLL, backward, 0)
     for i in range(DB):
         ret[:, D + i * BLK : D + (i + 1) * BLK] = gn[i].astype(BF16)
     copies += send(0)
@@ -177,7 +200,7 @@
         copy.wait()
 
 
-def finish_kernel(route_ref, gates_ref, patches_ref, teacher_ref, ret_ref, student_ref, grad_ref):
+def finish_kernel(route_ref, gates_ref, patches_ref, teacher_ref, ret_ref, student_ref, grad_ref, corner_ref):
     owners = ret_ref.shape[0] // SLOT
     place = slot_matrix(route_ref[...], owners).astype(F32)
     pick = place.T
@@ -188,6 +211,7 @@
     feats = patches_ref[...].astype(F32)
     summed = feats + gate * dot(pick, ret_ref[:, :D])
     student_ref[...] = summed.astype(BF16)
+    corner_ref[...] = summed[:8, :BLK]
     mismatch = summed - teacher_ref[...].astype(F32)
     grad = dot(pick, ret_ref[:, D:])
     normed, scale = layer_norm(feats)
@@ -196,11 +220,10 @@
     grad_ref[...] = mismatch + scale * (grad - mean_grad - normed * mean_both)
 
 
-def total_kernel(mine_in_ref, mine_out_ref, other_ref, in_ref, out_ref):
-    half = in_ref.shape[0]
-    for q in range(half):
-        in_ref[q] = mine_in_ref[q] + other_ref[q].astype(F32)
-        out_ref[q] = (mine_out_ref[q] + other_ref[half + q].astype(F32)).T
+def total_kernel(mine_in_ref, mine_out_ref, other_in_ref, other_out_ref, after_ref, in_ref, out_ref):
+    for q in range(in_ref.shape[0]):
+        in_ref[q] = mine_in_ref[q] + other_in_ref[q].astype(F32)
+        out_ref[q] = (mine_out_ref[q] + other_out_ref[q].astype(F32)).T
 
 
 def shift(n_x, dx, dy):
@@ -231,7 +254,7 @@
             pltpu.VMEM((rows, D), BF16),
             pltpu.VMEM((rows, D), BF16),
             pltpu.VMEM((slots, 2 * D + BLK), BF16),
-            pltpu.SemaphoreType.DMA((3,)),
+            pltpu.SemaphoreType.DMA((4,)),
         ],
         compiler_params=pltpu.CompilerParams(vmem_limit_bytes=60 << 20),
         name="pack",
@@ -246,13 +269,14 @@
     arrived = exchange(payload)
     me = lax.axis_index("dp")
     where = jnp.stack([me // 2, me % 2]).astype(jnp.int32)
-    part = jax.ShapeDtypeStruct((share, BLK, BLK), BF16)
+    part = pltpu.HBM((share, BLK, BLK), BF16)
     returned, *parts = pl.pallas_call(
         expert_kernel,
-        out_shape=(jax.ShapeDtypeStruct((slots, 2 * D), BF16),) + (part,) * (2 * n_x),
-        in_specs=[SMEM_SPEC] * 4 + [VMEM_SPEC] * 2 + [HBM_SPEC],
+        out_shape=(pltpu.HBM((slots, 2 * D), BF16),) + (part,) * (2 * n_x),
+        in_specs=[SMEM_SPEC] * 4 + [HBM_SPEC, VMEM_SPEC, HBM_SPEC],
         out_specs=(HBM_SPEC,) * (1 + 2 * n_x),
         scratch_shapes=[
+            pltpu.VMEM((slots, 2 * D + BLK), BF16),
             pltpu.VMEM((FB, BLK, BLK), BF16),
             pltpu.VMEM((slots, 2 * D), BF16),
             pltpu.VMEM((DB, BLK, slots), BF16),
@@ -262,11 +286,13 @@
             pltpu.VMEM((DB, slots, BLK), F32),
             pltpu.VMEM((2, n_x, share, BLK, BLK), BF16),
             pltpu.VMEM((slots, BLK), F32),
-            pltpu.SemaphoreType.DMA((1,)),
+            pltpu.VMEM((DB, slots, BLK), BF16),
+            pltpu.VMEM((DB, BLK, slots), BF16),
+            pltpu.SemaphoreType.DMA((3,)),
             pltpu.SemaphoreType.DMA((2,)),
             pltpu.SemaphoreType.DMA((2, n_x)),
         ],
-        compiler_params=pltpu.CompilerParams(vmem_limit_bytes=60 << 20),
+        compiler_params=pltpu.CompilerParams(vmem_limit_bytes=51 << 20),
         name="expert",
     )(in_rows[0], in_cols[0], out_rows[0], where, arrived, w_in[0], w_out[0])
     part_in, part_out = parts[:n_x], parts[n_x:]
@@ -288,28 +314,29 @@
     pair_out = pass_on(add(part_out[3], far_out).astype(BF16), 3)
     total_in = add(part_in[0], near_in, pair_in)
     total_out = add(part_out[0], near_out, pair_out)
-    other = pass_on(jnp.concatenate([total_in[half:], total_out[half:]]).astype(BF16), 0, 1)
+    other_in = pass_on(total_in[half:].astype(BF16), 0, 1)
+    other_out = pass_on(total_out[half:].astype(BF16), 0, 1)
+    student, grad_patches, corner = pl.pallas_call(
+        finish_kernel,
+        out_shape=(
+            jax.ShapeDtypeStruct((rows, D), BF16),
+            jax.ShapeDtypeStruct((rows, D), F32),
+            jax.ShapeDtypeStruct((8, BLK), F32),
+        ),
+        in_specs=[VMEM_SPEC] * 5,
+        out_specs=(VMEM_SPEC,) * 3,
+        compiler_params=pltpu.CompilerParams(vmem_limit_bytes=16 << 20),
+        name="finish",
+    )(route_row, gates_row, patches, teacher, back)
     block = jax.ShapeDtypeStruct((half, BLK, BLK), F32)
     grad_in, grad_out = pl.pallas_call(
         total_kernel,
         out_shape=(block, block),
-        in_specs=[VMEM_SPEC] * 3,
+        in_specs=[VMEM_SPEC] * 5,
         out_specs=(VMEM_SPEC, VMEM_SPEC),
         compiler_params=pltpu.CompilerParams(vmem_limit_bytes=16 << 20),
         name="total",
-    )(total_in[:half], total_out[:half], other)
-
-    student, grad_patches = pl.pallas_call(
-        finish_kernel,
-        out_shape=(
-            jax.ShapeDtypeStruct((rows, D), BF16),
-            jax.ShapeDtypeStruct((rows, D), F32),
-        ),
-        in_specs=[VMEM_SPEC] * 5,
-        out_specs=(VMEM_SPEC, VMEM_SPEC),
-        compiler_params=pltpu.CompilerParams(vmem_limit_bytes=16 << 20),
-        name="finish",
-    )(route_row, gates_row, patches, teacher, back)
+    )(total_in[:half], total_out[:half], other_in, other_out, corner)
     return (student, grad_patches, grad_in[None], grad_out[None])
 
 

time: 113 us -> 103 us (0.912)
  waiting for transfers between devices: 62.3 us -> 54.9 us
  Pallas kernels: 20.8 us -> 16.9 us
  starting transfers between devices: 26.3 us -> 29.3 us
    ppermute x7 -> x8, waiting for transfers between devices: 28.8 us -> 18.2 us  [pass_on(): return lax.ppermute(values, 'dp', shift(n_x, dx, dy))]
    pallas_call x1, Pallas kernels: 14.4 us -> 10.7 us  [local(): pl.pallas_call(expert_kernel, out_shape=(pltpu.HBM((slots, 2 * D), BF16),...]
    all_to_all x2, waiting for transfers between devices: 33.6 us -> 36.6 us  [exchange(): lax.all_to_all(blocks, 'expert', split_axis=0, concat_axis=0, tiled=True)]
    ppermute x7 -> x8, starting transfers between devices: 9.65 us -> 12.5 us  [pass_on(): return lax.ppermute(values, 'dp', shift(n_x, dx, dy))]
  transfers between devices with their start and end apart: 9 -> 10, of which waited for: 6 -> 7; matrix products, arithmetic and copies ran while one was open for 1% -> 1% of each run, Pallas kernels for 1% -> 2%
where the time goes in v3:
time: 103 us
  waiting for transfers between devices  54.9 us (53%)
  starting transfers between devices  29.3 us (28%)
  Pallas kernels  16.9 us (16%)
    all_to_all x2, waiting for transfers between devices, exchange(): lax.all_to_all(blocks, 'expert', split_axis=0, concat_axis=0, tiled=True)  36.6 us
    ppermute x8, waiting for transfers between devices, pass_on(): return lax.ppermute(values, 'dp', shift(n_x, dx, dy))  18.2 us
    all_to_all x2, starting transfers between devices, exchange(): lax.all_to_all(blocks, 'expert', split_axis=0, concat_axis=0, tiled=True)  16.8 us
    ppermute x8, starting transfers between devices, pass_on(): return lax.ppermute(values, 'dp', shift(n_x, dx, dy))  12.5 us
    pallas_call x1, Pallas kernels, local(): pl.pallas_call(expert_kernel, out_shape=(pltpu.HBM((slots, 2 * D), BF16),...  10.7 us
    pallas_call x1, Pallas kernels, local(): pl.pallas_call(pack_kernel, out_shape=jax.ShapeDtypeStruct((slots, 2 * D...  3.5 us
  transfers between devices with their start and end apart: 10, of which 7 were waited for; matrix products, arithmetic and copies ran while one was open for 1% of the time, Pallas kernels for 2%

profile of v3, /device:TPU:1, one launch (start us, length us, event | category | flops | bytes accessed | tf_op | source)
XLA Modules:
  0.0 102.7 jit_solution(18381296456252225961)
XLA Ops:
  0.6 3.5 %pack.1 = bf16[256,2688]{1,0:T(8,128)(2,1)} custom-call(s32[1,128]{1,0:T(1,128)} %bitcast.18, bf16[1,128]{1,0:T(2,128)(2,1)} %bitcast.20, bf16[128,1280]{1,0:T(8,128)(2,1)} %patches_ref.1, bf16[128,1280]{1,0:T(8,128)(2,1)} %teacher_ref.1), custom_call_target="tpu_custom_call" | custom-call | tf_op jit(solution)/shard_map/pack/pallas_call | solution.py:248
  4.1 0.0 copy-start
  4.2 0.0 copy-start.1
  4.2 0.0 copy-start.6
  4.2 0.0 copy-start.7
  4.2 0.0 copy-start.8
  4.2 11.3 %all-to-all-start = ((bf16[32,8,2688]{2,1,0:T(8,128)(2,1)}), bf16[32,8,2688]{2,1,0:T(8,128)(2,1)}, u32[]{:S(2)}, u32[]{:S(2)}) async-start(bf16[32,8,2688]{2,1,0:T(8,128)(2,1)} %bitcast.25), calls=%async_computation | async-start | bytes 2752512 | tf_op jit(solution)/shard_map/all_to_all | solution.py:266
  15.6 0.1 pad_add_fusion.where_ref
  15.6 34.1 %all-to-all-done = bf16[32,8,2688]{2,1,0:T(8,128)(2,1)} async-done(((bf16[32,8,2688]{2,1,0:T(8,128)(2,1)}), bf16[32,8,2688]{2,1,0:T(8,128)(2,1)}, u32[]{:S(2)}, u32[]{:S(2)}) %all-to-all-start) | async-done | bytes 1376288 | tf_op jit(solution)/shard_map/all_to_all | solution.py:266
  49.7 0.0 copy-done
  49.7 0.0 copy-done.1
  49.7 0.0 copy-done.6
  49.7 0.0 copy-done.7
  49.7 0.0 copy-done.8
  49.7 10.7 %expert.1 = (bf16[256,2560]{1,0:T(8,128)(2,1)}, bf16[10,128,128]{2,1,0:T(8,128)(2,1)}, bf16[10,128,128]{2,1,0:T(8,128)(2,1)}, bf16[10,128,128]{2,1,0:T(8,128)(2,...) custom-call(s32[40]{0:T(128)S(1)} %bitcast.22, ...), custom_call_target="tpu_custom_call" | custom-call | tf_op jit(solution)/shard_map/expert/pallas_call | solution.py:273
  60.5 0.0 copy-start.12
  60.5 5.5 %all-to-all-start.1 = ((bf16[32,8,2560]{2,1,0:T(8,128)(2,1)}), bf16[32,8,2560]{2,1,0:T(8,128)(2,1)S(1)}, u32[]{:S(2)}, u32[]{:S(2)}) async-start(bf16[32,8,2560]{2,1,0:T(8,128)(2,1)} %bitcast.26), calls=%async_computation.1 | async-start | bytes 2621440 | tf_op jit(solution)/shard_map/all_to_all | solution.py:266
  66.0 0.0 copy-start.10
  66.0 1.3 %collective-permute-start.1 = (bf16[10,128,128]{2,1,0:T(8,128)(2,1)}, bf16[10,128,128]{2,1,0:T(8,128)(2,1)S(1)}, u32[]{:S(2)}, u32[]{:S(2)}) collective-permute-start(bf16[10,128,128]{2,1,0:T(8,128)(2,1)} %get-tuple-element.24), channel_id=1, source_target_pairs={{0,64},{32,96},{64,128},{96,160},{128,192},{160,224},{192,0},{224,... | collective-permute-start | bytes 983048 | tf_op jit(solution)/shard_map/ppermute | solution.py:304
  67.3 1.5 %collective-permute-start.4 = (bf16[10,128,128]{2,1,0:T(8,128)(2,1)S(1)}, bf16[10,128,128]{2,1,0:T(8,128)(2,1)S(1)}, u32[]{:S(2)}, u32[]{:S(2)}) collective-permute-start(bf16[10,128,128]{2,1,0:T(8,128)(2,1)S(1)} %copy-done.14), channel_id=1, source_target_pairs={{0,192},{32,224},{64,0},{96,32},{128,64},{160,96},{192,128},{224,1... | collective-permute-start | bytes 983048 | tf_op jit(solution)/shard_map/ppermute | solution.py:304
  68.8 1.3 %collective-permute-start = (bf16[10,128,128]{2,1,0:T(8,128)(2,1)}, bf16[10,128,128]{2,1,0:T(8,128)(2,1)S(1)}, u32[]{:S(2)}, u32[]{:S(2)}) collective-permute-start(bf16[10,128,128]{2,1,0:T(8,128)(2,1)} %get-tuple-element.22), channel_id=1, source_target_pairs={{0,192},{32,224},{64,0},{96,32},{128,64},{160,96},{192,128},{224,1... | collective-permute-start | bytes 983048 | tf_op jit(solution)/shard_map/ppermute | solution.py:304
  70.1 6.5 %collective-permute-done.1 = bf16[10,128,128]{2,1,0:T(8,128)(2,1)S(1)} collective-permute-done((bf16[10,128,128]{2,1,0:T(8,128)(2,1)}, bf16[10,128,128]{2,1,0:T(8,128)(2,1)S(1)}, u32[]{:S(2)}, u32[]{:S(2)}) %collective-permute-start.1) | collective-permute-done | bytes 327712 | tf_op jit(solution)/shard_map/ppermute | solution.py:304
  76.6 0.1 add_convert_fusion.1
  76.7 0.1 collective-permute-start.2
  76.8 1.2 %collective-permute-start.3 = (bf16[10,128,128]{2,1,0:T(8,128)(2,1)S(1)}, bf16[10,128,128]{2,1,0:T(8,128)(2,1)S(1)}, u32[]{:S(2)}, u32[]{:S(2)}) collective-permute-start(bf16[10,128,128]{2,1,0:T(8,128)(2,1)S(1)} %copy-done.13), channel_id=1, source_target_pairs={{0,64},{32,96},{64,128},{96,160},{128,192},{160,224},{192,0},{224,... | collective-permute-start | bytes 983048 | tf_op jit(solution)/shard_map/ppermute | solution.py:304
  78.0 0.0 collective-permute-done.4
  78.0 0.0 copy-done.11
  78.0 0.1 add_convert_fusion
  78.1 1.8 %collective-permute-start.5 = (bf16[10,128,128]{2,1,0:T(8,128)(2,1)S(1)}, bf16[10,128,128]{2,1,0:T(8,128)(2,1)S(1)}, u32[]{:S(2)}, u32[]{:S(2)}) collective-permute-start(bf16[10,128,128]{2,1,0:T(8,128)(2,1)S(1)} %add_convert_fusion), channel_id=1, source_target_pairs={{0,192},{32,224},{64,0},{96,32},{128,64},{160,96},{192,128},{224,1... | collective-permute-start | bytes 983048 | tf_op jit(solution)/shard_map/ppermute | solution.py:304
  79.9 3.2 %collective-permute-done = bf16[10,128,128]{2,1,0:T(8,128)(2,1)S(1)} collective-permute-done((bf16[10,128,128]{2,1,0:T(8,128)(2,1)}, bf16[10,128,128]{2,1,0:T(8,128)(2,1)S(1)}, u32[]{:S(2)}, u32[]{:S(2)}) %collective-permute-start) | collective-permute-done | bytes 327712 | tf_op jit(solution)/shard_map/ppermute | solution.py:304
  83.1 3.0 %collective-permute-done.2 = bf16[10,128,128]{2,1,0:T(8,128)(2,1)S(1)} collective-permute-done((bf16[10,128,128]{2,1,0:T(8,128)(2,1)S(1)}, bf16[10,128,128]{2,1,0:T(8,128)(2,1)S(1)}, u32[]{:S(2)}, u32[]{:S(2)}) %collective-permute-start.2) | collective-permute-done | bytes 327712 | tf_op jit(solution)/shard_map/ppermute | solution.py:304
  86.2 0.1 convert_add_fusion.1
  86.3 2.7 %collective-permute-start.6 = (bf16[5,128,128]{2,1,0:T(8,128)(2,1)S(1)}, bf16[5,128,128]{2,1,0:T(8,128)(2,1)S(1)}, u32[]{:S(2)}, u32[]{:S(2)}) collective-permute-start(bf16[5,128,128]{2,1,0:T(8,128)(2,1)S(1)} %slice.25), channel_id=1, source_target_pairs={{0,32},{32,0},{64,96},{96,64},{128,160},{160,128},{192,224},{224,1... | collective-permute-start | bytes 491528 | tf_op jit(solution)/shard_map/ppermute | solution.py:304
  89.0 4.2 %collective-permute-done.3 = bf16[10,128,128]{2,1,0:T(8,128)(2,1)S(1)} collective-permute-done((bf16[10,128,128]{2,1,0:T(8,128)(2,1)S(1)}, bf16[10,128,128]{2,1,0:T(8,128)(2,1)S(1)}, u32[]{:S(2)}, u32[]{:S(2)}) %collective-permute-start.3) | collective-permute-done | bytes 327712 | tf_op jit(solution)/shard_map/ppermute | solution.py:304
  93.2 0.0 collective-permute-done.5
  93.2 0.0 copy-done.9
  93.2 0.0 copy-start.3
  93.2 0.0 copy-start.4
  93.2 0.0 copy-start.5
  93.2 0.1 convert_add_fusion
  93.4 2.7 %collective-permute-start.7 = (bf16[5,128,128]{2,1,0:T(8,128)(2,1)S(1)}, bf16[5,128,128]{2,1,0:T(8,128)(2,1)S(1)}, u32[]{:S(2)}, u32[]{:S(2)}) collective-permute-start(bf16[5,128,128]{2,1,0:T(8,128)(2,1)S(1)} %slice.24), channel_id=1, source_target_pairs={{0,32},{32,0},{64,96},{96,64},{128,160},{160,128},{192,224},{224,1... | collective-permute-start | bytes 491528 | tf_op jit(solution)/shard_map/ppermute | solution.py:304
  96.1 2.5 %all-to-all-done.1 = bf16[32,8,2560]{2,1,0:T(8,128)(2,1)S(1)} async-done(((bf16[32,8,2560]{2,1,0:T(8,128)(2,1)}), bf16[32,8,2560]{2,1,0:T(8,128)(2,1)S(1)}, u32[]{:S(2)}, u32[]{:S(2)}) %all-to-all-start.1) | async-done | bytes 1310752 | tf_op jit(solution)/shard_map/all_to_all | solution.py:266
  98.7 0.0 copy-done.4
  98.7 0.0 copy-done.5
  98.7 1.7 %finish.1 = (bf16[128,1280]{1,0:T(8,128)(2,1)}, f32[128,1280]{1,0:T(8,128)}, f32[8,128]{1,0:T(8,128)S(1)}) custom-call(s32[1,128]{1,0:T(1,128)S(1)} %bitcast.19, bf16[1,128]{1,0:T(2,128)(2,1)S(1)} %bitcast.21, bf16[128,1280]{1,0:T(8,128)(2,1)S(1)} %copy-done.2, bf16[128,1280]{1,0:T(8,128)(2,1)S(1)} %copy-done.3, bf16[256,2560]{1,0:T(8,128)(2,1)S(1)} %bitcast.15), custom_call_target="tpu_custom_call" | custom-call | tf_op jit(solution)/shard_map/finish/pallas_call | solution.py:319
  100.4 0.0 collective-permute-done.6.other_in_ref
  100.4 1.3 %collective-permute-done.7.other_out_ref = bf16[5,128,128]{2,1,0:T(8,128)(2,1)S(1)} collective-permute-done((bf16[5,128,128]{2,1,0:T(8,128)(2,1)S(1)}, bf16[5,128,128]{2,1,0:T(8,128)(2,1)S(1)}, u32[]{:S(2)}, u32[]{:S(2)}) %collective-permute-start.7) | collective-permute-done | bytes 163872 | tf_op jit(solution)/shard_map/ppermute | solution.py:304
  101.7 1.0 total.1
  (15 shorter events, 0.1 us)
Async XLA Ops:
  4.1 45.6 %copy-start = (bf16[1,40,128,128]{3,2,1,0:T(8,128)(2,1)S(1)}, bf16[1,40,128,128]{3,2,1,0:T(8,128)(2,1)}, u32[]{:S(2)}) copy-start(bf16[1,40,128,128]{3,2,1,0:T(8,128)(2,1)} %param.13) | copy-start | bytes 3932164
  4.2 45.6 %copy-start.1 = (bf16[1,40,128,128]{3,2,1,0:T(8,128)(2,1)S(1)}, bf16[1,40,128,128]{3,2,1,0:T(8,128)(2,1)}, u32[]{:S(2)}) copy-start(bf16[1,40,128,128]{3,2,1,0:T(8,128)(2,1)} %param.16) | copy-start | bytes 3932164
  4.2 45.6 %copy-start.6 = (s32[1,40]{1,0:T(1,128)S(1)}, s32[1,40]{1,0:T(1,128)}, u32[]{:S(2)}) copy-start(s32[1,40]{1,0:T(1,128)} %param.14) | copy-start | bytes 484
  4.2 45.6 %copy-start.7 = (s32[1,40]{1,0:T(1,128)S(1)}, s32[1,40]{1,0:T(1,128)}, u32[]{:S(2)}) copy-start(s32[1,40]{1,0:T(1,128)} %param.15) | copy-start | bytes 484
  4.2 45.6 %copy-start.8 = (s32[1,40]{1,0:T(1,128)S(1)}, s32[1,40]{1,0:T(1,128)}, u32[]{:S(2)}) copy-start(s32[1,40]{1,0:T(1,128)} %param.17) | copy-start | bytes 484
  4.2 45.5 %all-to-all-start = ((bf16[32,8,2688]{2,1,0:T(8,128)(2,1)}), bf16[32,8,2688]{2,1,0:T(8,128)(2,1)}, u32[]{:S(2)}, u32[]{:S(2)}) async-start(bf16[32,8,2688]{2,1,0:T(8,128)(2,1)} %bitcast.25), calls=%async_computation | async-start | bytes 2752512 | tf_op jit(solution)/shard_map/all_to_all | solution.py:266
  60.5 6.8 %copy-start.14 = (bf16[10,128,128]{2,1,0:T(8,128)(2,1)S(1)}, bf16[10,128,128]{2,1,0:T(8,128)(2,1)}, u32[]{:S(2)}) copy-start(bf16[10,128,128]{2,1,0:T(8,128)(2,1)} %get-tuple-element.28) | copy-start | bytes 983044
  60.5 16.1 %copy-start.12 = (bf16[10,128,128]{2,1,0:T(8,128)(2,1)S(1)}, bf16[10,128,128]{2,1,0:T(8,128)(2,1)}, u32[]{:S(2)}) copy-start(bf16[10,128,128]{2,1,0:T(8,128)(2,1)} %get-tuple-element.23) | copy-start | bytes 983044
  60.5 16.3 %copy-start.13 = (bf16[10,128,128]{2,1,0:T(8,128)(2,1)S(1)}, bf16[10,128,128]{2,1,0:T(8,128)(2,1)}, u32[]{:S(2)}) copy-start(bf16[10,128,128]{2,1,0:T(8,128)(2,1)} %get-tuple-element.26) | copy-start | bytes 983044
  60.5 17.5 %copy-start.11 = (bf16[10,128,128]{2,1,0:T(8,128)(2,1)S(1)}, bf16[10,128,128]{2,1,0:T(8,128)(2,1)}, u32[]{:S(2)}) copy-start(bf16[10,128,128]{2,1,0:T(8,128)(2,1)} %get-tuple-element.27) | copy-start | bytes 983044
  60.5 38.1 %all-to-all-start.1 = ((bf16[32,8,2560]{2,1,0:T(8,128)(2,1)}), bf16[32,8,2560]{2,1,0:T(8,128)(2,1)S(1)}, u32[]{:S(2)}, u32[]{:S(2)}) async-start(bf16[32,8,2560]{2,1,0:T(8,128)(2,1)} %bitcast.26), calls=%async_computation.1 | async-start | bytes 2621440 | tf_op jit(solution)/shard_map/all_to_all | solution.py:266
  66.0 20.1 %copy-start.10 = (bf16[10,128,128]{2,1,0:T(8,128)(2,1)S(1)}, bf16[10,128,128]{2,1,0:T(8,128)(2,1)}, u32[]{:S(2)}) copy-start(bf16[10,128,128]{2,1,0:T(8,128)(2,1)} %get-tuple-element.21) | copy-start | bytes 983044
  66.0 10.6 %collective-permute-start.1 = (bf16[10,128,128]{2,1,0:T(8,128)(2,1)}, bf16[10,128,128]{2,1,0:T(8,128)(2,1)S(1)}, u32[]{:S(2)}, u32[]{:S(2)}) collective-permute-start(bf16[10,128,128]{2,1,0:T(8,128)(2,1)} %get-tuple-element.24), channel_id=1, source_target_pairs={{0,64},{32,96},{64,128},{96,160},{128,192},{160,224},{192,0},{224,... | collective-permute-start | bytes 983048 | tf_op jit(solution)/shard_map/ppermute | solution.py:304
  67.3 10.7 %collective-permute-start.4 = (bf16[10,128,128]{2,1,0:T(8,128)(2,1)S(1)}, bf16[10,128,128]{2,1,0:T(8,128)(2,1)S(1)}, u32[]{:S(2)}, u32[]{:S(2)}) collective-permute-start(bf16[10,128,128]{2,1,0:T(8,128)(2,1)S(1)} %copy-done.14), channel_id=1, source_target_pairs={{0,192},{32,224},{64,0},{96,32},{128,64},{160,96},{192,128},{224,1... | collective-permute-start | bytes 983048 | tf_op jit(solution)/shard_map/ppermute | solution.py:304
  68.8 14.3 %collective-permute-start = (bf16[10,128,128]{2,1,0:T(8,128)(2,1)}, bf16[10,128,128]{2,1,0:T(8,128)(2,1)S(1)}, u32[]{:S(2)}, u32[]{:S(2)}) collective-permute-start(bf16[10,128,128]{2,1,0:T(8,128)(2,1)} %get-tuple-element.22), channel_id=1, source_target_pairs={{0,192},{32,224},{64,0},{96,32},{128,64},{160,96},{192,128},{224,1... | collective-permute-start | bytes 983048 | tf_op jit(solution)/shard_map/ppermute | solution.py:304
  76.7 9.4 %collective-permute-start.2 = (bf16[10,128,128]{2,1,0:T(8,128)(2,1)S(1)}, bf16[10,128,128]{2,1,0:T(8,128)(2,1)S(1)}, u32[]{:S(2)}, u32[]{:S(2)}) collective-permute-start(bf16[10,128,128]{2,1,0:T(8,128)(2,1)S(1)} %add_convert_fusion.1), channel_id=1, source_target_pairs={{0,64},{32,96},{64,128},{96,160},{128,192},{160,224},{192,0},{224,... | collective-permute-start | bytes 983048 | tf_op jit(solution)/shard_map/ppermute | solution.py:304
  76.8 16.4 %collective-permute-start.3 = (bf16[10,128,128]{2,1,0:T(8,128)(2,1)S(1)}, bf16[10,128,128]{2,1,0:T(8,128)(2,1)S(1)}, u32[]{:S(2)}, u32[]{:S(2)}) collective-permute-start(bf16[10,128,128]{2,1,0:T(8,128)(2,1)S(1)} %copy-done.13), channel_id=1, source_target_pairs={{0,64},{32,96},{64,128},{96,160},{128,192},{160,224},{192,0},{224,... | collective-permute-start | bytes 983048 | tf_op jit(solution)/shard_map/ppermute | solution.py:304
  78.0 15.2 %copy-start.9 = (bf16[10,128,128]{2,1,0:T(8,128)(2,1)S(1)}, bf16[10,128,128]{2,1,0:T(8,128)(2,1)}, u32[]{:S(2)}) copy-start(bf16[10,128,128]{2,1,0:T(8,128)(2,1)} %get-tuple-element.25) | copy-start | bytes 983044
  78.1 15.1 %collective-permute-start.5 = (bf16[10,128,128]{2,1,0:T(8,128)(2,1)S(1)}, bf16[10,128,128]{2,1,0:T(8,128)(2,1)S(1)}, u32[]{:S(2)}, u32[]{:S(2)}) collective-permute-start(bf16[10,128,128]{2,1,0:T(8,128)(2,1)S(1)} %add_convert_fusion), channel_id=1, source_target_pairs={{0,192},{32,224},{64,0},{96,32},{128,64},{160,96},{192,128},{224,1... | collective-permute-start | bytes 983048 | tf_op jit(solution)/shard_map/ppermute | solution.py:304
  86.3 14.1 %collective-permute-start.6 = (bf16[5,128,128]{2,1,0:T(8,128)(2,1)S(1)}, bf16[5,128,128]{2,1,0:T(8,128)(2,1)S(1)}, u32[]{:S(2)}, u32[]{:S(2)}) collective-permute-start(bf16[5,128,128]{2,1,0:T(8,128)(2,1)S(1)} %slice.25), channel_id=1, source_target_pairs={{0,32},{32,0},{64,96},{96,64},{128,160},{160,128},{192,224},{224,1... | collective-permute-start | bytes 491528 | tf_op jit(solution)/shard_map/ppermute | solution.py:304
  93.2 5.5 %copy-start.2 = (bf16[128,1280]{1,0:T(8,128)(2,1)S(1)}, bf16[128,1280]{1,0:T(8,128)(2,1)}, u32[]{:S(2)}) copy-start(bf16[128,1280]{1,0:T(8,128)(2,1)} %patches_ref.1) | copy-start | bytes 983044
  93.2 5.5 %copy-start.3 = (bf16[128,1280]{1,0:T(8,128)(2,1)S(1)}, bf16[128,1280]{1,0:T(8,128)(2,1)}, u32[]{:S(2)}) copy-start(bf16[128,1280]{1,0:T(8,128)(2,1)} %teacher_ref.1) | copy-start | bytes 983044
  93.2 5.5 %copy-start.4 = (s32[128,1]{0,1:T(1,128)S(1)}, s32[128,1]{0,1:T(1,128)}, u32[]{:S(2)}) copy-start(s32[128,1]{0,1:T(1,128)} %param.11) | copy-start | bytes 1540
  93.2 5.5 %copy-start.5 = (bf16[128]{0:T(256)(128)(2,1)S(1)}, bf16[128]{0:T(256)(128)(2,1)}, u32[]{:S(2)}) copy-start(bf16[128]{0:T(256)(128)(2,1)} %param.12) | copy-start | bytes 772
  93.4 8.3 %collective-permute-start.7 = (bf16[5,128,128]{2,1,0:T(8,128)(2,1)S(1)}, bf16[5,128,128]{2,1,0:T(8,128)(2,1)S(1)}, u32[]{:S(2)}, u32[]{:S(2)}) collective-permute-start(bf16[5,128,128]{2,1,0:T(8,128)(2,1)S(1)} %slice.24), channel_id=1, source_target_pairs={{0,32},{32,0},{64,96},{96,64},{128,160},{160,128},{192,224},{224,1... | collective-permute-start | bytes 491528 | tf_op jit(solution)/shard_map/ppermute | solution.py:304

commit v4 on v3

--- a/solution.py
+++ b/solution.py
@@ -49,32 +49,23 @@
     return centred * scale, scale
 
 
-def pack_kernel(route_ref, gates_ref, patches_hbm, teacher_hbm, out_hbm, patches, teacher, out, sems):
-    loads = [
-        pltpu.make_async_copy(patches_hbm, patches, sems.at[0]),
-        pltpu.make_async_copy(teacher_hbm, teacher, sems.at[1]),
-    ]
-    for load in loads:
-        load.start()
-
+def pack_kernel(route_ref, gates_ref, patches_ref, teacher_ref, out_hbm, out, sems):
     def store(second):
         lanes = pl.ds(second * D, D + second * BLK)
-        return pltpu.make_async_copy(out.at[:, lanes], out_hbm.at[:, lanes], sems.at[2 + second])
+        return pltpu.make_async_copy(out.at[:, lanes], out_hbm.at[:, lanes], sems.at[second])
 
     owners = out.shape[0] // SLOT
     place = slot_matrix(route_ref[...], owners)
     one_hot = place.astype(BF16)
-    gates = gates_ref[...].astype(F32)
-    gate = jnp.sum(jnp.where(place, gates, 0.0), axis=1, keepdims=True)
-    out[:, 2 * D :] = jnp.broadcast_to(gate, (place.shape[0], BLK)).astype(BF16)
-    loads[0].wait()
-    feats = patches[...].astype(F32)
+    feats = patches_ref[...].astype(F32)
     normed, _ = layer_norm(feats)
     out[:, :D] = dot(one_hot, normed.astype(BF16)).astype(BF16)
     early = store(0)
     early.start()
-    loads[1].wait()
-    differ = (feats - teacher[...].astype(F32)).astype(BF16)
+    gates = gates_ref[...].astype(F32)
+    gate = jnp.sum(jnp.where(place, gates, 0.0), axis=1, keepdims=True)
+    out[:, 2 * D :] = jnp.broadcast_to(gate, (place.shape[0], BLK)).astype(BF16)
+    differ = (feats - teacher_ref[...].astype(F32)).astype(BF16)
     out[:, D : 2 * D] = (gate * dot(one_hot, differ)).astype(BF16)
     late = store(1)
     late.start()
@@ -113,21 +104,19 @@
         y = (block % share) // half
         return lax.rem(x - my_x + n_x, n_x), lax.rem(y - my_y + 2, 2) * half + block % half
 
-    def send(kind):
-        copies = [
-            pltpu.make_async_copy(grads.at[kind, x], parts[kind][x], sems.at[kind, x])
-            for x in range(n_x)
-        ]
-        copies.append(
-            pltpu.make_async_copy(
-                ret.at[:, pl.ds((1 - kind) * D, D)],
-                ret_hbm.at[:, pl.ds((1 - kind) * D, D)],
-                ret_sems.at[kind],
-            )
-        )
-        for copy in copies:
-            copy.start()
-        return copies
+    copies = []
+
+    def send(source, target, sem):
+        copy = pltpu.make_async_copy(source, target, sem)
+        copy.start()
+        copies.append(copy)
+
+    def send_rows(kind):
+        lanes = pl.ds((1 - kind) * D, D)
+        send(ret.at[:, lanes], ret_hbm.at[:, lanes], ret_sems.at[kind])
+
+    def send_part(kind, x):
+        send(grads.at[kind, x], parts[kind][x], sems.at[kind, x])
 
     gn[...] = jnp.zeros_like(gn)
     loads[0].wait()
@@ -143,9 +132,10 @@
             v2 = v * v
             t = jnp.tanh(v * (GELU_K + (GELU_K * GELU_C) * v2))
             half_p = 0.5 + 0.5 * t
-            hid[c] = (v * half_p).astype(BF16)
-            slope[c] = half_p + v * (1.0 - t * t) * (
-                0.5 * GELU_K + (1.5 * GELU_K * GELU_C) * v2
+            active = v * half_p
+            hid[c] = active.astype(BF16)
+            slope[c] = half_p + (active - active * half_p) * (
+                2.0 * GELU_K + (6.0 * GELU_K * GELU_C) * v2
             )
             gh[c] = jnp.zeros_like(v)
         return carry
@@ -179,23 +169,25 @@
             grads[1, rel_x, pos] = outer[:, k * BLK : (k + 1) * BLK].astype(BF16)
             gh[r] += back[:, k * BLK : (k + 1) * BLK]
 
-    copies = send(1)
-
-    def backward(step, carry):
-        for q in range(UNROLL):
-            b = step * UNROLL + q
+    send_rows(1)
+    for x in range(n_x):
+        send_part(1, x)
+
+    for rel_x in (2, 1, 3, 0):
+        x = lax.rem(my_x + rel_x, n_x)
+        for q in range(share):
+            b = x * share + q
             c = in_cols[b]
             i = in_rows[b]
             grad_pre = (gh[c] * slope[c]).astype(BF16)
-            rel_x, pos = place(b)
-            grads[0, rel_x, pos] = dot(xnt[i], grad_pre).astype(BF16)
+            rel_y = q // half
+            rel_y = lax.rem(rel_y + my_y, 2)
+            grads[0, rel_x, rel_y * half + q % half] = dot(xnt[i], grad_pre).astype(BF16)
             gn[i] += dot_nt(grad_pre, w_in_ref[b])
-        return carry
-
-    lax.fori_loop(0, FB // UNROLL, backward, 0)
+        send_part(0, rel_x)
     for i in range(DB):
         ret[:, D + i * BLK : D + (i + 1) * BLK] = gn[i].astype(BF16)
-    copies += send(0)
+    send_rows(0)
     for copy in copies:
         copy.wait()
 
@@ -248,13 +240,11 @@
     payload = pl.pallas_call(
         pack_kernel,
         out_shape=jax.ShapeDtypeStruct((slots, 2 * D + BLK), BF16),
-        in_specs=[VMEM_SPEC] * 2 + [HBM_SPEC] * 2,
+        in_specs=[VMEM_SPEC] * 4,
         out_specs=HBM_SPEC,
         scratch_shapes=[
-            pltpu.VMEM((rows, D), BF16),
-            pltpu.VMEM((rows, D), BF16),
             pltpu.VMEM((slots, 2 * D + BLK), BF16),
-            pltpu.SemaphoreType.DMA((4,)),
+            pltpu.SemaphoreType.DMA((2,)),
         ],
         compiler_params=pltpu.CompilerParams(vmem_limit_bytes=60 << 20),
         name="pack",
@@ -312,6 +302,7 @@
     near_in = pass_on(part_in[3], 3)
     pair_in = pass_on(add(part_in[1], far_in).astype(BF16), 1)
     pair_out = pass_on(add(part_out[3], far_out).astype(BF16), 3)
+    pair_in, near_out = lax.optimization_barrier((pair_in, near_out))
     total_in = add(part_in[0], near_in, pair_in)
     total_out = add(part_out[0], near_out, pair_out)
     other_in = pass_on(total_in[half:].astype(BF16), 0, 1)

time: 103 us -> 103 us (level)
  waiting for transfers between devices: 54.9 us -> 59.5 us
  starting transfers between devices: 29.3 us -> 26 us
  Pallas kernels: 16.9 us -> 15.1 us
    ppermute x8, starting transfers between devices: 12.5 us -> 9.22 us  [pass_on(): return lax.ppermute(values, 'dp', shift(n_x, dx, dy))]
    ppermute x8, waiting for transfers between devices: 18.2 us -> 21.2 us  [pass_on(): return lax.ppermute(values, 'dp', shift(n_x, dx, dy))]
    all_to_all x2, waiting for transfers between devices: 36.6 us -> 38.3 us  [exchange(): lax.all_to_all(blocks, 'expert', split_axis=0, concat_axis=0, tiled=True)]
    pallas_call x1, Pallas kernels: 10.7 us -> 9.62 us  [local(): pl.pallas_call(expert_kernel, out_shape=(pltpu.HBM((slots, 2 * D), BF16),...]
  transfers between devices with their start and end apart: 10 -> 10, of which waited for: 7 -> 6; matrix products, arithmetic and copies ran while one was open for 1% -> 1% of each run, Pallas kernels for 2% -> 2%
where the time goes in v4:
time: 103 us; the launch traced here: 102 us
  waiting for transfers between devices  59.5 us (58%)
  starting transfers between devices  26 us (25%)
  Pallas kernels  15.1 us (15%)
    all_to_all x2, waiting for transfers between devices, exchange(): lax.all_to_all(blocks, 'expert', split_axis=0, concat_axis=0, tiled=True)  38.3 us
    ppermute x8, waiting for transfers between devices, pass_on(): return lax.ppermute(values, 'dp', shift(n_x, dx, dy))  21.2 us
    all_to_all x2, starting transfers between devices, exchange(): lax.all_to_all(blocks, 'expert', split_axis=0, concat_axis=0, tiled=True)  16.8 us
    pallas_call x1, Pallas kernels, local(): pl.pallas_call(expert_kernel, out_shape=(pltpu.HBM((slots, 2 * D), BF16),...  9.62 us
    ppermute x8, starting transfers between devices, pass_on(): return lax.ppermute(values, 'dp', shift(n_x, dx, dy))  9.22 us
    pallas_call x1, Pallas kernels, local(): pl.pallas_call(pack_kernel, out_shape=jax.ShapeDtypeStruct((slots, 2 * D...  2.82 us
  transfers between devices with their start and end apart: 10, of which 6 were waited for; matrix products, arithmetic and copies ran while one was open for 1% of the time, Pallas kernels for 2%

profile of v4, /device:TPU:1, one launch (start us, length us, event | category | flops | bytes accessed | tf_op | source)
XLA Modules:
  0.0 102.2 jit_solution(7858660353523569790)
XLA Ops:
  0.6 2.8 %pack.1 = bf16[256,2688]{1,0:T(8,128)(2,1)} custom-call(s32[1,128]{1,0:T(1,128)} %bitcast.18, bf16[1,128]{1,0:T(2,128)(2,1)} %bitcast.20, bf16[128,1280]{1,0:T(8,128)(2,1)} %patches_ref.3, bf16[128,1280]{1,0:T(8,128)(2,1)} %teacher_ref.3), custom_call_target="tpu_custom_call" | custom-call | tf_op jit(solution)/shard_map/pack/pallas_call | solution.py:240
  3.5 0.0 copy-start
  3.5 0.0 copy-start.1
  3.5 0.0 copy-start.6
  3.5 0.0 copy-start.7
  3.5 0.0 copy-start.8
  3.5 11.3 %all-to-all-start = ((bf16[32,8,2688]{2,1,0:T(8,128)(2,1)}), bf16[32,8,2688]{2,1,0:T(8,128)(2,1)}, u32[]{:S(2)}, u32[]{:S(2)}) async-start(bf16[32,8,2688]{2,1,0:T(8,128)(2,1)} %bitcast.25), calls=%async_computation | async-start | bytes 2752512 | tf_op jit(solution)/shard_map/all_to_all | solution.py:256
  14.9 0.1 pad_add_fusion.where_ref
  14.9 34.1 %all-to-all-done = bf16[32,8,2688]{2,1,0:T(8,128)(2,1)} async-done(((bf16[32,8,2688]{2,1,0:T(8,128)(2,1)}), bf16[32,8,2688]{2,1,0:T(8,128)(2,1)}, u32[]{:S(2)}, u32[]{:S(2)}) %all-to-all-start) | async-done | bytes 1376288 | tf_op jit(solution)/shard_map/all_to_all | solution.py:256
  49.0 0.0 copy-done
  49.0 0.0 copy-done.1
  49.0 0.0 copy-done.6
  49.0 0.0 copy-done.7
  49.1 0.0 copy-done.8
  49.1 9.6 %expert.1 = (bf16[256,2560]{1,0:T(8,128)(2,1)}, bf16[10,128,128]{2,1,0:T(8,128)(2,1)}, bf16[10,128,128]{2,1,0:T(8,128)(2,1)}, bf16[10,128,128]{2,1,0:T(8,128)(2,...) custom-call(s32[40]{0:T(128)S(1)} %bitcast.22, ...), custom_call_target="tpu_custom_call" | custom-call | tf_op jit(solution)/shard_map/expert/pallas_call | solution.py:263
  58.7 0.0 copy-start.14
  58.7 0.0 copy-start.12
  58.7 0.0 copy-start.13
  58.7 0.0 copy-start.11
  58.7 5.5 %all-to-all-start.1 = ((bf16[32,8,2560]{2,1,0:T(8,128)(2,1)}), bf16[32,8,2560]{2,1,0:T(8,128)(2,1)S(1)}, u32[]{:S(2)}, u32[]{:S(2)}) async-start(bf16[32,8,2560]{2,1,0:T(8,128)(2,1)} %bitcast.26), calls=%async_computation.1 | async-start | bytes 2621440 | tf_op jit(solution)/shard_map/all_to_all | solution.py:256
  64.2 0.0 copy-start.10
  64.2 1.3 %collective-permute-start.1 = (bf16[10,128,128]{2,1,0:T(8,128)(2,1)}, bf16[10,128,128]{2,1,0:T(8,128)(2,1)S(1)}, u32[]{:S(2)}, u32[]{:S(2)}) collective-permute-start(bf16[10,128,128]{2,1,0:T(8,128)(2,1)} %get-tuple-element.26), channel_id=1, source_target_pairs={{0,64},{32,96},{64,128},{96,160},{128,192},{160,224},{192,0},{224,... | collective-permute-start | bytes 983048 | tf_op jit(solution)/shard_map/ppermute | solution.py:294
  65.5 1.5 %collective-permute-start.4 = (bf16[10,128,128]{2,1,0:T(8,128)(2,1)S(1)}, bf16[10,128,128]{2,1,0:T(8,128)(2,1)S(1)}, u32[]{:S(2)}, u32[]{:S(2)}) collective-permute-start(bf16[10,128,128]{2,1,0:T(8,128)(2,1)S(1)} %copy-done.14), channel_id=1, source_target_pairs={{0,192},{32,224},{64,0},{96,32},{128,64},{160,96},{192,128},{224,1... | collective-permute-start | bytes 983048 | tf_op jit(solution)/shard_map/ppermute | solution.py:294
  67.0 0.0 collective-permute-start.3
  67.0 7.8 %collective-permute-done.1 = bf16[10,128,128]{2,1,0:T(8,128)(2,1)S(1)} collective-permute-done((bf16[10,128,128]{2,1,0:T(8,128)(2,1)}, bf16[10,128,128]{2,1,0:T(8,128)(2,1)S(1)}, u32[]{:S(2)}, u32[]{:S(2)}) %collective-permute-start.1) | collective-permute-done | bytes 327712 | tf_op jit(solution)/shard_map/ppermute | solution.py:294
  74.8 0.1 add_convert_fusion.1
  74.9 0.1 collective-permute-start.2
  75.0 2.7 %collective-permute-start = (bf16[10,128,128]{2,1,0:T(8,128)(2,1)S(1)}, bf16[10,128,128]{2,1,0:T(8,128)(2,1)S(1)}, u32[]{:S(2)}, u32[]{:S(2)}) collective-permute-start(bf16[10,128,128]{2,1,0:T(8,128)(2,1)S(1)} %copy-done.13), channel_id=1, source_target_pairs={{0,192},{32,224},{64,0},{96,32},{128,64},{160,96},{192,128},{224,1... | collective-permute-start | bytes 983048 | tf_op jit(solution)/shard_map/ppermute | solution.py:294
  77.7 0.0 collective-permute-done.4
  77.7 0.1 add_convert_fusion
  77.8 0.3 collective-permute-start.5
  78.1 3.7 %collective-permute-done.3 = bf16[10,128,128]{2,1,0:T(8,128)(2,1)S(1)} collective-permute-done((bf16[10,128,128]{2,1,0:T(8,128)(2,1)}, bf16[10,128,128]{2,1,0:T(8,128)(2,1)S(1)}, u32[]{:S(2)}, u32[]{:S(2)}) %collective-permute-start.3) | collective-permute-done | bytes 327712 | tf_op jit(solution)/shard_map/ppermute | solution.py:294
  81.8 7.0 %collective-permute-done.2 = bf16[10,128,128]{2,1,0:T(8,128)(2,1)S(1)} collective-permute-done((bf16[10,128,128]{2,1,0:T(8,128)(2,1)S(1)}, bf16[10,128,128]{2,1,0:T(8,128)(2,1)S(1)}, u32[]{:S(2)}, u32[]{:S(2)}) %collective-permute-start.2) | collective-permute-done | bytes 327712 | tf_op jit(solution)/shard_map/ppermute | solution.py:294
  88.9 0.0 collective-permute-done
  88.9 0.0 copy-done.10
  88.9 0.1 convert_add_fusion.1
  89.0 2.7 %collective-permute-start.6 = (bf16[5,128,128]{2,1,0:T(8,128)(2,1)S(1)}, bf16[5,128,128]{2,1,0:T(8,128)(2,1)S(1)}, u32[]{:S(2)}, u32[]{:S(2)}) collective-permute-start(bf16[5,128,128]{2,1,0:T(8,128)(2,1)S(1)} %slice.25), channel_id=1, source_target_pairs={{0,32},{32,0},{64,96},{96,64},{128,160},{160,128},{192,224},{224,1... | collective-permute-start | bytes 491528 | tf_op jit(solution)/shard_map/ppermute | solution.py:294
  91.7 0.0 collective-permute-done.5
  91.7 0.0 copy-start.4
  91.8 0.0 copy-start.5
  91.8 0.1 convert_add_fusion
  91.9 0.7 collective-permute-start.7
  92.7 4.2 %all-to-all-done.1 = bf16[32,8,2560]{2,1,0:T(8,128)(2,1)S(1)} async-done(((bf16[32,8,2560]{2,1,0:T(8,128)(2,1)}), bf16[32,8,2560]{2,1,0:T(8,128)(2,1)S(1)}, u32[]{:S(2)}, u32[]{:S(2)}) %all-to-all-start.1) | async-done | bytes 1310752 | tf_op jit(solution)/shard_map/all_to_all | solution.py:256
  96.9 0.0 copy-done.2
  96.9 1.7 %finish.1 = (bf16[128,1280]{1,0:T(8,128)(2,1)}, f32[128,1280]{1,0:T(8,128)}, f32[8,128]{1,0:T(8,128)S(1)}) custom-call(s32[1,128]{1,0:T(1,128)S(1)} %bitcast.19, bf16[1,128]{1,0:T(2,128)(2,1)S(1)} %bitcast.21, bf16[128,1280]{1,0:T(8,128)(2,1)S(1)} %copy-done.2, bf16[128,1280]{1,0:T(8,128)(2,1)S(1)} %copy-done.3, bf16[256,2560]{1,0:T(8,128)(2,1)S(1)} %bitcast.15), custom_call_target="tpu_custom_call" | custom-call | tf_op jit(solution)/shard_map/finish/pallas_call | solution.py:310
  98.6 0.0 collective-permute-done.6.other_in_ref
  98.6 2.6 %collective-permute-done.7.other_out_ref = bf16[5,128,128]{2,1,0:T(8,128)(2,1)S(1)} collective-permute-done((bf16[5,128,128]{2,1,0:T(8,128)(2,1)S(1)}, bf16[5,128,128]{2,1,0:T(8,128)(2,1)S(1)}, u32[]{:S(2)}, u32[]{:S(2)}) %collective-permute-start.7) | collective-permute-done | bytes 163872 | tf_op jit(solution)/shard_map/ppermute | solution.py:294
  101.3 1.0 total.1
  (15 shorter events, 0.1 us)
Async XLA Ops:
  3.5 45.6 %copy-start = (bf16[1,40,128,128]{3,2,1,0:T(8,128)(2,1)S(1)}, bf16[1,40,128,128]{3,2,1,0:T(8,128)(2,1)}, u32[]{:S(2)}) copy-start(bf16[1,40,128,128]{3,2,1,0:T(8,128)(2,1)} %param.13) | copy-start | bytes 3932164
  3.5 45.6 %copy-start.1 = (bf16[1,40,128,128]{3,2,1,0:T(8,128)(2,1)S(1)}, bf16[1,40,128,128]{3,2,1,0:T(8,128)(2,1)}, u32[]{:S(2)}) copy-start(bf16[1,40,128,128]{3,2,1,0:T(8,128)(2,1)} %param.16) | copy-start | bytes 3932164
  3.5 45.6 %copy-start.6 = (s32[1,40]{1,0:T(1,128)S(1)}, s32[1,40]{1,0:T(1,128)}, u32[]{:S(2)}) copy-start(s32[1,40]{1,0:T(1,128)} %param.14) | copy-start | bytes 484
  3.5 45.6 %copy-start.7 = (s32[1,40]{1,0:T(1,128)S(1)}, s32[1,40]{1,0:T(1,128)}, u32[]{:S(2)}) copy-start(s32[1,40]{1,0:T(1,128)} %param.15) | copy-start | bytes 484
  3.5 45.6 %copy-start.8 = (s32[1,40]{1,0:T(1,128)S(1)}, s32[1,40]{1,0:T(1,128)}, u32[]{:S(2)}) copy-start(s32[1,40]{1,0:T(1,128)} %param.17) | copy-start | bytes 484
  3.5 45.5 %all-to-all-start = ((bf16[32,8,2688]{2,1,0:T(8,128)(2,1)}), bf16[32,8,2688]{2,1,0:T(8,128)(2,1)}, u32[]{:S(2)}, u32[]{:S(2)}) async-start(bf16[32,8,2688]{2,1,0:T(8,128)(2,1)} %bitcast.25), calls=%async_computation | async-start | bytes 2752512 | tf_op jit(solution)/shard_map/all_to_all | solution.py:256
  58.7 6.8 %copy-start.14 = (bf16[10,128,128]{2,1,0:T(8,128)(2,1)S(1)}, bf16[10,128,128]{2,1,0:T(8,128)(2,1)}, u32[]{:S(2)}) copy-start(bf16[10,128,128]{2,1,0:T(8,128)(2,1)} %get-tuple-element.32) | copy-start | bytes 983044
  58.7 16.1 %copy-start.12 = (bf16[10,128,128]{2,1,0:T(8,128)(2,1)S(1)}, bf16[10,128,128]{2,1,0:T(8,128)(2,1)}, u32[]{:S(2)}) copy-start(bf16[10,128,128]{2,1,0:T(8,128)(2,1)} %get-tuple-element.25) | copy-start | bytes 983044
  58.7 16.3 %copy-start.13 = (bf16[10,128,128]{2,1,0:T(8,128)(2,1)S(1)}, bf16[10,128,128]{2,1,0:T(8,128)(2,1)}, u32[]{:S(2)}) copy-start(bf16[10,128,128]{2,1,0:T(8,128)(2,1)} %get-tuple-element.24) | copy-start | bytes 983044
  58.7 19.0 %copy-start.11 = (bf16[10,128,128]{2,1,0:T(8,128)(2,1)S(1)}, bf16[10,128,128]{2,1,0:T(8,128)(2,1)}, u32[]{:S(2)}) copy-start(bf16[10,128,128]{2,1,0:T(8,128)(2,1)} %get-tuple-element.31) | copy-start | bytes 983044
  58.7 38.1 %all-to-all-start.1 = ((bf16[32,8,2560]{2,1,0:T(8,128)(2,1)}), bf16[32,8,2560]{2,1,0:T(8,128)(2,1)S(1)}, u32[]{:S(2)}, u32[]{:S(2)}) async-start(bf16[32,8,2560]{2,1,0:T(8,128)(2,1)} %bitcast.26), calls=%async_computation.1 | async-start | bytes 2621440 | tf_op jit(solution)/shard_map/all_to_all | solution.py:256
  64.2 24.6 %copy-start.10 = (bf16[10,128,128]{2,1,0:T(8,128)(2,1)S(1)}, bf16[10,128,128]{2,1,0:T(8,128)(2,1)}, u32[]{:S(2)}) copy-start(bf16[10,128,128]{2,1,0:T(8,128)(2,1)} %get-tuple-element.23) | copy-start | bytes 983044
  64.2 10.6 %collective-permute-start.1 = (bf16[10,128,128]{2,1,0:T(8,128)(2,1)}, bf16[10,128,128]{2,1,0:T(8,128)(2,1)S(1)}, u32[]{:S(2)}, u32[]{:S(2)}) collective-permute-start(bf16[10,128,128]{2,1,0:T(8,128)(2,1)} %get-tuple-element.26), channel_id=1, source_target_pairs={{0,64},{32,96},{64,128},{96,160},{128,192},{160,224},{192,0},{224,... | collective-permute-start | bytes 983048 | tf_op jit(solution)/shard_map/ppermute | solution.py:294
  65.5 12.1 %collective-permute-start.4 = (bf16[10,128,128]{2,1,0:T(8,128)(2,1)S(1)}, bf16[10,128,128]{2,1,0:T(8,128)(2,1)S(1)}, u32[]{:S(2)}, u32[]{:S(2)}) collective-permute-start(bf16[10,128,128]{2,1,0:T(8,128)(2,1)S(1)} %copy-done.14), channel_id=1, source_target_pairs={{0,192},{32,224},{64,0},{96,32},{128,64},{160,96},{192,128},{224,1... | collective-permute-start | bytes 983048 | tf_op jit(solution)/shard_map/ppermute | solution.py:294
  67.0 14.8 %collective-permute-start.3 = (bf16[10,128,128]{2,1,0:T(8,128)(2,1)}, bf16[10,128,128]{2,1,0:T(8,128)(2,1)S(1)}, u32[]{:S(2)}, u32[]{:S(2)}) collective-permute-start(bf16[10,128,128]{2,1,0:T(8,128)(2,1)} %get-tuple-element.27), channel_id=1, source_target_pairs={{0,64},{32,96},{64,128},{96,160},{128,192},{160,224},{192,0},{224,... | collective-permute-start | bytes 983048 | tf_op jit(solution)/shard_map/ppermute | solution.py:294
  74.9 13.9 %collective-permute-start.2 = (bf16[10,128,128]{2,1,0:T(8,128)(2,1)S(1)}, bf16[10,128,128]{2,1,0:T(8,128)(2,1)S(1)}, u32[]{:S(2)}, u32[]{:S(2)}) collective-permute-start(bf16[10,128,128]{2,1,0:T(8,128)(2,1)S(1)} %add_convert_fusion.1), channel_id=1, source_target_pairs={{0,64},{32,96},{64,128},{96,160},{128,192},{160,224},{192,0},{224,... | collective-permute-start | bytes 983048 | tf_op jit(solution)/shard_map/ppermute | solution.py:294
  75.0 13.8 %collective-permute-start = (bf16[10,128,128]{2,1,0:T(8,128)(2,1)S(1)}, bf16[10,128,128]{2,1,0:T(8,128)(2,1)S(1)}, u32[]{:S(2)}, u32[]{:S(2)}) collective-permute-start(bf16[10,128,128]{2,1,0:T(8,128)(2,1)S(1)} %copy-done.13), channel_id=1, source_target_pairs={{0,192},{32,224},{64,0},{96,32},{128,64},{160,96},{192,128},{224,1... | collective-permute-start | bytes 983048 | tf_op jit(solution)/shard_map/ppermute | solution.py:294
  77.7 14.0 %copy-start.9 = (bf16[10,128,128]{2,1,0:T(8,128)(2,1)S(1)}, bf16[10,128,128]{2,1,0:T(8,128)(2,1)}, u32[]{:S(2)}) copy-start(bf16[10,128,128]{2,1,0:T(8,128)(2,1)} %get-tuple-element.29) | copy-start | bytes 983044
  77.8 13.9 %collective-permute-start.5 = (bf16[10,128,128]{2,1,0:T(8,128)(2,1)S(1)}, bf16[10,128,128]{2,1,0:T(8,128)(2,1)S(1)}, u32[]{:S(2)}, u32[]{:S(2)}) collective-permute-start(bf16[10,128,128]{2,1,0:T(8,128)(2,1)S(1)} %add_convert_fusion), channel_id=1, source_target_pairs={{0,192},{32,224},{64,0},{96,32},{128,64},{160,96},{192,128},{224,1... | collective-permute-start | bytes 983048 | tf_op jit(solution)/shard_map/ppermute | solution.py:294
  89.0 9.6 %collective-permute-start.6 = (bf16[5,128,128]{2,1,0:T(8,128)(2,1)S(1)}, bf16[5,128,128]{2,1,0:T(8,128)(2,1)S(1)}, u32[]{:S(2)}, u32[]{:S(2)}) collective-permute-start(bf16[5,128,128]{2,1,0:T(8,128)(2,1)S(1)} %slice.25), channel_id=1, source_target_pairs={{0,32},{32,0},{64,96},{96,64},{128,160},{160,128},{192,224},{224,1... | collective-permute-start | bytes 491528 | tf_op jit(solution)/shard_map/ppermute | solution.py:294
  91.7 5.1 %copy-start.2 = (bf16[128,1280]{1,0:T(8,128)(2,1)S(1)}, bf16[128,1280]{1,0:T(8,128)(2,1)}, u32[]{:S(2)}) copy-start(bf16[128,1280]{1,0:T(8,128)(2,1)} %patches_ref.3) | copy-start | bytes 983044
  91.7 5.1 %copy-start.3 = (bf16[128,1280]{1,0:T(8,128)(2,1)S(1)}, bf16[128,1280]{1,0:T(8,128)(2,1)}, u32[]{:S(2)}) copy-start(bf16[128,1280]{1,0:T(8,128)(2,1)} %teacher_ref.3) | copy-start | bytes 983044
  91.7 5.1 %copy-start.4 = (s32[128,1]{0,1:T(1,128)S(1)}, s32[128,1]{0,1:T(1,128)}, u32[]{:S(2)}) copy-start(s32[128,1]{0,1:T(1,128)} %param.11) | copy-start | bytes 1540
  91.8 5.1 %copy-start.5 = (bf16[128]{0:T(256)(128)(2,1)S(1)}, bf16[128]{0:T(256)(128)(2,1)}, u32[]{:S(2)}) copy-start(bf16[128]{0:T(256)(128)(2,1)} %param.12) | copy-start | bytes 772
  91.9 9.3 %collective-permute-start.7 = (bf16[5,128,128]{2,1,0:T(8,128)(2,1)S(1)}, bf16[5,128,128]{2,1,0:T(8,128)(2,1)S(1)}, u32[]{:S(2)}, u32[]{:S(2)}) collective-permute-start(bf16[5,128,128]{2,1,0:T(8,128)(2,1)S(1)} %slice.24), channel_id=1, source_target_pairs={{0,32},{32,0},{64,96},{96,64},{128,160},{160,128},{192,224},{224,1... | collective-permute-start | bytes 491528 | tf_op jit(solution)/shard_map/ppermute | solution.py:294

commit v5 on v4

--- a/solution.py
+++ b/solution.py
@@ -111,17 +111,15 @@
         copy.start()
         copies.append(copy)
 
-    def send_rows(kind):
-        lanes = pl.ds((1 - kind) * D, D)
-        send(ret.at[:, lanes], ret_hbm.at[:, lanes], ret_sems.at[kind])
+    def send_rows(start, width, sem):
+        lanes = pl.ds(start, width)
+        send(ret.at[:, lanes], ret_hbm.at[:, lanes], ret_sems.at[sem])
 
     def send_part(kind, x):
         send(grads.at[kind, x], parts[kind][x], sems.at[kind, x])
 
     gn[...] = jnp.zeros_like(gn)
     loads[0].wait()
-    for i in range(DB):
-        xnt[i] = pay_ref[:, i * BLK : (i + 1) * BLK].T
 
     def forward(step, carry):
         for q in range(UNROLL):
@@ -155,6 +153,7 @@
         return w_out_ref[K2 * j : K2 * (j + 1)].reshape(K2 * BLK, BLK)
 
     for j in range(DB):
+        xnt[j] = pay_ref[:, j * BLK : (j + 1) * BLK].T
         produced = dot(spread(j), weight(j)).astype(BF16)
         ret[:, j * BLK : (j + 1) * BLK] = produced
         given = pay_ref[:, D + j * BLK : D + (j + 1) * BLK].astype(F32)
@@ -169,7 +168,7 @@
             grads[1, rel_x, pos] = outer[:, k * BLK : (k + 1) * BLK].astype(BF16)
             gh[r] += back[:, k * BLK : (k + 1) * BLK]
 
-    send_rows(1)
+    send_rows(0, D, 0)
     for x in range(n_x):
         send_part(1, x)
 
@@ -187,7 +186,8 @@
         send_part(0, rel_x)
     for i in range(DB):
         ret[:, D + i * BLK : D + (i + 1) * BLK] = gn[i].astype(BF16)
-    send_rows(0)
+        if i % 2:
+            send_rows(D + (i - 1) * BLK, 2 * BLK, 1 + i // 2)
     for copy in copies:
         copy.wait()
 
@@ -212,10 +212,13 @@
     grad_ref[...] = mismatch + scale * (grad - mean_grad - normed * mean_both)
 
 
-def total_kernel(mine_in_ref, mine_out_ref, other_in_ref, other_out_ref, after_ref, in_ref, out_ref):
-    for q in range(in_ref.shape[0]):
-        in_ref[q] = mine_in_ref[q] + other_in_ref[q].astype(F32)
-        out_ref[q] = (mine_out_ref[q] + other_out_ref[q].astype(F32)).T
+def total_out_kernel(mine_ref, other_ref, out_ref):
+    for q in range(out_ref.shape[0]):
+        out_ref[q] = (mine_ref[q] + other_ref[q].astype(F32)).T
+
+
+def total_in_kernel(mine_ref, other_ref, after_ref, out_ref):
+    out_ref[...] = mine_ref[...] + other_ref[...].astype(F32)
 
 
 def shift(n_x, dx, dy):
@@ -279,7 +282,7 @@
             pltpu.VMEM((DB, slots, BLK), BF16),
             pltpu.VMEM((DB, BLK, slots), BF16),
             pltpu.SemaphoreType.DMA((3,)),
-            pltpu.SemaphoreType.DMA((2,)),
+            pltpu.SemaphoreType.DMA((6,)),
             pltpu.SemaphoreType.DMA((2, n_x)),
         ],
         compiler_params=pltpu.CompilerParams(vmem_limit_bytes=51 << 20),
@@ -296,17 +299,17 @@
     def add(*values):
         return sum(v.astype(F32) for v in values)
 
-    far_in = pass_on(part_in[2], 1)
-    far_out = pass_on(part_out[2], 3)
-    near_out = pass_on(part_out[1], 1)
-    near_in = pass_on(part_in[3], 3)
-    pair_in = pass_on(add(part_in[1], far_in).astype(BF16), 1)
-    pair_out = pass_on(add(part_out[3], far_out).astype(BF16), 3)
-    pair_in, near_out = lax.optimization_barrier((pair_in, near_out))
+    far_out = pass_on(part_out[2], 1)
+    far_in = pass_on(part_in[2], 3)
+    near_in = pass_on(part_in[1], 1)
+    near_out = pass_on(part_out[3], 3)
+    pair_out = pass_on(add(part_out[1], far_out).astype(BF16), 1)
+    pair_in = pass_on(add(part_in[3], far_in).astype(BF16), 3)
+    pair_out, near_in = lax.optimization_barrier((pair_out, near_in))
+    total_out = add(part_out[0], near_out, pair_out)
     total_in = add(part_in[0], near_in, pair_in)
-    total_out = add(part_out[0], near_out, pair_out)
+    other_out = pass_on(total_out[half:].astype(BF16), 0, 1)
     other_in = pass_on(total_in[half:].astype(BF16), 0, 1)
-    other_out = pass_on(total_out[half:].astype(BF16), 0, 1)
     student, grad_patches, corner = pl.pallas_call(
         finish_kernel,
         out_shape=(
@@ -319,15 +322,18 @@
         compiler_params=pltpu.CompilerParams(vmem_limit_bytes=16 << 20),
         name="finish",
     )(route_row, gates_row, patches, teacher, back)
-    block = jax.ShapeDtypeStruct((half, BLK, BLK), F32)
-    grad_in, grad_out = pl.pallas_call(
-        total_kernel,
-        out_shape=(block, block),
-        in_specs=[VMEM_SPEC] * 5,
-        out_specs=(VMEM_SPEC, VMEM_SPEC),
-        compiler_params=pltpu.CompilerParams(vmem_limit_bytes=16 << 20),
-        name="total",
-    )(total_in[:half], total_out[:half], other_in, other_out, corner)
+    def total(kernel, *operands):
+        return pl.pallas_call(
+            kernel,
+            out_shape=jax.ShapeDtypeStruct((half, BLK, BLK), F32),
+            in_specs=[VMEM_SPEC] * len(operands),
+            out_specs=VMEM_SPEC,
+            compiler_params=pltpu.CompilerParams(vmem_limit_bytes=16 << 20),
+            name="total",
+        )(*operands)
+
+    grad_out = total(total_out_kernel, total_out[:half], other_out)
+    grad_in = total(total_in_kernel, total_in[:half], other_in, corner)
     return (student, grad_patches, grad_in[None], grad_out[None])
 
 

time: 103 us -> 102 us (level)
    all_to_all x2, waiting for transfers between devices: 38.3 us -> 34.1 us  [exchange(): lax.all_to_all(blocks, 'expert', split_axis=0, concat_axis=0, tiled=True)]
    ppermute x8, waiting for transfers between devices: 21.2 us -> 24.4 us  [pass_on(): return lax.ppermute(values, 'dp', shift(n_x, dx, dy))]
  transfers between devices with their start and end apart: 10 -> 10, of which waited for: 6 -> 6; matrix products, arithmetic and copies ran while one was open for 1% -> 1% of each run, Pallas kernels for 2% -> 3%
where the time goes in v5:
time: 102 us
  waiting for transfers between devices  58.5 us (57%)
  starting transfers between devices  26 us (25%)
  Pallas kernels  15.6 us (15%)
    all_to_all x2, waiting for transfers between devices, exchange(): lax.all_to_all(blocks, 'expert', split_axis=0, concat_axis=0, tiled=True)  34.1 us
    ppermute x8, waiting for transfers between devices, pass_on(): return lax.ppermute(values, 'dp', shift(n_x, dx, dy))  24.4 us
    all_to_all x2, starting transfers between devices, exchange(): lax.all_to_all(blocks, 'expert', split_axis=0, concat_axis=0, tiled=True)  16.8 us
    pallas_call x1, Pallas kernels, local(): pl.pallas_call(expert_kernel, out_shape=(pltpu.HBM((slots, 2 * D), BF16),...  9.39 us
    ppermute x8, starting transfers between devices, pass_on(): return lax.ppermute(values, 'dp', shift(n_x, dx, dy))  9.22 us
    pallas_call x1, Pallas kernels, local(): pl.pallas_call(pack_kernel, out_shape=jax.ShapeDtypeStruct((slots, 2 * D...  2.83 us
  transfers between devices with their start and end apart: 10, of which 6 were waited for; matrix products, arithmetic and copies ran while one was open for 1% of the time, Pallas kernels for 3%

profile of v5, /device:TPU:1, one launch (start us, length us, event | category | flops | bytes accessed | tf_op | source)
XLA Modules:
  0.0 101.7 jit_solution(223967944368774506)
XLA Ops:
  0.6 2.8 %pack.1 = bf16[256,2688]{1,0:T(8,128)(2,1)} custom-call(s32[1,128]{1,0:T(1,128)} %bitcast.18, bf16[1,128]{1,0:T(2,128)(2,1)} %bitcast.20, bf16[128,1280]{1,0:T(8,128)(2,1)} %patches_ref.3, bf16[128,1280]{1,0:T(8,128)(2,1)} %teacher_ref.3), custom_call_target="tpu_custom_call" | custom-call | tf_op jit(solution)/shard_map/pack/pallas_call | solution.py:243
  3.5 0.0 copy-start
  3.5 0.0 copy-start.1
  3.5 0.0 copy-start.6
  3.5 0.0 copy-start.7
  3.5 0.0 copy-start.8
  3.5 11.3 %all-to-all-start = ((bf16[32,8,2688]{2,1,0:T(8,128)(2,1)}), bf16[32,8,2688]{2,1,0:T(8,128)(2,1)}, u32[]{:S(2)}, u32[]{:S(2)}) async-start(bf16[32,8,2688]{2,1,0:T(8,128)(2,1)} %bitcast.25), calls=%async_computation | async-start | bytes 2752512 | tf_op jit(solution)/shard_map/all_to_all | solution.py:259
  14.9 0.1 pad_add_fusion.where_ref
  15.0 34.1 %all-to-all-done = bf16[32,8,2688]{2,1,0:T(8,128)(2,1)} async-done(((bf16[32,8,2688]{2,1,0:T(8,128)(2,1)}), bf16[32,8,2688]{2,1,0:T(8,128)(2,1)}, u32[]{:S(2)}, u32[]{:S(2)}) %all-to-all-start) | async-done | bytes 1376288 | tf_op jit(solution)/shard_map/all_to_all | solution.py:259
  49.1 9.4 %expert.1 = (bf16[256,2560]{1,0:T(8,128)(2,1)}, bf16[10,128,128]{2,1,0:T(8,128)(2,1)}, bf16[10,128,128]{2,1,0:T(8,128)(2,1)}, bf16[10,128,128]{2,1,0:T(8,128)(2,...) custom-call(s32[40]{0:T(128)S(1)} %bitcast.22, ...), custom_call_target="tpu_custom_call" | custom-call | tf_op jit(solution)/shard_map/expert/pallas_call | solution.py:266
  58.5 0.0 copy-start.16
  58.5 0.0 copy-start.15
  58.5 0.0 copy-start.14
  58.5 0.0 copy-start.11
  58.5 5.5 %all-to-all-start.1 = ((bf16[32,8,2560]{2,1,0:T(8,128)(2,1)}), bf16[32,8,2560]{2,1,0:T(8,128)(2,1)S(1)}, u32[]{:S(2)}, u32[]{:S(2)}) async-start(bf16[32,8,2560]{2,1,0:T(8,128)(2,1)} %bitcast.26), calls=%async_computation.1 | async-start | bytes 2621440 | tf_op jit(solution)/shard_map/all_to_all | solution.py:259
  64.0 0.0 copy-start.10
  64.1 0.0 copy-done.16
  64.1 1.3 %collective-permute-start = (bf16[10,128,128]{2,1,0:T(8,128)(2,1)S(1)}, bf16[10,128,128]{2,1,0:T(8,128)(2,1)S(1)}, u32[]{:S(2)}, u32[]{:S(2)}) collective-permute-start(bf16[10,128,128]{2,1,0:T(8,128)(2,1)S(1)} %copy-done.16), channel_id=1, source_target_pairs={{0,64},{32,96},{64,128},{96,160},{128,192},{160,224},{192,0},{224,... | collective-permute-start | bytes 983048 | tf_op jit(solution)/shard_map/ppermute | solution.py:297
  65.4 1.5 %collective-permute-start.3 = (bf16[10,128,128]{2,1,0:T(8,128)(2,1)S(1)}, bf16[10,128,128]{2,1,0:T(8,128)(2,1)S(1)}, u32[]{:S(2)}, u32[]{:S(2)}) collective-permute-start(bf16[10,128,128]{2,1,0:T(8,128)(2,1)S(1)} %copy-done.15), channel_id=1, source_target_pairs={{0,192},{32,224},{64,0},{96,32},{128,64},{160,96},{192,128},{224,1... | collective-permute-start | bytes 983048 | tf_op jit(solution)/shard_map/ppermute | solution.py:297
  66.8 0.0 collective-permute-start.2
  66.8 7.6 %collective-permute-done = bf16[10,128,128]{2,1,0:T(8,128)(2,1)S(1)} collective-permute-done((bf16[10,128,128]{2,1,0:T(8,128)(2,1)S(1)}, bf16[10,128,128]{2,1,0:T(8,128)(2,1)S(1)}, u32[]{:S(2)}, u32[]{:S(2)}) %collective-permute-start) | collective-permute-done | bytes 327712 | tf_op jit(solution)/shard_map/ppermute | solution.py:297
  74.4 0.1 add_convert_fusion.1
  74.5 0.1 collective-permute-start.1
  74.6 2.7 %collective-permute-start.6 = (bf16[10,128,128]{2,1,0:T(8,128)(2,1)S(1)}, bf16[10,128,128]{2,1,0:T(8,128)(2,1)S(1)}, u32[]{:S(2)}, u32[]{:S(2)}) collective-permute-start(bf16[10,128,128]{2,1,0:T(8,128)(2,1)S(1)} %copy-done.13), channel_id=1, source_target_pairs={{0,192},{32,224},{64,0},{96,32},{128,64},{160,96},{192,128},{224,1... | collective-permute-start | bytes 983048 | tf_op jit(solution)/shard_map/ppermute | solution.py:297
  77.3 0.0 collective-permute-done.3
  77.3 0.0 copy-done.11
  77.3 0.1 add_convert_fusion
  77.4 0.3 collective-permute-start.4
  77.7 3.7 %collective-permute-done.2 = bf16[10,128,128]{2,1,0:T(8,128)(2,1)S(1)} collective-permute-done((bf16[10,128,128]{2,1,0:T(8,128)(2,1)S(1)}, bf16[10,128,128]{2,1,0:T(8,128)(2,1)S(1)}, u32[]{:S(2)}, u32[]{:S(2)}) %collective-permute-start.2) | collective-permute-done | bytes 327712 | tf_op jit(solution)/shard_map/ppermute | solution.py:297
  81.5 7.0 %collective-permute-done.1 = bf16[10,128,128]{2,1,0:T(8,128)(2,1)S(1)} collective-permute-done((bf16[10,128,128]{2,1,0:T(8,128)(2,1)S(1)}, bf16[10,128,128]{2,1,0:T(8,128)(2,1)S(1)}, u32[]{:S(2)}, u32[]{:S(2)}) %collective-permute-start.1) | collective-permute-done | bytes 327712 | tf_op jit(solution)/shard_map/ppermute | solution.py:297
  88.5 0.0 collective-permute-done.6
  88.5 0.1 convert_add_fusion
  88.6 2.7 %collective-permute-start.7 = (bf16[5,128,128]{2,1,0:T(8,128)(2,1)S(1)}, bf16[5,128,128]{2,1,0:T(8,128)(2,1)S(1)}, u32[]{:S(2)}, u32[]{:S(2)}) collective-permute-start(bf16[5,128,128]{2,1,0:T(8,128)(2,1)S(1)} %slice.24), channel_id=1, source_target_pairs={{0,32},{32,0},{64,96},{96,64},{128,160},{160,128},{192,224},{224,1... | collective-permute-start | bytes 491528 | tf_op jit(solution)/shard_map/ppermute | solution.py:297
  91.3 0.0 collective-permute-done.4
  91.3 0.0 copy-done.9
  91.3 0.1 convert_add_fusion.1
  91.5 0.0 copy-start.2
  91.5 0.0 copy-start.3
  91.5 0.0 copy-start.4
  91.5 0.0 copy-start.5
  91.5 0.7 collective-permute-start.5
  92.3 3.9 %collective-permute-done.7.other_ref = bf16[5,128,128]{2,1,0:T(8,128)(2,1)S(1)} collective-permute-done((bf16[5,128,128]{2,1,0:T(8,128)(2,1)S(1)}, bf16[5,128,128]{2,1,0:T(8,128)(2,1)S(1)}, u32[]{:S(2)}, u32[]{:S(2)}) %collective-permute-start.7) | collective-permute-done | bytes 163872 | tf_op jit(solution)/shard_map/ppermute | solution.py:297
  96.2 0.9 total.3
  97.1 0.0 all-to-all-done.1
  97.1 0.0 copy-done.2
  97.1 1.7 %finish.1 = (bf16[128,1280]{1,0:T(8,128)(2,1)}, f32[128,1280]{1,0:T(8,128)}, f32[8,128]{1,0:T(8,128)S(1)}) custom-call(s32[1,128]{1,0:T(1,128)S(1)} %bitcast.19, bf16[1,128]{1,0:T(2,128)(2,1)S(1)} %bitcast.21, bf16[128,1280]{1,0:T(8,128)(2,1)S(1)} %copy-done.2, bf16[128,1280]{1,0:T(8,128)(2,1)S(1)} %copy-done.3, bf16[256,2560]{1,0:T(8,128)(2,1)S(1)} %bitcast.15), custom_call_target="tpu_custom_call" | custom-call | tf_op jit(solution)/shard_map/finish/pallas_call | solution.py:313
  98.9 2.1 %collective-permute-done.5.other_ref = bf16[5,128,128]{2,1,0:T(8,128)(2,1)S(1)} collective-permute-done((bf16[5,128,128]{2,1,0:T(8,128)(2,1)S(1)}, bf16[5,128,128]{2,1,0:T(8,128)(2,1)S(1)}, u32[]{:S(2)}, u32[]{:S(2)}) %collective-permute-start.5) | collective-permute-done | bytes 163872 | tf_op jit(solution)/shard_map/ppermute | solution.py:297
  101.0 0.8 total.2
  (20 shorter events, 0.1 us)
Async XLA Ops:
  3.5 45.6 %copy-start = (bf16[1,40,128,128]{3,2,1,0:T(8,128)(2,1)S(1)}, bf16[1,40,128,128]{3,2,1,0:T(8,128)(2,1)}, u32[]{:S(2)}) copy-start(bf16[1,40,128,128]{3,2,1,0:T(8,128)(2,1)} %param.13) | copy-start | bytes 3932164
  3.5 45.6 %copy-start.1 = (bf16[1,40,128,128]{3,2,1,0:T(8,128)(2,1)S(1)}, bf16[1,40,128,128]{3,2,1,0:T(8,128)(2,1)}, u32[]{:S(2)}) copy-start(bf16[1,40,128,128]{3,2,1,0:T(8,128)(2,1)} %param.16) | copy-start | bytes 3932164
  3.5 45.6 %copy-start.6 = (s32[1,40]{1,0:T(1,128)S(1)}, s32[1,40]{1,0:T(1,128)}, u32[]{:S(2)}) copy-start(s32[1,40]{1,0:T(1,128)} %param.14) | copy-start | bytes 484
  3.5 45.6 %copy-start.7 = (s32[1,40]{1,0:T(1,128)S(1)}, s32[1,40]{1,0:T(1,128)}, u32[]{:S(2)}) copy-start(s32[1,40]{1,0:T(1,128)} %param.15) | copy-start | bytes 484
  3.5 45.6 %copy-start.8 = (s32[1,40]{1,0:T(1,128)S(1)}, s32[1,40]{1,0:T(1,128)}, u32[]{:S(2)}) copy-start(s32[1,40]{1,0:T(1,128)} %param.17) | copy-start | bytes 484
  3.5 45.5 %all-to-all-start = ((bf16[32,8,2688]{2,1,0:T(8,128)(2,1)}), bf16[32,8,2688]{2,1,0:T(8,128)(2,1)}, u32[]{:S(2)}, u32[]{:S(2)}) async-start(bf16[32,8,2688]{2,1,0:T(8,128)(2,1)} %bitcast.25), calls=%async_computation | async-start | bytes 2752512 | tf_op jit(solution)/shard_map/all_to_all | solution.py:259
  58.5 5.6 %copy-start.16 = (bf16[10,128,128]{2,1,0:T(8,128)(2,1)S(1)}, bf16[10,128,128]{2,1,0:T(8,128)(2,1)}, u32[]{:S(2)}) copy-start(bf16[10,128,128]{2,1,0:T(8,128)(2,1)} %get-tuple-element.23) | copy-start | bytes 983044
  58.5 6.9 %copy-start.15 = (bf16[10,128,128]{2,1,0:T(8,128)(2,1)S(1)}, bf16[10,128,128]{2,1,0:T(8,128)(2,1)}, u32[]{:S(2)}) copy-start(bf16[10,128,128]{2,1,0:T(8,128)(2,1)} %get-tuple-element.27) | copy-start | bytes 983044
  58.5 8.3 %copy-start.14 = (bf16[10,128,128]{2,1,0:T(8,128)(2,1)S(1)}, bf16[10,128,128]{2,1,0:T(8,128)(2,1)}, u32[]{:S(2)}) copy-start(bf16[10,128,128]{2,1,0:T(8,128)(2,1)} %get-tuple-element.24) | copy-start | bytes 983044
  58.5 15.9 %copy-start.12 = (bf16[10,128,128]{2,1,0:T(8,128)(2,1)S(1)}, bf16[10,128,128]{2,1,0:T(8,128)(2,1)}, u32[]{:S(2)}) copy-start(bf16[10,128,128]{2,1,0:T(8,128)(2,1)} %get-tuple-element.22) | copy-start | bytes 983044
  58.5 16.1 %copy-start.13 = (bf16[10,128,128]{2,1,0:T(8,128)(2,1)S(1)}, bf16[10,128,128]{2,1,0:T(8,128)(2,1)}, u32[]{:S(2)}) copy-start(bf16[10,128,128]{2,1,0:T(8,128)(2,1)} %get-tuple-element.30) | copy-start | bytes 983044
  58.5 18.8 %copy-start.11 = (bf16[10,128,128]{2,1,0:T(8,128)(2,1)S(1)}, bf16[10,128,128]{2,1,0:T(8,128)(2,1)}, u32[]{:S(2)}) copy-start(bf16[10,128,128]{2,1,0:T(8,128)(2,1)} %get-tuple-element.26) | copy-start | bytes 983044
  58.5 38.5 %all-to-all-start.1 = ((bf16[32,8,2560]{2,1,0:T(8,128)(2,1)}), bf16[32,8,2560]{2,1,0:T(8,128)(2,1)S(1)}, u32[]{:S(2)}, u32[]{:S(2)}) async-start(bf16[32,8,2560]{2,1,0:T(8,128)(2,1)} %bitcast.26), calls=%async_computation.1 | async-start | bytes 2621440 | tf_op jit(solution)/shard_map/all_to_all | solution.py:259
  64.0 24.4 %copy-start.10 = (bf16[10,128,128]{2,1,0:T(8,128)(2,1)S(1)}, bf16[10,128,128]{2,1,0:T(8,128)(2,1)}, u32[]{:S(2)}) copy-start(bf16[10,128,128]{2,1,0:T(8,128)(2,1)} %get-tuple-element.29) | copy-start | bytes 983044
  64.1 10.4 %collective-permute-start = (bf16[10,128,128]{2,1,0:T(8,128)(2,1)S(1)}, bf16[10,128,128]{2,1,0:T(8,128)(2,1)S(1)}, u32[]{:S(2)}, u32[]{:S(2)}) collective-permute-start(bf16[10,128,128]{2,1,0:T(8,128)(2,1)S(1)} %copy-done.16), channel_id=1, source_target_pairs={{0,64},{32,96},{64,128},{96,160},{128,192},{160,224},{192,0},{224,... | collective-permute-start | bytes 983048 | tf_op jit(solution)/shard_map/ppermute | solution.py:297
  65.4 11.9 %collective-permute-start.3 = (bf16[10,128,128]{2,1,0:T(8,128)(2,1)S(1)}, bf16[10,128,128]{2,1,0:T(8,128)(2,1)S(1)}, u32[]{:S(2)}, u32[]{:S(2)}) collective-permute-start(bf16[10,128,128]{2,1,0:T(8,128)(2,1)S(1)} %copy-done.15), channel_id=1, source_target_pairs={{0,192},{32,224},{64,0},{96,32},{128,64},{160,96},{192,128},{224,1... | collective-permute-start | bytes 983048 | tf_op jit(solution)/shard_map/ppermute | solution.py:297
  66.8 14.6 %collective-permute-start.2 = (bf16[10,128,128]{2,1,0:T(8,128)(2,1)S(1)}, bf16[10,128,128]{2,1,0:T(8,128)(2,1)S(1)}, u32[]{:S(2)}, u32[]{:S(2)}) collective-permute-start(bf16[10,128,128]{2,1,0:T(8,128)(2,1)S(1)} %copy-done.14), channel_id=1, source_target_pairs={{0,64},{32,96},{64,128},{96,160},{128,192},{160,224},{192,0},{224,... | collective-permute-start | bytes 983048 | tf_op jit(solution)/shard_map/ppermute | solution.py:297
  74.5 13.9 %collective-permute-start.1 = (bf16[10,128,128]{2,1,0:T(8,128)(2,1)S(1)}, bf16[10,128,128]{2,1,0:T(8,128)(2,1)S(1)}, u32[]{:S(2)}, u32[]{:S(2)}) collective-permute-start(bf16[10,128,128]{2,1,0:T(8,128)(2,1)S(1)} %add_convert_fusion.1), channel_id=1, source_target_pairs={{0,64},{32,96},{64,128},{96,160},{128,192},{160,224},{192,0},{224,... | collective-permute-start | bytes 983048 | tf_op jit(solution)/shard_map/ppermute | solution.py:297
  74.6 13.8 %collective-permute-start.6 = (bf16[10,128,128]{2,1,0:T(8,128)(2,1)S(1)}, bf16[10,128,128]{2,1,0:T(8,128)(2,1)S(1)}, u32[]{:S(2)}, u32[]{:S(2)}) collective-permute-start(bf16[10,128,128]{2,1,0:T(8,128)(2,1)S(1)} %copy-done.13), channel_id=1, source_target_pairs={{0,192},{32,224},{64,0},{96,32},{128,64},{160,96},{192,128},{224,1... | collective-permute-start | bytes 983048 | tf_op jit(solution)/shard_map/ppermute | solution.py:297
  77.3 14.1 %copy-start.9 = (bf16[10,128,128]{2,1,0:T(8,128)(2,1)S(1)}, bf16[10,128,128]{2,1,0:T(8,128)(2,1)}, u32[]{:S(2)}) copy-start(bf16[10,128,128]{2,1,0:T(8,128)(2,1)} %get-tuple-element.21) | copy-start | bytes 983044
  77.4 13.9 %collective-permute-start.4 = (bf16[10,128,128]{2,1,0:T(8,128)(2,1)S(1)}, bf16[10,128,128]{2,1,0:T(8,128)(2,1)S(1)}, u32[]{:S(2)}, u32[]{:S(2)}) collective-permute-start(bf16[10,128,128]{2,1,0:T(8,128)(2,1)S(1)} %add_convert_fusion), channel_id=1, source_target_pairs={{0,192},{32,224},{64,0},{96,32},{128,64},{160,96},{192,128},{224,1... | collective-permute-start | bytes 983048 | tf_op jit(solution)/shard_map/ppermute | solution.py:297
  88.6 7.5 %collective-permute-start.7 = (bf16[5,128,128]{2,1,0:T(8,128)(2,1)S(1)}, bf16[5,128,128]{2,1,0:T(8,128)(2,1)S(1)}, u32[]{:S(2)}, u32[]{:S(2)}) collective-permute-start(bf16[5,128,128]{2,1,0:T(8,128)(2,1)S(1)} %slice.24), channel_id=1, source_target_pairs={{0,32},{32,0},{64,96},{96,64},{128,160},{160,128},{192,224},{224,1... | collective-permute-start | bytes 491528 | tf_op jit(solution)/shard_map/ppermute | solution.py:297
  91.5 5.6 %copy-start.2 = (bf16[128,1280]{1,0:T(8,128)(2,1)S(1)}, bf16[128,1280]{1,0:T(8,128)(2,1)}, u32[]{:S(2)}) copy-start(bf16[128,1280]{1,0:T(8,128)(2,1)} %patches_ref.3) | copy-start | bytes 983044
  91.5 5.6 %copy-start.3 = (bf16[128,1280]{1,0:T(8,128)(2,1)S(1)}, bf16[128,1280]{1,0:T(8,128)(2,1)}, u32[]{:S(2)}) copy-start(bf16[128,1280]{1,0:T(8,128)(2,1)} %teacher_ref.3) | copy-start | bytes 983044
  91.5 5.6 %copy-start.4 = (s32[128,1]{0,1:T(1,128)S(1)}, s32[128,1]{0,1:T(1,128)}, u32[]{:S(2)}) copy-start(s32[128,1]{0,1:T(1,128)} %param.11) | copy-start | bytes 1540
  91.5 5.6 %copy-start.5 = (bf16[128]{0:T(256)(128)(2,1)S(1)}, bf16[128]{0:T(256)(128)(2,1)}, u32[]{:S(2)}) copy-start(bf16[128]{0:T(256)(128)(2,1)} %param.12) | copy-start | bytes 772
  91.5 9.4 %collective-permute-start.5 = (bf16[5,128,128]{2,1,0:T(8,128)(2,1)S(1)}, bf16[5,128,128]{2,1,0:T(8,128)(2,1)S(1)}, u32[]{:S(2)}, u32[]{:S(2)}) collective-permute-start(bf16[5,128,128]{2,1,0:T(8,128)(2,1)S(1)} %slice.25), channel_id=1, source_target_pairs={{0,32},{32,0},{64,96},{96,64},{128,160},{160,128},{192,224},{224,1... | collective-permute-start | bytes 491528 | tf_op jit(solution)/shard_map/ppermute | solution.py:297

commit v6 on v4

--- a/solution.py
+++ b/solution.py
@@ -11,7 +11,6 @@
 FB = 40
 D = DB * BLK
 SLOT = 8
-UNROLL = 20
 EPS = 1e-06
 GELU_K = 0.7978845608028654
 GELU_C = 0.044715
@@ -50,27 +49,35 @@
 
 
 def pack_kernel(route_ref, gates_ref, patches_ref, teacher_ref, out_hbm, out, sems):
-    def store(second):
-        lanes = pl.ds(second * D, D + second * BLK)
-        return pltpu.make_async_copy(out.at[:, lanes], out_hbm.at[:, lanes], sems.at[second])
+    copies = []
+
+    def store(start, width):
+        lanes = pl.ds(start, width)
+        copy = pltpu.make_async_copy(
+            out.at[:, lanes], out_hbm.at[:, lanes], sems.at[len(copies)]
+        )
+        copy.start()
+        copies.append(copy)
 
     owners = out.shape[0] // SLOT
     place = slot_matrix(route_ref[...], owners)
     one_hot = place.astype(BF16)
-    feats = patches_ref[...].astype(F32)
-    normed, _ = layer_norm(feats)
-    out[:, :D] = dot(one_hot, normed.astype(BF16)).astype(BF16)
-    early = store(0)
-    early.start()
     gates = gates_ref[...].astype(F32)
     gate = jnp.sum(jnp.where(place, gates, 0.0), axis=1, keepdims=True)
     out[:, 2 * D :] = jnp.broadcast_to(gate, (place.shape[0], BLK)).astype(BF16)
+    store(2 * D, BLK)
+    feats = patches_ref[...].astype(F32)
     differ = (feats - teacher_ref[...].astype(F32)).astype(BF16)
-    out[:, D : 2 * D] = (gate * dot(one_hot, differ)).astype(BF16)
-    late = store(1)
-    late.start()
-    early.wait()
-    late.wait()
+    normed, _ = layer_norm(feats)
+    normed = normed.astype(BF16)
+    wide = 2 * BLK
+    for values, scale, base in ((differ, gate, D), (normed, 1.0, 0)):
+        for start in range(0, D, wide):
+            lanes = slice(base + start, base + start + wide)
+            out[:, lanes] = (scale * dot(one_hot, values[:, start : start + wide])).astype(BF16)
+            store(base + start, wide)
+    for copy in copies:
+        copy.wait()
 
 
 def expert_kernel(
@@ -80,13 +87,13 @@
     where_ref,
     pay_hbm,
     w_in_ref,
-    w_out_hbm,
+    w_out_ref,
     ret_hbm,
     *rest,
 ):
-    n_x = (len(rest) - 15) // 2
+    n_x = (len(rest) - 14) // 2
     parts = (rest[:n_x], rest[n_x : 2 * n_x])
-    pay_ref, w_out_ref, ret, xnt, hid, slope, gh, gn, grads, gate, ge, get, load_sem, ret_sems, sems = rest[2 * n_x :]
+    pay_ref, ret, xnt, hid, slope, gh, gn, grads, gate, ge, get, load_sem, ret_sems, sems = rest[2 * n_x :]
     share = FB // n_x
     half = share // 2
     my_x, my_y = where_ref[0], where_ref[1]
@@ -94,10 +101,8 @@
     loads = [
         pltpu.make_async_copy(pay_hbm.at[:, first], pay_ref.at[:, first], load_sem.at[0]),
         pltpu.make_async_copy(pay_hbm.at[:, rest_of], pay_ref.at[:, rest_of], load_sem.at[1]),
-        pltpu.make_async_copy(w_out_hbm, w_out_ref, load_sem.at[2]),
     ]
-    for load in loads:
-        load.start()
+    loads[0].start()
 
     def place(block):
         x = block // share
@@ -111,38 +116,32 @@
         copy.start()
         copies.append(copy)
 
-    def send_rows(kind):
-        lanes = pl.ds((1 - kind) * D, D)
-        send(ret.at[:, lanes], ret_hbm.at[:, lanes], ret_sems.at[kind])
+    def send_rows(start, width, sem):
+        lanes = pl.ds(start, width)
+        send(ret.at[:, lanes], ret_hbm.at[:, lanes], ret_sems.at[sem])
 
     def send_part(kind, x):
         send(grads.at[kind, x], parts[kind][x], sems.at[kind, x])
 
     gn[...] = jnp.zeros_like(gn)
     loads[0].wait()
-    for i in range(DB):
-        xnt[i] = pay_ref[:, i * BLK : (i + 1) * BLK].T
-
-    def forward(step, carry):
-        for q in range(UNROLL):
-            b = step * UNROLL + q
-            c = in_cols[b]
-            lanes = pl.ds(pl.multiple_of(in_rows[b] * BLK, BLK), BLK)
-            v = dot(pay_ref[:, lanes], w_in_ref[b])
-            v2 = v * v
-            t = jnp.tanh(v * (GELU_K + (GELU_K * GELU_C) * v2))
-            half_p = 0.5 + 0.5 * t
-            active = v * half_p
-            hid[c] = active.astype(BF16)
-            slope[c] = half_p + (active - active * half_p) * (
-                2.0 * GELU_K + (6.0 * GELU_K * GELU_C) * v2
-            )
-            gh[c] = jnp.zeros_like(v)
-        return carry
-
-    lax.fori_loop(0, FB // UNROLL, forward, 0)
+    loads[1].start()
+
+    for b in range(FB):
+        c = in_cols[b]
+        lanes = pl.ds(pl.multiple_of(in_rows[b] * BLK, BLK), BLK)
+        v = dot(pay_ref[:, lanes], w_in_ref[b])
+        v2 = v * v
+        t = jnp.tanh(v * (GELU_K + (GELU_K * GELU_C) * v2))
+        half_p = 0.5 + 0.5 * t
+        active = v * half_p
+        hid[c] = active.astype(BF16)
+        slope[c] = half_p + (active - active * half_p) * (
+            2.0 * GELU_K + (6.0 * GELU_K * GELU_C) * v2
+        )
+        gh[c] = jnp.zeros_like(v)
+
     loads[1].wait()
-    loads[2].wait()
     gate[...] = jnp.square(pay_ref[:, 2 * D :].astype(F32))
 
     def read(j):
@@ -155,6 +154,7 @@
         return w_out_ref[K2 * j : K2 * (j + 1)].reshape(K2 * BLK, BLK)
 
     for j in range(DB):
+        xnt[j] = pay_ref[:, j * BLK : (j + 1) * BLK].T
         produced = dot(spread(j), weight(j)).astype(BF16)
         ret[:, j * BLK : (j + 1) * BLK] = produced
         given = pay_ref[:, D + j * BLK : D + (j + 1) * BLK].astype(F32)
@@ -169,7 +169,7 @@
             grads[1, rel_x, pos] = outer[:, k * BLK : (k + 1) * BLK].astype(BF16)
             gh[r] += back[:, k * BLK : (k + 1) * BLK]
 
-    send_rows(1)
+    send_rows(0, D, 0)
     for x in range(n_x):
         send_part(1, x)
 
@@ -187,7 +187,8 @@
         send_part(0, rel_x)
     for i in range(DB):
         ret[:, D + i * BLK : D + (i + 1) * BLK] = gn[i].astype(BF16)
-    send_rows(0)
+        if i % 2:
+            send_rows(D + (i - 1) * BLK, 2 * BLK, 1 + i // 2)
     for copy in copies:
         copy.wait()
 
@@ -244,7 +245,7 @@
         out_specs=HBM_SPEC,
         scratch_shapes=[
             pltpu.VMEM((slots, 2 * D + BLK), BF16),
-            pltpu.SemaphoreType.DMA((2,)),
+            pltpu.SemaphoreType.DMA((11,)),
         ],
         compiler_params=pltpu.CompilerParams(vmem_limit_bytes=60 << 20),
         name="pack",
@@ -263,11 +264,10 @@
     returned, *parts = pl.pallas_call(
         expert_kernel,
         out_shape=(pltpu.HBM((slots, 2 * D), BF16),) + (part,) * (2 * n_x),
-        in_specs=[SMEM_SPEC] * 4 + [HBM_SPEC, VMEM_SPEC, HBM_SPEC],
+        in_specs=[SMEM_SPEC] * 4 + [HBM_SPEC, VMEM_SPEC, VMEM_SPEC],
         out_specs=(HBM_SPEC,) * (1 + 2 * n_x),
         scratch_shapes=[
             pltpu.VMEM((slots, 2 * D + BLK), BF16),
-            pltpu.VMEM((FB, BLK, BLK), BF16),
             pltpu.VMEM((slots, 2 * D), BF16),
             pltpu.VMEM((DB, BLK, slots), BF16),
             pltpu.VMEM((FB, slots, BLK), BF16),
@@ -278,8 +278,8 @@
             pltpu.VMEM((slots, BLK), F32),
             pltpu.VMEM((DB, slots, BLK), BF16),
             pltpu.VMEM((DB, BLK, slots), BF16),
-            pltpu.SemaphoreType.DMA((3,)),
             pltpu.SemaphoreType.DMA((2,)),
+            pltpu.SemaphoreType.DMA((6,)),
             pltpu.SemaphoreType.DMA((2, n_x)),
         ],
         compiler_params=pltpu.CompilerParams(vmem_limit_bytes=51 << 20),

time: 103 us -> 102 us (level)
  no operation moved by 1% of the time
where the time goes in v6:
time: 102 us
  waiting for transfers between devices  59.6 us (58%)
  starting transfers between devices  25.9 us (25%)
  Pallas kernels  14.8 us (15%)
    all_to_all x2, waiting for transfers between devices, exchange(): lax.all_to_all(blocks, 'expert', split_axis=0, concat_axis=0, tiled=True)  38.2 us
    ppermute x8, waiting for transfers between devices, pass_on(): return lax.ppermute(values, 'dp', shift(n_x, dx, dy))  21.4 us
    all_to_all x2, starting transfers between devices, exchange(): lax.all_to_all(blocks, 'expert', split_axis=0, concat_axis=0, tiled=True)  16.8 us
    pallas_call x1, Pallas kernels, local(): pl.pallas_call(expert_kernel, out_shape=(pltpu.HBM((slots, 2 * D), BF16),...  9.36 us
    ppermute x8, starting transfers between devices, pass_on(): return lax.ppermute(values, 'dp', shift(n_x, dx, dy))  9.12 us
    pallas_call x1, Pallas kernels, local(): pl.pallas_call(pack_kernel, out_shape=jax.ShapeDtypeStruct((slots, 2 * D...  2.75 us
  transfers between devices with their start and end apart: 10, of which 6 were waited for; matrix products, arithmetic and copies ran while one was open for 1% of the time, Pallas kernels for 2%

profile of v6, /device:TPU:1, one launch (start us, length us, event | category | flops | bytes accessed | tf_op | source)
XLA Modules:
  0.0 101.9 jit_solution(16387555549066059476)
XLA Ops:
  0.6 2.7 %pack.1 = bf16[256,2688]{1,0:T(8,128)(2,1)} custom-call(s32[1,128]{1,0:T(1,128)} %bitcast.18, bf16[1,128]{1,0:T(2,128)(2,1)} %bitcast.20, bf16[128,1280]{1,0:T(8,128)(2,1)} %patches_ref.3, bf16[128,1280]{1,0:T(8,128)(2,1)} %teacher_ref.3), custom_call_target="tpu_custom_call" | custom-call | tf_op jit(solution)/shard_map/pack/pallas_call | solution.py:241
  3.4 0.0 copy-start
  3.4 0.0 copy-start.1
  3.4 0.0 copy-start.6
  3.4 0.0 copy-start.7
  3.4 0.0 copy-start.8
  3.4 11.3 %all-to-all-start = ((bf16[32,8,2688]{2,1,0:T(8,128)(2,1)}), bf16[32,8,2688]{2,1,0:T(8,128)(2,1)}, u32[]{:S(2)}, u32[]{:S(2)}) async-start(bf16[32,8,2688]{2,1,0:T(8,128)(2,1)} %bitcast.25), calls=%async_computation | async-start | bytes 2752512 | tf_op jit(solution)/shard_map/all_to_all | solution.py:257
  14.8 0.1 pad_add_fusion.where_ref
  14.9 34.1 %all-to-all-done = bf16[32,8,2688]{2,1,0:T(8,128)(2,1)} async-done(((bf16[32,8,2688]{2,1,0:T(8,128)(2,1)}), bf16[32,8,2688]{2,1,0:T(8,128)(2,1)}, u32[]{:S(2)}, u32[]{:S(2)}) %all-to-all-start) | async-done | bytes 1376288 | tf_op jit(solution)/shard_map/all_to_all | solution.py:257
  49.0 0.0 copy-done
  49.0 0.0 copy-done.1
  49.0 0.0 copy-done.6
  49.0 0.0 copy-done.7
  49.0 0.0 copy-done.8
  49.0 9.4 %expert.1 = (bf16[256,2560]{1,0:T(8,128)(2,1)}, bf16[10,128,128]{2,1,0:T(8,128)(2,1)}, bf16[10,128,128]{2,1,0:T(8,128)(2,1)}, bf16[10,128,128]{2,1,0:T(8,128)(2,...) custom-call(s32[40]{0:T(128)S(1)} %bitcast.22, ...), custom_call_target="tpu_custom_call" | custom-call | tf_op jit(solution)/shard_map/expert/pallas_call | solution.py:264
  58.4 0.0 copy-start.14
  58.4 0.0 copy-start.12
  58.4 0.0 copy-start.13
  58.4 0.0 copy-start.11
  58.4 5.5 %all-to-all-start.1 = ((bf16[32,8,2560]{2,1,0:T(8,128)(2,1)}), bf16[32,8,2560]{2,1,0:T(8,128)(2,1)S(1)}, u32[]{:S(2)}, u32[]{:S(2)}) async-start(bf16[32,8,2560]{2,1,0:T(8,128)(2,1)} %bitcast.26), calls=%async_computation.1 | async-start | bytes 2621440 | tf_op jit(solution)/shard_map/all_to_all | solution.py:257
  63.9 0.0 copy-start.10
  63.9 1.3 %collective-permute-start.1 = (bf16[10,128,128]{2,1,0:T(8,128)(2,1)}, bf16[10,128,128]{2,1,0:T(8,128)(2,1)S(1)}, u32[]{:S(2)}, u32[]{:S(2)}) collective-permute-start(bf16[10,128,128]{2,1,0:T(8,128)(2,1)} %get-tuple-element.26), channel_id=1, source_target_pairs={{0,64},{32,96},{64,128},{96,160},{128,192},{160,224},{192,0},{224,... | collective-permute-start | bytes 983048 | tf_op jit(solution)/shard_map/ppermute | solution.py:294
  65.2 1.5 %collective-permute-start.4 = (bf16[10,128,128]{2,1,0:T(8,128)(2,1)S(1)}, bf16[10,128,128]{2,1,0:T(8,128)(2,1)S(1)}, u32[]{:S(2)}, u32[]{:S(2)}) collective-permute-start(bf16[10,128,128]{2,1,0:T(8,128)(2,1)S(1)} %copy-done.14), channel_id=1, source_target_pairs={{0,192},{32,224},{64,0},{96,32},{128,64},{160,96},{192,128},{224,1... | collective-permute-start | bytes 983048 | tf_op jit(solution)/shard_map/ppermute | solution.py:294
  66.7 0.0 collective-permute-start.3
  66.7 7.8 %collective-permute-done.1 = bf16[10,128,128]{2,1,0:T(8,128)(2,1)S(1)} collective-permute-done((bf16[10,128,128]{2,1,0:T(8,128)(2,1)}, bf16[10,128,128]{2,1,0:T(8,128)(2,1)S(1)}, u32[]{:S(2)}, u32[]{:S(2)}) %collective-permute-start.1) | collective-permute-done | bytes 327712 | tf_op jit(solution)/shard_map/ppermute | solution.py:294
  74.5 0.1 add_convert_fusion.1
  74.6 0.1 collective-permute-start.2
  74.7 2.7 %collective-permute-start = (bf16[10,128,128]{2,1,0:T(8,128)(2,1)S(1)}, bf16[10,128,128]{2,1,0:T(8,128)(2,1)S(1)}, u32[]{:S(2)}, u32[]{:S(2)}) collective-permute-start(bf16[10,128,128]{2,1,0:T(8,128)(2,1)S(1)} %copy-done.13), channel_id=1, source_target_pairs={{0,192},{32,224},{64,0},{96,32},{128,64},{160,96},{192,128},{224,1... | collective-permute-start | bytes 983048 | tf_op jit(solution)/shard_map/ppermute | solution.py:294
  77.3 0.0 collective-permute-done.4
  77.4 0.1 add_convert_fusion
  77.5 0.1 collective-permute-start.5
  77.6 3.9 %collective-permute-done.3 = bf16[10,128,128]{2,1,0:T(8,128)(2,1)S(1)} collective-permute-done((bf16[10,128,128]{2,1,0:T(8,128)(2,1)}, bf16[10,128,128]{2,1,0:T(8,128)(2,1)S(1)}, u32[]{:S(2)}, u32[]{:S(2)}) %collective-permute-start.3) | collective-permute-done | bytes 327712 | tf_op jit(solution)/shard_map/ppermute | solution.py:294
  81.5 7.0 %collective-permute-done.2 = bf16[10,128,128]{2,1,0:T(8,128)(2,1)S(1)} collective-permute-done((bf16[10,128,128]{2,1,0:T(8,128)(2,1)S(1)}, bf16[10,128,128]{2,1,0:T(8,128)(2,1)S(1)}, u32[]{:S(2)}, u32[]{:S(2)}) %collective-permute-start.2) | collective-permute-done | bytes 327712 | tf_op jit(solution)/shard_map/ppermute | solution.py:294
  88.5 0.0 collective-permute-done
  88.5 0.1 convert_add_fusion.1
  88.7 2.7 %collective-permute-start.6 = (bf16[5,128,128]{2,1,0:T(8,128)(2,1)S(1)}, bf16[5,128,128]{2,1,0:T(8,128)(2,1)S(1)}, u32[]{:S(2)}, u32[]{:S(2)}) collective-permute-start(bf16[5,128,128]{2,1,0:T(8,128)(2,1)S(1)} %slice.25), channel_id=1, source_target_pairs={{0,32},{32,0},{64,96},{96,64},{128,160},{160,128},{192,224},{224,1... | collective-permute-start | bytes 491528 | tf_op jit(solution)/shard_map/ppermute | solution.py:294
  91.4 0.0 collective-permute-done.5
  91.4 0.0 copy-done.9
  91.4 0.0 copy-start.4
  91.4 0.0 copy-start.5
  91.4 0.1 convert_add_fusion
  91.6 0.8 collective-permute-start.7
  92.4 4.1 %all-to-all-done.1 = bf16[32,8,2560]{2,1,0:T(8,128)(2,1)S(1)} async-done(((bf16[32,8,2560]{2,1,0:T(8,128)(2,1)}), bf16[32,8,2560]{2,1,0:T(8,128)(2,1)S(1)}, u32[]{:S(2)}, u32[]{:S(2)}) %all-to-all-start.1) | async-done | bytes 1310752 | tf_op jit(solution)/shard_map/all_to_all | solution.py:257
  96.6 0.0 copy-done.5
  96.6 1.7 %finish.1 = (bf16[128,1280]{1,0:T(8,128)(2,1)}, f32[128,1280]{1,0:T(8,128)}, f32[8,128]{1,0:T(8,128)S(1)}) custom-call(s32[1,128]{1,0:T(1,128)S(1)} %bitcast.19, bf16[1,128]{1,0:T(2,128)(2,1)S(1)} %bitcast.21, bf16[128,1280]{1,0:T(8,128)(2,1)S(1)} %copy-done.2, bf16[128,1280]{1,0:T(8,128)(2,1)S(1)} %copy-done.3, bf16[256,2560]{1,0:T(8,128)(2,1)S(1)} %bitcast.15), custom_call_target="tpu_custom_call" | custom-call | tf_op jit(solution)/shard_map/finish/pallas_call | solution.py:310
  98.3 0.0 collective-permute-done.6.other_in_ref
  98.3 2.6 %collective-permute-done.7.other_out_ref = bf16[5,128,128]{2,1,0:T(8,128)(2,1)S(1)} collective-permute-done((bf16[5,128,128]{2,1,0:T(8,128)(2,1)S(1)}, bf16[5,128,128]{2,1,0:T(8,128)(2,1)S(1)}, u32[]{:S(2)}, u32[]{:S(2)}) %collective-permute-start.7) | collective-permute-done | bytes 163872 | tf_op jit(solution)/shard_map/ppermute | solution.py:294
  100.9 1.0 total.1
  (15 shorter events, 0.1 us)
Async XLA Ops:
  3.4 45.6 %copy-start = (bf16[1,40,128,128]{3,2,1,0:T(8,128)(2,1)S(1)}, bf16[1,40,128,128]{3,2,1,0:T(8,128)(2,1)}, u32[]{:S(2)}) copy-start(bf16[1,40,128,128]{3,2,1,0:T(8,128)(2,1)} %param.13) | copy-start | bytes 3932164
  3.4 45.6 %copy-start.1 = (bf16[1,40,128,128]{3,2,1,0:T(8,128)(2,1)S(1)}, bf16[1,40,128,128]{3,2,1,0:T(8,128)(2,1)}, u32[]{:S(2)}) copy-start(bf16[1,40,128,128]{3,2,1,0:T(8,128)(2,1)} %param.16) | copy-start | bytes 3932164
  3.4 45.6 %copy-start.6 = (s32[1,40]{1,0:T(1,128)S(1)}, s32[1,40]{1,0:T(1,128)}, u32[]{:S(2)}) copy-start(s32[1,40]{1,0:T(1,128)} %param.14) | copy-start | bytes 484
  3.4 45.6 %copy-start.7 = (s32[1,40]{1,0:T(1,128)S(1)}, s32[1,40]{1,0:T(1,128)}, u32[]{:S(2)}) copy-start(s32[1,40]{1,0:T(1,128)} %param.15) | copy-start | bytes 484
  3.4 45.6 %copy-start.8 = (s32[1,40]{1,0:T(1,128)S(1)}, s32[1,40]{1,0:T(1,128)}, u32[]{:S(2)}) copy-start(s32[1,40]{1,0:T(1,128)} %param.17) | copy-start | bytes 484
  3.4 45.5 %all-to-all-start = ((bf16[32,8,2688]{2,1,0:T(8,128)(2,1)}), bf16[32,8,2688]{2,1,0:T(8,128)(2,1)}, u32[]{:S(2)}, u32[]{:S(2)}) async-start(bf16[32,8,2688]{2,1,0:T(8,128)(2,1)} %bitcast.25), calls=%async_computation | async-start | bytes 2752512 | tf_op jit(solution)/shard_map/all_to_all | solution.py:257
  58.4 6.8 %copy-start.14 = (bf16[10,128,128]{2,1,0:T(8,128)(2,1)S(1)}, bf16[10,128,128]{2,1,0:T(8,128)(2,1)}, u32[]{:S(2)}) copy-start(bf16[10,128,128]{2,1,0:T(8,128)(2,1)} %get-tuple-element.32) | copy-start | bytes 983044
  58.4 16.1 %copy-start.12 = (bf16[10,128,128]{2,1,0:T(8,128)(2,1)S(1)}, bf16[10,128,128]{2,1,0:T(8,128)(2,1)}, u32[]{:S(2)}) copy-start(bf16[10,128,128]{2,1,0:T(8,128)(2,1)} %get-tuple-element.25) | copy-start | bytes 983044
  58.4 16.3 %copy-start.13 = (bf16[10,128,128]{2,1,0:T(8,128)(2,1)S(1)}, bf16[10,128,128]{2,1,0:T(8,128)(2,1)}, u32[]{:S(2)}) copy-start(bf16[10,128,128]{2,1,0:T(8,128)(2,1)} %get-tuple-element.24) | copy-start | bytes 983044
  58.4 19.0 %copy-start.11 = (bf16[10,128,128]{2,1,0:T(8,128)(2,1)S(1)}, bf16[10,128,128]{2,1,0:T(8,128)(2,1)}, u32[]{:S(2)}) copy-start(bf16[10,128,128]{2,1,0:T(8,128)(2,1)} %get-tuple-element.31) | copy-start | bytes 983044
  58.4 38.1 %all-to-all-start.1 = ((bf16[32,8,2560]{2,1,0:T(8,128)(2,1)}), bf16[32,8,2560]{2,1,0:T(8,128)(2,1)S(1)}, u32[]{:S(2)}, u32[]{:S(2)}) async-start(bf16[32,8,2560]{2,1,0:T(8,128)(2,1)} %bitcast.26), calls=%async_computation.1 | async-start | bytes 2621440 | tf_op jit(solution)/shard_map/all_to_all | solution.py:257
  63.9 24.6 %copy-start.10 = (bf16[10,128,128]{2,1,0:T(8,128)(2,1)S(1)}, bf16[10,128,128]{2,1,0:T(8,128)(2,1)}, u32[]{:S(2)}) copy-start(bf16[10,128,128]{2,1,0:T(8,128)(2,1)} %get-tuple-element.23) | copy-start | bytes 983044
  63.9 10.6 %collective-permute-start.1 = (bf16[10,128,128]{2,1,0:T(8,128)(2,1)}, bf16[10,128,128]{2,1,0:T(8,128)(2,1)S(1)}, u32[]{:S(2)}, u32[]{:S(2)}) collective-permute-start(bf16[10,128,128]{2,1,0:T(8,128)(2,1)} %get-tuple-element.26), channel_id=1, source_target_pairs={{0,64},{32,96},{64,128},{96,160},{128,192},{160,224},{192,0},{224,... | collective-permute-start | bytes 983048 | tf_op jit(solution)/shard_map/ppermute | solution.py:294
  65.2 12.2 %collective-permute-start.4 = (bf16[10,128,128]{2,1,0:T(8,128)(2,1)S(1)}, bf16[10,128,128]{2,1,0:T(8,128)(2,1)S(1)}, u32[]{:S(2)}, u32[]{:S(2)}) collective-permute-start(bf16[10,128,128]{2,1,0:T(8,128)(2,1)S(1)} %copy-done.14), channel_id=1, source_target_pairs={{0,192},{32,224},{64,0},{96,32},{128,64},{160,96},{192,128},{224,1... | collective-permute-start | bytes 983048 | tf_op jit(solution)/shard_map/ppermute | solution.py:294
  66.7 14.8 %collective-permute-start.3 = (bf16[10,128,128]{2,1,0:T(8,128)(2,1)}, bf16[10,128,128]{2,1,0:T(8,128)(2,1)S(1)}, u32[]{:S(2)}, u32[]{:S(2)}) collective-permute-start(bf16[10,128,128]{2,1,0:T(8,128)(2,1)} %get-tuple-element.27), channel_id=1, source_target_pairs={{0,64},{32,96},{64,128},{96,160},{128,192},{160,224},{192,0},{224,... | collective-permute-start | bytes 983048 | tf_op jit(solution)/shard_map/ppermute | solution.py:294
  74.6 13.9 %collective-permute-start.2 = (bf16[10,128,128]{2,1,0:T(8,128)(2,1)S(1)}, bf16[10,128,128]{2,1,0:T(8,128)(2,1)S(1)}, u32[]{:S(2)}, u32[]{:S(2)}) collective-permute-start(bf16[10,128,128]{2,1,0:T(8,128)(2,1)S(1)} %add_convert_fusion.1), channel_id=1, source_target_pairs={{0,64},{32,96},{64,128},{96,160},{128,192},{160,224},{192,0},{224,... | collective-permute-start | bytes 983048 | tf_op jit(solution)/shard_map/ppermute | solution.py:294
  74.7 13.8 %collective-permute-start = (bf16[10,128,128]{2,1,0:T(8,128)(2,1)S(1)}, bf16[10,128,128]{2,1,0:T(8,128)(2,1)S(1)}, u32[]{:S(2)}, u32[]{:S(2)}) collective-permute-start(bf16[10,128,128]{2,1,0:T(8,128)(2,1)S(1)} %copy-done.13), channel_id=1, source_target_pairs={{0,192},{32,224},{64,0},{96,32},{128,64},{160,96},{192,128},{224,1... | collective-permute-start | bytes 983048 | tf_op jit(solution)/shard_map/ppermute | solution.py:294
  77.4 14.0 %copy-start.9 = (bf16[10,128,128]{2,1,0:T(8,128)(2,1)S(1)}, bf16[10,128,128]{2,1,0:T(8,128)(2,1)}, u32[]{:S(2)}) copy-start(bf16[10,128,128]{2,1,0:T(8,128)(2,1)} %get-tuple-element.29) | copy-start | bytes 983044
  77.5 13.9 %collective-permute-start.5 = (bf16[10,128,128]{2,1,0:T(8,128)(2,1)S(1)}, bf16[10,128,128]{2,1,0:T(8,128)(2,1)S(1)}, u32[]{:S(2)}, u32[]{:S(2)}) collective-permute-start(bf16[10,128,128]{2,1,0:T(8,128)(2,1)S(1)} %add_convert_fusion), channel_id=1, source_target_pairs={{0,192},{32,224},{64,0},{96,32},{128,64},{160,96},{192,128},{224,1... | collective-permute-start | bytes 983048 | tf_op jit(solution)/shard_map/ppermute | solution.py:294
  88.7 9.6 %collective-permute-start.6 = (bf16[5,128,128]{2,1,0:T(8,128)(2,1)S(1)}, bf16[5,128,128]{2,1,0:T(8,128)(2,1)S(1)}, u32[]{:S(2)}, u32[]{:S(2)}) collective-permute-start(bf16[5,128,128]{2,1,0:T(8,128)(2,1)S(1)} %slice.25), channel_id=1, source_target_pairs={{0,32},{32,0},{64,96},{96,64},{128,160},{160,128},{192,224},{224,1... | collective-permute-start | bytes 491528 | tf_op jit(solution)/shard_map/ppermute | solution.py:294
  91.4 5.1 %copy-start.2 = (bf16[128,1280]{1,0:T(8,128)(2,1)S(1)}, bf16[128,1280]{1,0:T(8,128)(2,1)}, u32[]{:S(2)}) copy-start(bf16[128,1280]{1,0:T(8,128)(2,1)} %patches_ref.3) | copy-start | bytes 983044
  91.4 5.1 %copy-start.3 = (bf16[128,1280]{1,0:T(8,128)(2,1)S(1)}, bf16[128,1280]{1,0:T(8,128)(2,1)}, u32[]{:S(2)}) copy-start(bf16[128,1280]{1,0:T(8,128)(2,1)} %teacher_ref.3) | copy-start | bytes 983044
  91.4 5.1 %copy-start.4 = (s32[128,1]{0,1:T(1,128)S(1)}, s32[128,1]{0,1:T(1,128)}, u32[]{:S(2)}) copy-start(s32[128,1]{0,1:T(1,128)} %param.11) | copy-start | bytes 1540
  91.4 5.1 %copy-start.5 = (bf16[128]{0:T(256)(128)(2,1)S(1)}, bf16[128]{0:T(256)(128)(2,1)}, u32[]{:S(2)}) copy-start(bf16[128]{0:T(256)(128)(2,1)} %param.12) | copy-start | bytes 772
  91.6 9.3 %collective-permute-start.7 = (bf16[5,128,128]{2,1,0:T(8,128)(2,1)S(1)}, bf16[5,128,128]{2,1,0:T(8,128)(2,1)S(1)}, u32[]{:S(2)}, u32[]{:S(2)}) collective-permute-start(bf16[5,128,128]{2,1,0:T(8,128)(2,1)S(1)} %slice.24), channel_id=1, source_target_pairs={{0,32},{32,0},{64,96},{96,64},{128,160},{160,128},{192,224},{224,1... | collective-permute-start | bytes 491528 | tf_op jit(solution)/shard_map/ppermute | solution.py:294

commit v7 on v6

--- a/solution.py
+++ b/solution.py
@@ -85,24 +85,18 @@
     in_cols,
     out_rows,
     where_ref,
-    pay_hbm,
+    pay_ref,
     w_in_ref,
     w_out_ref,
     ret_hbm,
     *rest,
 ):
-    n_x = (len(rest) - 14) // 2
+    n_x = (len(rest) - 12) // 2
     parts = (rest[:n_x], rest[n_x : 2 * n_x])
-    pay_ref, ret, xnt, hid, slope, gh, gn, grads, gate, ge, get, load_sem, ret_sems, sems = rest[2 * n_x :]
+    ret, xnt, hid, slope, gh, gn, grads, gate, ge, get, ret_sems, sems = rest[2 * n_x :]
     share = FB // n_x
     half = share // 2
     my_x, my_y = where_ref[0], where_ref[1]
-    first, rest_of = pl.ds(0, D), pl.ds(D, D + BLK)
-    loads = [
-        pltpu.make_async_copy(pay_hbm.at[:, first], pay_ref.at[:, first], load_sem.at[0]),
-        pltpu.make_async_copy(pay_hbm.at[:, rest_of], pay_ref.at[:, rest_of], load_sem.at[1]),
-    ]
-    loads[0].start()
 
     def place(block):
         x = block // share
@@ -124,8 +118,6 @@
         send(grads.at[kind, x], parts[kind][x], sems.at[kind, x])
 
     gn[...] = jnp.zeros_like(gn)
-    loads[0].wait()
-    loads[1].start()
 
     for b in range(FB):
         c = in_cols[b]
@@ -141,7 +133,6 @@
         )
         gh[c] = jnp.zeros_like(v)
 
-    loads[1].wait()
     gate[...] = jnp.square(pay_ref[:, 2 * D :].astype(F32))
 
     def read(j):
@@ -191,6 +182,11 @@
             send_rows(D + (i - 1) * BLK, 2 * BLK, 1 + i // 2)
     for copy in copies:
         copy.wait()
+
+
+def stage_kernel(w_in_ref, w_out_ref, in_ref, out_ref):
+    in_ref[...] = w_in_ref[...]
+    out_ref[...] = w_out_ref[...]
 
 
 def finish_kernel(route_ref, gates_ref, patches_ref, teacher_ref, ret_ref, student_ref, grad_ref, corner_ref):
@@ -258,16 +254,24 @@
         return out.reshape(slots, width)
 
     arrived = exchange(payload)
+    blocks = jax.ShapeDtypeStruct((FB, BLK, BLK), BF16)
+    staged_in, staged_out = pl.pallas_call(
+        stage_kernel,
+        out_shape=(blocks, blocks),
+        in_specs=[VMEM_SPEC] * 2,
+        out_specs=(VMEM_SPEC, VMEM_SPEC),
+        compiler_params=pltpu.CompilerParams(vmem_limit_bytes=16 << 20),
+        name="stage",
+    )(w_in[0], w_out[0])
     me = lax.axis_index("dp")
     where = jnp.stack([me // 2, me % 2]).astype(jnp.int32)
     part = pltpu.HBM((share, BLK, BLK), BF16)
     returned, *parts = pl.pallas_call(
         expert_kernel,
         out_shape=(pltpu.HBM((slots, 2 * D), BF16),) + (part,) * (2 * n_x),
-        in_specs=[SMEM_SPEC] * 4 + [HBM_SPEC, VMEM_SPEC, VMEM_SPEC],
+        in_specs=[SMEM_SPEC] * 4 + [VMEM_SPEC] * 3,
         out_specs=(HBM_SPEC,) * (1 + 2 * n_x),
         scratch_shapes=[
-            pltpu.VMEM((slots, 2 * D + BLK), BF16),
             pltpu.VMEM((slots, 2 * D), BF16),
             pltpu.VMEM((DB, BLK, slots), BF16),
             pltpu.VMEM((FB, slots, BLK), BF16),
@@ -278,13 +282,12 @@
             pltpu.VMEM((slots, BLK), F32),
             pltpu.VMEM((DB, slots, BLK), BF16),
             pltpu.VMEM((DB, BLK, slots), BF16),
-            pltpu.SemaphoreType.DMA((2,)),
             pltpu.SemaphoreType.DMA((6,)),
             pltpu.SemaphoreType.DMA((2, n_x)),
         ],
-        compiler_params=pltpu.CompilerParams(vmem_limit_bytes=51 << 20),
+        compiler_params=pltpu.CompilerParams(vmem_limit_bytes=30 << 20),
         name="expert",
-    )(in_rows[0], in_cols[0], out_rows[0], where, arrived, w_in[0], w_out[0])
+    )(in_rows[0], in_cols[0], out_rows[0], where, arrived, staged_in, staged_out)
     part_in, part_out = parts[:n_x], parts[n_x:]
 
     back = exchange(returned)

time: 102 us -> 103 us (level)
  local copies, waits for them, and re-layouts: 0.18 us -> 5.16 us
  waiting for transfers between devices: 59.6 us -> 55.4 us
    unnamed x30 -> x34, local copies, waits for them, and re-layouts: 0.08 us -> 5.07 us
    all_to_all x2, waiting for transfers between devices: 38.2 us -> 34.2 us  [exchange(): lax.all_to_all(blocks, 'expert', split_axis=0, concat_axis=0, tiled=True)]
where the time goes in v7:
time: 103 us; the launch traced here: 102 us
  waiting for transfers between devices  55.4 us (54%)
  starting transfers between devices  26 us (25%)
  Pallas kernels  14.3 us (14%)
  local copies, waits for them, and re-layouts  5.16 us (5%)
    all_to_all x2, waiting for transfers between devices, exchange(): lax.all_to_all(blocks, 'expert', split_axis=0, concat_axis=0, tiled=True)  34.2 us
    ppermute x8, waiting for transfers between devices, pass_on(): return lax.ppermute(values, 'dp', shift(n_x, dx, dy))  21.2 us
    all_to_all x2, starting transfers between devices, exchange(): lax.all_to_all(blocks, 'expert', split_axis=0, concat_axis=0, tiled=True)  16.6 us
    ppermute x8, starting transfers between devices, pass_on(): return lax.ppermute(values, 'dp', shift(n_x, dx, dy))  9.4 us
    pallas_call x1, Pallas kernels, local(): pl.pallas_call(expert_kernel, out_shape=(pltpu.HBM((slots, 2 * D), BF16),...  8.71 us
    unnamed x34, local copies, waits for them, and re-layouts  5.07 us
    pallas_call x1, Pallas kernels, local(): pl.pallas_call(pack_kernel, out_shape=jax.ShapeDtypeStruct((slots, 2 * D...  2.7 us
  transfers between devices with their start and end apart: 10, of which 6 were waited for; matrix products, arithmetic and copies ran while one was open for 1% of the time, Pallas kernels for 2%

profile of v7, /device:TPU:1, one launch (start us, length us, event | category | flops | bytes accessed | tf_op | source)
XLA Modules:
  0.0 102.2 jit_solution(12034793361093386334)
XLA Ops:
  0.6 2.7 %pack.1 = bf16[256,2688]{1,0:T(8,128)(2,1)} custom-call(s32[1,128]{1,0:T(1,128)} %bitcast.19, bf16[1,128]{1,0:T(2,128)(2,1)} %bitcast.21, bf16[128,1280]{1,0:T(8,128)(2,1)} %patches_ref.3, bf16[128,1280]{1,0:T(8,128)(2,1)} %teacher_ref.3), custom_call_target="tpu_custom_call" | custom-call | tf_op jit(solution)/shard_map/pack/pallas_call | solution.py:237
  3.3 11.1 %all-to-all-start = ((bf16[32,8,2688]{2,1,0:T(8,128)(2,1)}), bf16[32,8,2688]{2,1,0:T(8,128)(2,1)S(1)}, u32[]{:S(2)}, u32[]{:S(2)}) async-start(bf16[32,8,2688]{2,1,0:T(8,128)(2,1)} %bitcast.26), calls=%async_computation | async-start | bytes 2752512 | tf_op jit(solution)/shard_map/all_to_all | solution.py:253
  14.5 0.0 copy-start.4
  14.5 1.3 %copy-done.4 = bf16[1,40,128,128]{3,2,1,0:T(8,128)(2,1)S(1)} copy-done((bf16[1,40,128,128]{3,2,1,0:T(8,128)(2,1)S(1)}, bf16[1,40,128,128]{3,2,1,0:T(8,128)(2,1)}, u32[]{:S(2)}) %copy-start.4) | copy-done | bytes 1310744
  15.8 1.3 %copy-done.5 = bf16[1,40,128,128]{3,2,1,0:T(8,128)(2,1)S(1)} copy-done((bf16[1,40,128,128]{3,2,1,0:T(8,128)(2,1)S(1)}, bf16[1,40,128,128]{3,2,1,0:T(8,128)(2,1)}, u32[]{:S(2)}) %copy-start.5) | copy-done | bytes 1310744
  17.2 0.2 stage.1
  17.3 0.0 copy-start
  17.3 1.1 %copy-done = bf16[40,128,128]{2,1,0:T(8,128)(2,1)} copy-done((bf16[40,128,128]{2,1,0:T(8,128)(2,1)}, bf16[40,128,128]{2,1,0:T(8,128)(2,1)S(1)}, u32[]{:S(2)}) %copy-start) | copy-done | bytes 1310744
  18.4 0.1 pad_add_fusion.where_ref
  18.5 30.1 %all-to-all-done = bf16[32,8,2688]{2,1,0:T(8,128)(2,1)S(1)} async-done(((bf16[32,8,2688]{2,1,0:T(8,128)(2,1)}), bf16[32,8,2688]{2,1,0:T(8,128)(2,1)S(1)}, u32[]{:S(2)}, u32[]{:S(2)}) %all-to-all-start) | async-done | bytes 1376288 | tf_op jit(solution)/shard_map/all_to_all | solution.py:253
  48.6 0.0 copy-done.8
  48.6 0.0 copy-done.9
  48.6 0.0 copy-done.10
  48.6 0.0 copy-start.1
  48.6 1.3 %copy-done.1 = bf16[40,128,128]{2,1,0:T(8,128)(2,1)S(1)} copy-done((bf16[40,128,128]{2,1,0:T(8,128)(2,1)S(1)}, bf16[40,128,128]{2,1,0:T(8,128)(2,1)}, u32[]{:S(2)}) %copy-start.1) | copy-done | bytes 1310744
  49.9 8.7 %expert.1 = (bf16[256,2560]{1,0:T(8,128)(2,1)}, bf16[10,128,128]{2,1,0:T(8,128)(2,1)}, bf16[10,128,128]{2,1,0:T(8,128)(2,1)}, bf16[10,128,128]{2,1,0:T(8,128)(2,...) custom-call(s32[40]{0:T(128)S(1)} %bitcast.23, ...), custom_call_target="tpu_custom_call" | custom-call | tf_op jit(solution)/shard_map/expert/pallas_call | solution.py:269
  58.7 0.0 copy-start.16
  58.7 0.0 copy-start.14
  58.7 0.0 copy-start.15
  58.7 5.5 %all-to-all-start.1 = ((bf16[32,8,2560]{2,1,0:T(8,128)(2,1)}), bf16[32,8,2560]{2,1,0:T(8,128)(2,1)S(1)}, u32[]{:S(2)}, u32[]{:S(2)}) async-start(bf16[32,8,2560]{2,1,0:T(8,128)(2,1)} %bitcast.27), calls=%async_computation.1 | async-start | bytes 2621440 | tf_op jit(solution)/shard_map/all_to_all | solution.py:253
  64.2 0.0 copy-start.12
  64.2 1.3 %collective-permute-start.1 = (bf16[10,128,128]{2,1,0:T(8,128)(2,1)}, bf16[10,128,128]{2,1,0:T(8,128)(2,1)S(1)}, u32[]{:S(2)}, u32[]{:S(2)}) collective-permute-start(bf16[10,128,128]{2,1,0:T(8,128)(2,1)} %get-tuple-element.30), channel_id=1, source_target_pairs={{0,64},{32,96},{64,128},{96,160},{128,192},{160,224},{192,0},{224,... | collective-permute-start | bytes 983048 | tf_op jit(solution)/shard_map/ppermute | solution.py:297
  65.5 1.5 %collective-permute-start.4 = (bf16[10,128,128]{2,1,0:T(8,128)(2,1)S(1)}, bf16[10,128,128]{2,1,0:T(8,128)(2,1)S(1)}, u32[]{:S(2)}, u32[]{:S(2)}) collective-permute-start(bf16[10,128,128]{2,1,0:T(8,128)(2,1)S(1)} %copy-done.16), channel_id=1, source_target_pairs={{0,192},{32,224},{64,0},{96,32},{128,64},{160,96},{192,128},{224,1... | collective-permute-start | bytes 983048 | tf_op jit(solution)/shard_map/ppermute | solution.py:297
  67.0 0.0 collective-permute-start.3
  67.0 7.8 %collective-permute-done.1 = bf16[10,128,128]{2,1,0:T(8,128)(2,1)S(1)} collective-permute-done((bf16[10,128,128]{2,1,0:T(8,128)(2,1)}, bf16[10,128,128]{2,1,0:T(8,128)(2,1)S(1)}, u32[]{:S(2)}, u32[]{:S(2)}) %collective-permute-start.1) | collective-permute-done | bytes 327712 | tf_op jit(solution)/shard_map/ppermute | solution.py:297
  74.8 0.1 add_convert_fusion.1
  74.9 0.3 collective-permute-start.2
  75.2 2.7 %collective-permute-start = (bf16[10,128,128]{2,1,0:T(8,128)(2,1)S(1)}, bf16[10,128,128]{2,1,0:T(8,128)(2,1)S(1)}, u32[]{:S(2)}, u32[]{:S(2)}) collective-permute-start(bf16[10,128,128]{2,1,0:T(8,128)(2,1)S(1)} %copy-done.15), channel_id=1, source_target_pairs={{0,192},{32,224},{64,0},{96,32},{128,64},{160,96},{192,128},{224,1... | collective-permute-start | bytes 983048 | tf_op jit(solution)/shard_map/ppermute | solution.py:297
  77.8 0.0 collective-permute-done.4
  77.8 0.1 add_convert_fusion
  77.9 0.1 collective-permute-start.5
  78.1 3.7 %collective-permute-done.3 = bf16[10,128,128]{2,1,0:T(8,128)(2,1)S(1)} collective-permute-done((bf16[10,128,128]{2,1,0:T(8,128)(2,1)}, bf16[10,128,128]{2,1,0:T(8,128)(2,1)S(1)}, u32[]{:S(2)}, u32[]{:S(2)}) %collective-permute-start.3) | collective-permute-done | bytes 327712 | tf_op jit(solution)/shard_map/ppermute | solution.py:297
  81.8 7.0 %collective-permute-done.2 = bf16[10,128,128]{2,1,0:T(8,128)(2,1)S(1)} collective-permute-done((bf16[10,128,128]{2,1,0:T(8,128)(2,1)S(1)}, bf16[10,128,128]{2,1,0:T(8,128)(2,1)S(1)}, u32[]{:S(2)}, u32[]{:S(2)}) %collective-permute-start.2) | collective-permute-done | bytes 327712 | tf_op jit(solution)/shard_map/ppermute | solution.py:297
  88.8 0.0 collective-permute-done
  88.8 0.1 convert_add_fusion.1
  89.0 2.7 %collective-permute-start.6 = (bf16[5,128,128]{2,1,0:T(8,128)(2,1)S(1)}, bf16[5,128,128]{2,1,0:T(8,128)(2,1)S(1)}, u32[]{:S(2)}, u32[]{:S(2)}) collective-permute-start(bf16[5,128,128]{2,1,0:T(8,128)(2,1)S(1)} %slice.25), channel_id=1, source_target_pairs={{0,32},{32,0},{64,96},{96,64},{128,160},{160,128},{192,224},{224,1... | collective-permute-start | bytes 491528 | tf_op jit(solution)/shard_map/ppermute | solution.py:297
  91.7 0.0 collective-permute-done.5
  91.7 0.0 copy-done.11
  91.7 0.0 copy-start.6
  91.7 0.0 copy-start.7
  91.7 0.1 convert_add_fusion
  91.9 0.9 collective-permute-start.7
  92.8 4.0 %all-to-all-done.1 = bf16[32,8,2560]{2,1,0:T(8,128)(2,1)S(1)} async-done(((bf16[32,8,2560]{2,1,0:T(8,128)(2,1)}), bf16[32,8,2560]{2,1,0:T(8,128)(2,1)S(1)}, u32[]{:S(2)}, u32[]{:S(2)}) %all-to-all-start.1) | async-done | bytes 1310752 | tf_op jit(solution)/shard_map/all_to_all | solution.py:253
  96.9 0.0 copy-done.7
  96.9 1.7 %finish.1 = (bf16[128,1280]{1,0:T(8,128)(2,1)}, f32[128,1280]{1,0:T(8,128)}, f32[8,128]{1,0:T(8,128)S(1)}) custom-call(s32[1,128]{1,0:T(1,128)S(1)} %bitcast.20, bf16[1,128]{1,0:T(2,128)(2,1)S(1)} %bitcast.22, bf16[128,1280]{1,0:T(8,128)(2,1)S(1)} %copy-done.2, bf16[128,1280]{1,0:T(8,128)(2,1)S(1)} %copy-done.3, bf16[256,2560]{1,0:T(8,128)(2,1)S(1)} %bitcast.16), custom_call_target="tpu_custom_call" | custom-call | tf_op jit(solution)/shard_map/finish/pallas_call | solution.py:313
  98.6 0.0 collective-permute-done.6.other_in_ref
  98.6 2.6 %collective-permute-done.7.other_out_ref = bf16[5,128,128]{2,1,0:T(8,128)(2,1)S(1)} collective-permute-done((bf16[5,128,128]{2,1,0:T(8,128)(2,1)S(1)}, bf16[5,128,128]{2,1,0:T(8,128)(2,1)S(1)}, u32[]{:S(2)}, u32[]{:S(2)}) %collective-permute-start.7) | collective-permute-done | bytes 163872 | tf_op jit(solution)/shard_map/ppermute | solution.py:297
  101.2 1.0 total.1
  (20 shorter events, 0.1 us)
Async XLA Ops:
  3.3 45.3 %all-to-all-start = ((bf16[32,8,2688]{2,1,0:T(8,128)(2,1)}), bf16[32,8,2688]{2,1,0:T(8,128)(2,1)S(1)}, u32[]{:S(2)}, u32[]{:S(2)}) async-start(bf16[32,8,2688]{2,1,0:T(8,128)(2,1)} %bitcast.26), calls=%async_computation | async-start | bytes 2752512 | tf_op jit(solution)/shard_map/all_to_all | solution.py:253
  14.5 1.3 %copy-start.4 = (bf16[1,40,128,128]{3,2,1,0:T(8,128)(2,1)S(1)}, bf16[1,40,128,128]{3,2,1,0:T(8,128)(2,1)}, u32[]{:S(2)}) copy-start(bf16[1,40,128,128]{3,2,1,0:T(8,128)(2,1)} %param.13) | copy-start | bytes 3932164
  15.8 1.3 %copy-start.5 = (bf16[1,40,128,128]{3,2,1,0:T(8,128)(2,1)S(1)}, bf16[1,40,128,128]{3,2,1,0:T(8,128)(2,1)}, u32[]{:S(2)}) copy-start(bf16[1,40,128,128]{3,2,1,0:T(8,128)(2,1)} %param.16) | copy-start | bytes 3932164
  17.1 31.5 %copy-start.8 = (s32[1,40]{1,0:T(1,128)S(1)}, s32[1,40]{1,0:T(1,128)}, u32[]{:S(2)}) copy-start(s32[1,40]{1,0:T(1,128)} %param.14) | copy-start | bytes 484
  17.1 31.5 %copy-start.9 = (s32[1,40]{1,0:T(1,128)S(1)}, s32[1,40]{1,0:T(1,128)}, u32[]{:S(2)}) copy-start(s32[1,40]{1,0:T(1,128)} %param.15) | copy-start | bytes 484
  17.1 31.5 %copy-start.10 = (s32[1,40]{1,0:T(1,128)S(1)}, s32[1,40]{1,0:T(1,128)}, u32[]{:S(2)}) copy-start(s32[1,40]{1,0:T(1,128)} %param.17) | copy-start | bytes 484
  17.3 1.1 %copy-start = (bf16[40,128,128]{2,1,0:T(8,128)(2,1)}, bf16[40,128,128]{2,1,0:T(8,128)(2,1)S(1)}, u32[]{:S(2)}) copy-start(bf16[40,128,128]{2,1,0:T(8,128)(2,1)S(1)} %get-tuple-element.23.w_out_ref) | copy-start | bytes 3932164
  48.6 1.3 %copy-start.1 = (bf16[40,128,128]{2,1,0:T(8,128)(2,1)S(1)}, bf16[40,128,128]{2,1,0:T(8,128)(2,1)}, u32[]{:S(2)}) copy-start(bf16[40,128,128]{2,1,0:T(8,128)(2,1)} %copy-done) | copy-start | bytes 3932164
  58.7 6.8 %copy-start.16 = (bf16[10,128,128]{2,1,0:T(8,128)(2,1)S(1)}, bf16[10,128,128]{2,1,0:T(8,128)(2,1)}, u32[]{:S(2)}) copy-start(bf16[10,128,128]{2,1,0:T(8,128)(2,1)} %get-tuple-element.36) | copy-start | bytes 983044
  58.7 16.1 %copy-start.14 = (bf16[10,128,128]{2,1,0:T(8,128)(2,1)S(1)}, bf16[10,128,128]{2,1,0:T(8,128)(2,1)}, u32[]{:S(2)}) copy-start(bf16[10,128,128]{2,1,0:T(8,128)(2,1)} %get-tuple-element.29) | copy-start | bytes 983044
  58.7 16.5 %copy-start.15 = (bf16[10,128,128]{2,1,0:T(8,128)(2,1)S(1)}, bf16[10,128,128]{2,1,0:T(8,128)(2,1)}, u32[]{:S(2)}) copy-start(bf16[10,128,128]{2,1,0:T(8,128)(2,1)} %get-tuple-element.28) | copy-start | bytes 983044
  58.7 19.1 %copy-start.13 = (bf16[10,128,128]{2,1,0:T(8,128)(2,1)S(1)}, bf16[10,128,128]{2,1,0:T(8,128)(2,1)}, u32[]{:S(2)}) copy-start(bf16[10,128,128]{2,1,0:T(8,128)(2,1)} %get-tuple-element.35) | copy-start | bytes 983044
  58.7 38.1 %all-to-all-start.1 = ((bf16[32,8,2560]{2,1,0:T(8,128)(2,1)}), bf16[32,8,2560]{2,1,0:T(8,128)(2,1)S(1)}, u32[]{:S(2)}, u32[]{:S(2)}) async-start(bf16[32,8,2560]{2,1,0:T(8,128)(2,1)} %bitcast.27), calls=%async_computation.1 | async-start | bytes 2621440 | tf_op jit(solution)/shard_map/all_to_all | solution.py:253
  64.2 24.6 %copy-start.12 = (bf16[10,128,128]{2,1,0:T(8,128)(2,1)S(1)}, bf16[10,128,128]{2,1,0:T(8,128)(2,1)}, u32[]{:S(2)}) copy-start(bf16[10,128,128]{2,1,0:T(8,128)(2,1)} %get-tuple-element.27) | copy-start | bytes 983044
  64.2 10.6 %collective-permute-start.1 = (bf16[10,128,128]{2,1,0:T(8,128)(2,1)}, bf16[10,128,128]{2,1,0:T(8,128)(2,1)S(1)}, u32[]{:S(2)}, u32[]{:S(2)}) collective-permute-start(bf16[10,128,128]{2,1,0:T(8,128)(2,1)} %get-tuple-element.30), channel_id=1, source_target_pairs={{0,64},{32,96},{64,128},{96,160},{128,192},{160,224},{192,0},{224,... | collective-permute-start | bytes 983048 | tf_op jit(solution)/shard_map/ppermute | solution.py:297
  65.5 12.3 %collective-permute-start.4 = (bf16[10,128,128]{2,1,0:T(8,128)(2,1)S(1)}, bf16[10,128,128]{2,1,0:T(8,128)(2,1)S(1)}, u32[]{:S(2)}, u32[]{:S(2)}) collective-permute-start(bf16[10,128,128]{2,1,0:T(8,128)(2,1)S(1)} %copy-done.16), channel_id=1, source_target_pairs={{0,192},{32,224},{64,0},{96,32},{128,64},{160,96},{192,128},{224,1... | collective-permute-start | bytes 983048 | tf_op jit(solution)/shard_map/ppermute | solution.py:297
  67.0 14.8 %collective-permute-start.3 = (bf16[10,128,128]{2,1,0:T(8,128)(2,1)}, bf16[10,128,128]{2,1,0:T(8,128)(2,1)S(1)}, u32[]{:S(2)}, u32[]{:S(2)}) collective-permute-start(bf16[10,128,128]{2,1,0:T(8,128)(2,1)} %get-tuple-element.31), channel_id=1, source_target_pairs={{0,64},{32,96},{64,128},{96,160},{128,192},{160,224},{192,0},{224,... | collective-permute-start | bytes 983048 | tf_op jit(solution)/shard_map/ppermute | solution.py:297
  74.9 13.9 %collective-permute-start.2 = (bf16[10,128,128]{2,1,0:T(8,128)(2,1)S(1)}, bf16[10,128,128]{2,1,0:T(8,128)(2,1)S(1)}, u32[]{:S(2)}, u32[]{:S(2)}) collective-permute-start(bf16[10,128,128]{2,1,0:T(8,128)(2,1)S(1)} %add_convert_fusion.1), channel_id=1, source_target_pairs={{0,64},{32,96},{64,128},{96,160},{128,192},{160,224},{192,0},{224,... | collective-permute-start | bytes 983048 | tf_op jit(solution)/shard_map/ppermute | solution.py:297
  75.2 13.7 %collective-permute-start = (bf16[10,128,128]{2,1,0:T(8,128)(2,1)S(1)}, bf16[10,128,128]{2,1,0:T(8,128)(2,1)S(1)}, u32[]{:S(2)}, u32[]{:S(2)}) collective-permute-start(bf16[10,128,128]{2,1,0:T(8,128)(2,1)S(1)} %copy-done.15), channel_id=1, source_target_pairs={{0,192},{32,224},{64,0},{96,32},{128,64},{160,96},{192,128},{224,1... | collective-permute-start | bytes 983048 | tf_op jit(solution)/shard_map/ppermute | solution.py:297
  77.8 13.9 %copy-start.11 = (bf16[10,128,128]{2,1,0:T(8,128)(2,1)S(1)}, bf16[10,128,128]{2,1,0:T(8,128)(2,1)}, u32[]{:S(2)}) copy-start(bf16[10,128,128]{2,1,0:T(8,128)(2,1)} %get-tuple-element.33) | copy-start | bytes 983044
  77.9 13.8 %collective-permute-start.5 = (bf16[10,128,128]{2,1,0:T(8,128)(2,1)S(1)}, bf16[10,128,128]{2,1,0:T(8,128)(2,1)S(1)}, u32[]{:S(2)}, u32[]{:S(2)}) collective-permute-start(bf16[10,128,128]{2,1,0:T(8,128)(2,1)S(1)} %add_convert_fusion), channel_id=1, source_target_pairs={{0,192},{32,224},{64,0},{96,32},{128,64},{160,96},{192,128},{224,1... | collective-permute-start | bytes 983048 | tf_op jit(solution)/shard_map/ppermute | solution.py:297
  89.0 9.6 %collective-permute-start.6 = (bf16[5,128,128]{2,1,0:T(8,128)(2,1)S(1)}, bf16[5,128,128]{2,1,0:T(8,128)(2,1)S(1)}, u32[]{:S(2)}, u32[]{:S(2)}) collective-permute-start(bf16[5,128,128]{2,1,0:T(8,128)(2,1)S(1)} %slice.25), channel_id=1, source_target_pairs={{0,32},{32,0},{64,96},{96,64},{128,160},{160,128},{192,224},{224,1... | collective-permute-start | bytes 491528 | tf_op jit(solution)/shard_map/ppermute | solution.py:297
  91.7 5.1 %copy-start.2 = (bf16[128,1280]{1,0:T(8,128)(2,1)S(1)}, bf16[128,1280]{1,0:T(8,128)(2,1)}, u32[]{:S(2)}) copy-start(bf16[128,1280]{1,0:T(8,128)(2,1)} %patches_ref.3) | copy-start | bytes 983044
  91.7 5.1 %copy-start.3 = (bf16[128,1280]{1,0:T(8,128)(2,1)S(1)}, bf16[128,1280]{1,0:T(8,128)(2,1)}, u32[]{:S(2)}) copy-start(bf16[128,1280]{1,0:T(8,128)(2,1)} %teacher_ref.3) | copy-start | bytes 983044
  91.7 5.1 %copy-start.6 = (s32[128,1]{0,1:T(1,128)S(1)}, s32[128,1]{0,1:T(1,128)}, u32[]{:S(2)}) copy-start(s32[128,1]{0,1:T(1,128)} %param.11) | copy-start | bytes 1540
  91.7 5.1 %copy-start.7 = (bf16[128]{0:T(256)(128)(2,1)S(1)}, bf16[128]{0:T(256)(128)(2,1)}, u32[]{:S(2)}) copy-start(bf16[128]{0:T(256)(128)(2,1)} %param.12) | copy-start | bytes 772
  91.9 9.3 %collective-permute-start.7 = (bf16[5,128,128]{2,1,0:T(8,128)(2,1)S(1)}, bf16[5,128,128]{2,1,0:T(8,128)(2,1)S(1)}, u32[]{:S(2)}, u32[]{:S(2)}) collective-permute-start(bf16[5,128,128]{2,1,0:T(8,128)(2,1)S(1)} %slice.24), channel_id=1, source_target_pairs={{0,32},{32,0},{64,96},{96,64},{128,160},{160,128},{192,224},{224,1... | collective-permute-start | bytes 491528 | tf_op jit(solution)/shard_map/ppermute | solution.py:297
